TPU v7x, 256 devices: a whole 4x4x8 slice. The times are simulated.
256 devices in a mesh: ctx: 8 (over y, core), exp: 32 (over z, x).
Axes of the slice: x: 4, y: 4, z: 8, core: 2. Of those that a mesh axis runs over, the one named last changes fastest.
Arguments:
- kv_cache: bfloat16 [32, 192, 2, 32, 512], P('exp', 'ctx'), may hold values from -6 to 30
- slot_owner: int32 [32, 192], P('exp', 'ctx'), may hold values from -1 to 3, as said below
- slot_fill: int32 [32, 192], P('exp', 'ctx'), may hold values from 1 to 32
- phased: bfloat16 [32, 64, 2, 32, 512], P('exp', 'ctx'), may hold values from -6 to 30
- phase_owner: int32 [32, 64], P('exp'), may hold values from 0 to 3
- phase_fill: int32 [32, 64], P('exp'), may hold values from 1 to 32
- relay_page: int32 [32, 8, 8], P('exp'), may hold values from -1 to 7, as said below
- relay_slot: int32 [32, 8, 8], P('exp'), may hold values from 0 to 23, as said below
- queries: bfloat16 [2, 128, 6, 8192], P(None, 'exp'), may hold values from -6 to 120
- new_kv: bfloat16 [2, 128, 6, 2, 512], P(None, 'exp'), may hold values from -6 to 30
- hidden_in: bfloat16 [2, 128, 6, 4096], P(None, 'exp'), may hold values from -18 to 18
- o_proj: bfloat16 [8192, 4096], P('ctx', 'exp'), may hold values from -0.5 to 0.5
- expert_ids: int32 [2, 128, 6, 8], P(None, 'exp'), may hold values from 0 to 63, all different within a row; in each aligned block of 24 rows (0 to 23, 24 to 47, ..., all dimensions but the last counted through in order) at most 6 rows name the same one
- gate_weights: float32 [2, 128, 6, 8], P(None, 'exp'), may hold values from 0.05 to 1
- w_gate: bfloat16 [64, 4096, 1536], P('exp', None, 'ctx'), may hold values from -0.09375 to 0.09375
- w_up: bfloat16 [64, 4096, 1536], P('exp', None, 'ctx'), may hold values from -0.09375 to 0.09375
- w_down: bfloat16 [64, 1536, 4096], P('exp', 'ctx'), may hold values from -0.15625 to 0.15625
Outputs:
- layer_out: bfloat16 [2, 128, 6, 4096], P(None, 'exp', None, 'ctx')
Inputs may be any that keep to these rules, and one draw needn't show every extreme that they name: `slot_owner`: local index within the group's 4 requests of the page a slot holds, -1 for an empty slot; every device holds at least 8 empty slots, and one device of each group exactly 8. `relay_page`: index within the source's 8 phased pages of the page that source s of a group sends to destination d, or -1; a source names each phased page at most once; in every group some destination receives a page from every source. `relay_slot`: slot of destination d receiving that page; the slots named for one destination are distinct and empty in slot_owner. `expert_ids`: in the 24 rows of one index of exp and one step (aligned blocks), no expert is named more than 6 times.
All inputs are finite; a program needn't handle non-finite values.
Results may differ from a plain program's by a relative error of at most 0.02.
Values may be sent and summed in bfloat16 or wider, within the bound.
No kernel may reach another device: no remote copies, remote signals or barrier semaphores. Data moves between devices by JAX's collectives and lax.ppermute only.
A program may use at most 128 MiB of HBM per device.

v0:
```python
import jax
import jax.numpy as jnp
from jax import lax
from jax.sharding import PartitionSpec as P

HEADS = 64
KV_HEADS = 4
HEAD = 128
TOPK = 8


masked_score = -1e30
norm_epsilon = 1e-06
highest_precision = lax.Precision.HIGHEST


def combined_all(value, axis, join):
    pieces = jax.tree.map(lambda part: lax.all_gather(part, axis), value)
    head = jax.tree.map(lambda part: part[0], pieces)
    tail = jax.tree.map(lambda part: part[1:], pieces)
    so_far, _ = lax.scan(lambda so_far, section: (join(so_far, section), None), head, tail)
    return so_far


def join_parts(first_part, second_part):
    best_a, mass_a, sum_a = first_part
    best_b, mass_b, sum_b = second_part
    best_score = jnp.maximum(best_a, best_b)
    scale_a = jnp.exp(best_a - best_score)
    scale_b = jnp.exp(best_b - best_score)
    return (
        best_score,
        mass_a * scale_a + mass_b * scale_b,
        sum_a * scale_a[..., None] + sum_b * scale_b[..., None],
    )


def body(
    kv_cache,
    slot_owner,
    slot_fill,
    phased,
    phase_owner,
    phase_fill,
    relay_page,
    relay_slot,
    queries,
    new_kv,
    hidden_in,
    o_proj,
    expert_ids,
    gate_weights,
    w_gate,
    w_up,
    w_down,
):
    ctx_count = lax.axis_size("ctx")
    exp_count = lax.axis_size("exp")
    place_ctx = lax.axis_index("ctx")
    cache_now = kv_cache[0]
    slot_count = cache_now.shape[0]
    page_len = cache_now.shape[2]
    phase_pages = phased[0]
    phase_count = phase_pages.shape[0]
    plan_page = relay_page[0]
    plan_slot = relay_slot[0]
    sent_page = lax.dynamic_index_in_dim(plan_page, place_ctx, 0, keepdims=False)
    picker = (sent_page[:, None] == jnp.arange(phase_count)[None, :]).astype(jnp.bfloat16)
    outgoing = jnp.dot(
        picker, phase_pages.reshape(phase_count, -1), preferred_element_type=jnp.float32
    ).astype(jnp.bfloat16)
    incoming = lax.all_to_all(outgoing, "ctx", split_axis=0, concat_axis=0, tiled=True)
    came_page = lax.dynamic_index_in_dim(plan_page, place_ctx, 1, keepdims=False)
    came_slot = lax.dynamic_index_in_dim(plan_slot, place_ctx, 1, keepdims=False)
    arrive = (came_page >= 0)[None, :] & (came_slot[None, :] == jnp.arange(slot_count)[:, None])
    landed = jnp.dot(
        arrive.astype(jnp.bfloat16), incoming, preferred_element_type=jnp.float32
    ).astype(jnp.bfloat16)
    taken_slot = jnp.any(arrive, axis=1)
    cache_now = jnp.where(taken_slot[:, None], landed, cache_now.reshape(slot_count, -1)).reshape(
        cache_now.shape
    )
    anchor = jnp.arange(ctx_count) * phase_count + jnp.maximum(came_page, 0)
    lookup = anchor[:, None] == jnp.arange(phase_owner.shape[1])[None, :]
    came_owner = jnp.sum(jnp.where(lookup, phase_owner[0][None, :], 0), axis=1)
    came_fill = jnp.sum(jnp.where(lookup, phase_fill[0][None, :], 0), axis=1)
    owner_now = jnp.where(
        taken_slot, jnp.sum(jnp.where(arrive, came_owner[None, :], 0), axis=1), slot_owner[0]
    )
    fill_now = jnp.where(
        taken_slot, jnp.sum(jnp.where(arrive, came_fill[None, :], 0), axis=1), slot_fill[0]
    )
    request_count = queries.shape[1]
    draft_count = queries.shape[2]
    group_size = HEADS // KV_HEADS
    head_share = HEADS // ctx_count
    query_cols = head_share * HEAD
    score_scale = HEAD ** (-0.5)
    model_width = hidden_in.shape[3]
    col_width = model_width // ctx_count
    row_count = request_count * draft_count
    experts_here = w_gate.shape[0]
    experts_all = experts_here * exp_count
    capacity = 2 * row_count * TOPK // experts_all
    slots_out = experts_here * exp_count * capacity
    key_heads = cache_now[:, 0].reshape(slot_count, page_len, KV_HEADS, HEAD)
    value_heads = cache_now[:, 1].reshape(slot_count, page_len, KV_HEADS, HEAD)
    live_mask = (owner_now >= 0)[:, None] & (jnp.arange(page_len)[None, :] < fill_now[:, None])
    owned_by = owner_now[None, :] == jnp.arange(request_count)[:, None]
    owned_float = owned_by.astype(jnp.float32)
    owned_half = owned_by.astype(jnp.bfloat16)
    leader = place_ctx == 0
    draft_index = jnp.arange(draft_count)
    results = []
    for step_index in range(queries.shape[0]):
        query_rows = queries[step_index]
        chosen = jnp.dot(
            owned_half.T, query_rows.reshape(request_count, -1), preferred_element_type=jnp.float32
        ).astype(jnp.bfloat16)
        chosen = chosen.reshape(slot_count, draft_count, KV_HEADS, group_size, HEAD)
        scores = (
            jnp.einsum("sqkgd,stkd->sqkgt", chosen, key_heads, preferred_element_type=jnp.float32)
            * score_scale
        )
        scores = jnp.where(live_mask[:, None, None, None, :], scores, masked_score)
        query_heads = query_rows.reshape(request_count, draft_count, KV_HEADS, group_size, HEAD)
        recent = new_kv[: step_index + 1]
        recent_keys = recent[:, :, :, 0].reshape(
            step_index + 1, request_count, draft_count, KV_HEADS, HEAD
        )
        recent_values = recent[:, :, :, 1].reshape(
            step_index + 1, request_count, draft_count, KV_HEADS, HEAD
        )
        allowed = (
            (jnp.arange(step_index + 1)[None, :, None] < step_index)
            | (draft_index[None, None, :] <= draft_index[:, None, None])
        ) & leader
        fresh_scores = (
            jnp.einsum(
                "rqkgd,nrjkd->rqkgnj", query_heads, recent_keys, preferred_element_type=jnp.float32
            )
            * score_scale
        )
        fresh_scores = jnp.where(allowed[None, :, None, None], fresh_scores, masked_score)
        slot_best = jnp.max(scores, axis=-1)
        highest = jnp.max(
            jnp.where(owned_by[:, :, None, None, None], slot_best[None], masked_score), axis=1
        )
        highest = jnp.maximum(highest, jnp.max(fresh_scores, axis=(-2, -1)))
        slot_shift = jnp.sum(
            jnp.where(owned_by[:, :, None, None, None], highest[:, None], 0.0), axis=0
        )
        probs = jnp.where(
            live_mask[:, None, None, None, :], jnp.exp(scores - slot_shift[..., None]), 0.0
        )
        fresh_probs = jnp.where(
            allowed[None, :, None, None], jnp.exp(fresh_scores - highest[..., None, None]), 0.0
        )
        total_mass = jnp.einsum(
            "rs,sqkg->rqkg", owned_float, jnp.sum(probs, axis=-1), precision=highest_precision
        )
        total_mass = total_mass + jnp.sum(fresh_probs, axis=(-2, -1))
        slot_sum = jnp.einsum(
            "sqkgt,stkd->sqkgd",
            probs.astype(jnp.bfloat16),
            value_heads,
            preferred_element_type=jnp.float32,
        )
        accumulated = jnp.einsum(
            "rs,sqkgd->rqkgd", owned_float, slot_sum, precision=highest_precision
        )
        accumulated = accumulated + jnp.einsum(
            "rqkgnj,nrjkd->rqkgd",
            fresh_probs.astype(jnp.bfloat16),
            recent_values,
            preferred_element_type=jnp.float32,
        )
        whole_best, whole_mass, whole_sum = combined_all(
            (highest, total_mass, accumulated), "ctx", join_parts
        )
        attended = (
            (whole_sum / whole_mass[..., None])
            .reshape(row_count, HEADS * HEAD)
            .astype(jnp.bfloat16)
        )
        mine_cols = lax.dynamic_slice_in_dim(attended, place_ctx * query_cols, query_cols, 1)
        partial_value = jnp.dot(
            lax.all_gather(mine_cols, "exp", axis=0, tiled=True),
            o_proj,
            preferred_element_type=jnp.float32,
        )
        spread = lax.all_to_all(
            partial_value.astype(jnp.bfloat16), "exp", split_axis=0, concat_axis=1, tiled=True
        ).astype(partial_value.dtype)
        projected = lax.psum(spread.astype(jnp.bfloat16), "ctx").astype(jnp.float32)
        residual = (
            hidden_in[step_index].reshape(row_count, model_width).astype(jnp.float32) + projected
        )
        normed = (
            residual
            * lax.rsqrt(jnp.mean(residual * residual, axis=-1, keepdims=True) + norm_epsilon)
        ).astype(jnp.bfloat16)
        flat_ids = expert_ids[step_index].reshape(-1)
        hit_table = (flat_ids[:, None] == jnp.arange(experts_all)[None, :]).astype(jnp.int32)
        rank_pos = jnp.sum((jnp.cumsum(hit_table, axis=0) - hit_table) * hit_table, axis=1)
        position = (
            flat_ids % experts_here * (exp_count * capacity)
            + flat_ids // experts_here * capacity
            + rank_pos
        )
        at_slot = position[:, None] == jnp.arange(slots_out)[None, :]
        at_row = (jnp.arange(row_count * TOPK) // TOPK)[:, None] == jnp.arange(row_count)[None, :]
        sender = jnp.dot(
            at_slot.T.astype(jnp.bfloat16),
            at_row.astype(jnp.bfloat16),
            preferred_element_type=jnp.float32,
        ).astype(jnp.bfloat16)
        packed = jnp.dot(sender, normed, preferred_element_type=jnp.float32).astype(jnp.bfloat16)
        arrived = lax.all_to_all(
            packed.reshape(experts_here, exp_count, capacity, model_width),
            "exp",
            split_axis=1,
            concat_axis=1,
            tiled=True,
        )
        batch_rows = arrived.reshape(experts_here, exp_count * capacity, model_width)
        gate_act = jnp.einsum(
            "erd,edf->erf", batch_rows, w_gate, preferred_element_type=jnp.float32
        )
        up_act = jnp.einsum("erd,edf->erf", batch_rows, w_up, preferred_element_type=jnp.float32)
        hidden_units = (jax.nn.silu(gate_act) * up_act).astype(jnp.bfloat16)
        partial_out = jnp.einsum(
            "erf,efd->erd", hidden_units, w_down, preferred_element_type=jnp.float32
        )
        gate_rows = gate_weights[step_index].reshape(row_count, TOPK)
        mixing_flat = (gate_rows / jnp.sum(gate_rows, axis=-1, keepdims=True)).reshape(-1)
        mixing = jnp.dot(
            (at_row.astype(jnp.float32) * mixing_flat[:, None]).T,
            at_slot.astype(jnp.float32),
            precision=highest_precision,
        )
        shares = lax.psum_scatter(
            partial_out.astype(jnp.bfloat16), "ctx", scatter_dimension=2, tiled=True
        ).astype(jnp.float32)
        outcome = shares.reshape(experts_here, exp_count, capacity, col_width)
        returned = lax.all_to_all(
            outcome.astype(jnp.bfloat16), "exp", split_axis=1, concat_axis=1, tiled=True
        ).astype(outcome.dtype)
        mixed_part = jnp.dot(
            mixing, returned.reshape(slots_out, col_width), precision=highest_precision
        )
        residual_cols = lax.dynamic_slice_in_dim(residual, place_ctx * col_width, col_width, 1)
        results.append(
            (residual_cols + mixed_part)
            .astype(jnp.bfloat16)
            .reshape(request_count, draft_count, col_width)
        )
    return jnp.stack(results)


def solution(mesh):
    in_specs = (
        P("exp", "ctx", None, None, None),
        P("exp", "ctx"),
        P("exp", "ctx"),
        P("exp", "ctx", None, None, None),
        P("exp", None),
        P("exp", None),
        P("exp", None, None),
        P("exp", None, None),
        P(None, "exp", None, None),
        P(None, "exp", None, None, None),
        P(None, "exp", None, None),
        P("ctx", "exp"),
        P(None, "exp", None, None),
        P(None, "exp", None, None),
        P("exp", None, "ctx"),
        P("exp", None, "ctx"),
        P("exp", "ctx", None),
    )
    out_specs = P(None, "exp", None, "ctx")
    return jax.shard_map(body, mesh=mesh, in_specs=in_specs, out_specs=out_specs, check_vma=False)
```

profile of v0, /device:TPU:24, one launch (start us, length us, event | category | flops | bytes accessed | tf_op | source)
XLA Modules:
  0.0 737.3 jit_solution(1377758626759130532)
XLA Ops:
  17.2 6.0 all-to-all-start
  68.1 6.2 bitcast_reduce_fusion.1
  78.7 9.0 %fusion.17 = (f32[24,6,4,16]{3,1,2,0:T(8,128)}, f32[24,6,4,16]{3,1,2,0:T(8,128)}, f32[24,4,32,6,16]{2,4,3,1,0:T(8,128)}) fusion(f32[24,4,32,6,16]{2,4,3,1,0:T(8,128)} %get-tuple-element.180, f32[24,6,4,16]{3,1,2,0:T(8,128)S(1)} %copy.286, pred[24,32]{1,0:T(8,128)(4,1)S(1)} %fusion.147, bf16[24,6,4,16,128]{4,3,2,1,0:T(8,128)(2,1)} %bitcast.255, ...), kind=kOutput, calls=%fused_computation.41 | convolution fusion | flops 77838336 | bytes 5616384 | tf_op jit(solution)/shard_map/sqkgd,stkd->sqkgt/dot_general | solution.py:122
  123.5 13.9 %all-gather.3 = f32[32,6,4,16]{3,2,1,0:T(4,128)S(1)} all-gather(f32[4,6,4,16]{3,2,1,0:T(4,128)} %copy-done.12), channel_id=5, replica_groups=mesh['ctx'=8,'exp'=32] {'ctx'}, dimensions={0}, use_global_device_ids=true | all-gather | bytes 55296 | tf_op jit(solution)/shard_map/all_gather | solution.py:18
  144.1 13.6 %all-gather.4 = f32[32,6,4,16]{3,2,1,0:T(4,128)S(1)} all-gather(f32[4,6,4,16]{3,2,1,0:T(4,128)S(1)} %copy.323), channel_id=6, replica_groups=mesh['ctx'=8,'exp'=32] {'ctx'}, dimensions={0}, use_global_device_ids=true | all-gather | bytes 55296 | tf_op jit(solution)/shard_map/all_gather | solution.py:18
  158.5 13.0 %all-gather = f32[32,6,4,16]{3,2,1,0:T(4,128)S(1)} all-gather(f32[4,6,4,16]{3,2,1,0:T(4,128)S(1)} %copy-done.11), channel_id=2, replica_groups=mesh['ctx'=8,'exp'=32] {'ctx'}, dimensions={0}, use_global_device_ids=true | all-gather | bytes 55296 | tf_op jit(solution)/shard_map/all_gather | solution.py:18
  172.9 13.7 %all-gather.1 = f32[32,6,4,16]{3,2,1,0:T(4,128)S(1)} all-gather(f32[4,6,4,16]{3,2,1,0:T(4,128)S(1)} %copy.290), channel_id=3, replica_groups=mesh['ctx'=8,'exp'=32] {'ctx'}, dimensions={0}, use_global_device_ids=true | all-gather | bytes 55296 | tf_op jit(solution)/shard_map/all_gather | solution.py:18
  189.6 6.0 slice.158
  195.5 25.7 %while.29 = (s32[]{:T(128)}, f32[4,6,4,16]{3,2,1,0:T(4,128)S(1)}, f32[4,6,4,16]{3,2,1,0:T(4,128)S(1)}, f32[4,6,4,16,128]{4,3,2,1,0:T(8,128)}, f32[7,4,6,4,16]{4,...) while((s32[]{:T(128)}, f32[4,6,4,16]{3,2,1,0:T(4,128)S(1)}, ...), condition=%wide.region_27.28_spmd, body=%wide.region_26.27_spmd.sunk | while | flops 599042 | bytes 2420837 | solution.py:21
  229.1 5.9 slice.150
  235.0 25.5 %while.28 = (s32[]{:T(128)}, f32[4,6,4,16]{3,2,1,0:T(4,128)S(1)}, f32[4,6,4,16]{3,2,1,0:T(4,128)S(1)}, f32[4,6,4,16,128]{4,3,2,1,0:T(8,128)}, f32[7,4,6,4,16]{4,...) while((s32[]{:T(128)}, f32[4,6,4,16]{3,2,1,0:T(4,128)S(1)}, ...), condition=%wide.region_12.13_spmd, body=%wide.region_11.12_spmd.sunk | while | flops 599042 | bytes 2420837 | solution.py:21
  277.0 28.3 %all-gather.13.cloned.1.call-done = bf16[768,1024]{1,0:T(8,128)(2,1)} async-done(((bf16[24,1024]{1,0:T(8,128)(2,1)}), bf16[768,1024]{1,0:T(8,128)(2,1)}) %all-gather.13.cloned.1.call-update) | async-done | bytes 1572880 | tf_op jit(solution)/shard_map/all_gather | solution.py:188
  308.0 6.1 all-to-all-start.4
  314.1 68.3 %all-gather.11.cloned.1.call-done = bf16[768,1024]{1,0:T(8,128)(2,1)} async-done(((bf16[24,1024]{1,0:T(8,128)(2,1)}), bf16[768,1024]{1,0:T(8,128)(2,1)}) %all-gather.11.cloned.1.call-update) | async-done | bytes 1572880 | tf_op jit(solution)/shard_map/all_gather | solution.py:188
  385.1 5.9 all-to-all-start.1
  392.7 9.4 %all-to-all-done.1 = bf16[32,24,128]{2,1,0:T(8,128)(2,1)S(1)} async-done(((bf16[32,24,128]{2,1,0:T(8,128)(2,1)}), bf16[32,24,128]{2,1,0:T(8,128)(2,1)S(1)}, u32[]{:S(2)}, u32[]{:S(2)}) %all-to-all-start.1) | async-done | bytes 196640 | tf_op jit(solution)/shard_map/all_to_all | solution.py:192
  402.8 58.6 %all-reduce.5.cloned.1.call-done = (bf16[24,4096]{1,0:T(8,128)(2,1)}, bf16[24,4096]{1,0:T(8,128)(2,1)}) async-done(((bf16[24,4096]{1,0:T(8,128)(2,1)}, bf16[24,4096]{1,0:T(8,128)(2,1)}), (bf16[24,4096]{1,0:T(8,128)(2,1)}, bf16[24,4096]{1,0:T(8,128)(2,1)})) %all-reduce.5.cloned.1.call-update) | async-done | bytes 393232 | tf_op jit(solution)/shard_map/psum | solution.py:195
  468.1 5.6 reshape.457
  473.7 7.2 copy.337
  480.9 10.3 %all-to-all-start.5 = ((bf16[2,32,6,4096]{3,0,2,1:T(2,128)(2,1)}), bf16[2,32,6,4096]{3,0,2,1:T(2,128)(2,1)}, u32[]{:S(2)}, u32[]{:S(2)}) async-start(bf16[2,32,6,4096]{3,0,2,1:T(2,128)(2,1)} %copy.337), calls=%async_computation.6 | async-start | bytes 6291456 | tf_op jit(solution)/shard_map/all_to_all | solution.py:219
  494.2 5.6 reshape.451
  499.9 7.2 copy.304
  507.1 57.4 %all-to-all-done.5 = bf16[2,32,6,4096]{3,0,2,1:T(2,128)(2,1)} async-done(((bf16[2,32,6,4096]{3,0,2,1:T(2,128)(2,1)}), bf16[2,32,6,4096]{3,0,2,1:T(2,128)(2,1)}, u32[]{:S(2)}, u32[]{:S(2)}) %all-to-all-start.5) | async-done | bytes 3145760 | tf_op jit(solution)/shard_map/all_to_all | solution.py:219
  564.6 8.8 %all-to-all-start.2 = ((bf16[2,32,6,4096]{3,0,2,1:T(2,128)(2,1)}), bf16[2,32,6,4096]{3,0,2,1:T(2,128)(2,1)}, u32[]{:S(2)}, u32[]{:S(2)}) async-start(bf16[2,32,6,4096]{3,0,2,1:T(2,128)(2,1)} %copy.304), calls=%async_computation.2 | async-start | bytes 6291456 | tf_op jit(solution)/shard_map/all_to_all | solution.py:219
  573.4 5.8 fusion.22
  579.1 7.6 %convolution_convert_fusion.6 = bf16[2,192,4096]{2,1,0:T(8,128)(2,1)} fusion(bf16[2,192,4096]{2,1,0:T(8,128)(2,1)S(1)} %copy-done, bf16[2,4096,192]{1,2,0:T(8,128)(2,1)} %param.36, bf16[2,192,4096]{2,0,1:T(2,128)(2,1)} %bitcast.58, f32[2,192,192]{2,1,0:T(8,128)} %fusion.22), kind=kOutput, calls=%fused_computation.24 | convolution fusion | flops 1209974784 | bytes 12877824 | tf_op jit(solution)/shard_map/erf,efd->erd/dot_general | solution.py:232
  587.1 58.8 %all-to-all-done.2 = bf16[2,32,6,4096]{3,0,2,1:T(2,128)(2,1)} async-done(((bf16[2,32,6,4096]{3,0,2,1:T(2,128)(2,1)}), bf16[2,32,6,4096]{3,0,2,1:T(2,128)(2,1)}, u32[]{:S(2)}, u32[]{:S(2)}) %all-to-all-start.2) | async-done | bytes 3145760 | tf_op jit(solution)/shard_map/all_to_all | solution.py:219
  645.8 5.8 fusion.26
  651.6 7.6 %convolution_convert_fusion.7 = bf16[2,192,4096]{2,1,0:T(8,128)(2,1)} fusion(bf16[2,192,4096]{2,1,0:T(8,128)(2,1)S(1)} %copy-done, bf16[2,4096,192]{1,2,0:T(8,128)(2,1)} %param.36, bf16[2,192,4096]{2,0,1:T(2,128)(2,1)} %bitcast.36, f32[2,192,192]{2,1,0:T(8,128)} %fusion.26), kind=kOutput, calls=%fused_computation.25 | convolution fusion | flops 1209974784 | bytes 12877824 | tf_op jit(solution)/shard_map/erf,efd->erd/dot_general | solution.py:232
  661.5 6.3 all-to-all-start.6
  667.7 24.5 %reduce-scatter.3.cloned.1.call-done = bf16[2,192,512]{2,1,0:T(8,128)(2,1)} async-done(((bf16[2,192,4096]{2,1,0:T(8,128)(2,1)}), bf16[2,192,512]{2,1,0:T(8,128)(2,1)}) %reduce-scatter.3.cloned.1.call-update) | async-done | bytes 393232 | tf_op jit(solution)/shard_map/reduce_scatter | solution.py:242
  694.4 9.8 %all-to-all-start.3 = ((bf16[2,32,6,512]{3,0,2,1:T(2,128)(2,1)}), bf16[2,32,6,512]{3,0,2,1:T(2,128)(2,1)}, u32[]{:S(2)}, u32[]{:S(2)}) async-start(bf16[2,32,6,512]{3,0,2,1:T(2,128)(2,1)} %bitcast.257), calls=%async_computation.4 | async-start | bytes 786432 | tf_op jit(solution)/shard_map/all_to_all | solution.py:246
  (270 shorter events, 231.0 us)
Async XLA Ops:
  6.5 572.6 %copy-start = (bf16[2,192,4096]{2,1,0:T(8,128)(2,1)S(1)}, bf16[2,192,4096]{2,1,0:T(8,128)(2,1)}, u32[]{:S(2)}) copy-start(bf16[2,192,4096]{2,1,0:T(8,128)(2,1)} %param.37) | copy-start | bytes 9437188
  6.5 16.6 %copy-start.20 = (s32[1,8,8]{2,1,0:T(8,128)S(1)}, s32[1,8,8]{2,1,0:T(8,128)}, u32[]{:S(2)}) copy-start(s32[1,8,8]{2,1,0:T(8,128)} %param.27) | copy-start | bytes 772
  6.5 17.0 %copy-start.28 = (s32[1,8,8]{2,1,0:T(8,128)S(1)}, s32[1,8,8]{2,1,0:T(8,128)}, u32[]{:S(2)}) copy-start(s32[1,8,8]{2,1,0:T(8,128)} %param.28) | copy-start | bytes 772
  6.5 17.3 %copy-start.31 = (s32[1,64]{1,0:T(1,128)S(1)}, s32[1,64]{1,0:T(1,128)}, u32[]{:S(2)}) copy-start(s32[1,64]{1,0:T(1,128)} %param.26) | copy-start | bytes 772
  6.5 17.3 %copy-start.32 = (s32[1,64]{1,0:T(1,128)S(1)}, s32[1,64]{1,0:T(1,128)}, u32[]{:S(2)}) copy-start(s32[1,64]{1,0:T(1,128)} %param.25) | copy-start | bytes 772
  6.5 18.2 %copy-start.29 = (s32[1,24]{1,0:T(1,128)S(1)}, s32[1,24]{1,0:T(1,128)}, u32[]{:S(2)}) copy-start(s32[1,24]{1,0:T(1,128)} %param.22) | copy-start | bytes 292
  6.6 18.7 %copy-start.9 = (bf16[2,4,6,2,512]{4,3,2,1,0:T(2,128)(2,1)S(1)}, bf16[2,4,6,2,512]{4,3,2,1,0:T(2,128)(2,1)}, u32[]{:S(2)}) copy-start(bf16[2,4,6,2,512]{4,3,2,1,0:T(2,128)(2,1)} %param.30) | copy-start | bytes 294916
  17.2 40.6 %all-to-all-start = ((bf16[8,2,16384]{2,1,0:T(2,128)(2,1)}), bf16[8,2,16384]{2,1,0:T(2,128)(2,1)}, u32[]{:S(2)}, u32[]{:S(2)}) async-start(bf16[8,2,16384]{2,1,0:T(2,128)(2,1)} %reshape.513), calls=%async_computation | async-start | bytes 1048576 | tf_op jit(solution)/shard_map/all_to_all | solution.py:72
  23.2 164.2 %all-gather.17.cloned.1.call-start = ((), (), s32[]{:S(2)}) async-start(), calls=%async_computation.14 | async-start | bytes 7077888 | tf_op jit(solution)/shard_map/all_gather | solution.py:18
  23.9 24.8 %copy-start.23 = (pred[24]{0:T(512)(128)(4,1)}, pred[24]{0:T(512)(128)(4,1)S(1)}, u32[]{:S(2)}) copy-start(pred[24]{0:T(512)(128)(4,1)S(1)} %fusion.150) | copy-start | bytes 76
  43.7 11.0 %copy-start.7 = (bf16[4,6,4,16,128]{4,3,2,0,1:T(8,128)(2,1)S(1)}, bf16[4,6,4,16,128]{4,3,2,0,1:T(8,128)(2,1)}, u32[]{:S(2)}) copy-start(bf16[4,6,4,16,128]{4,3,2,0,1:T(8,128)(2,1)} %reshape_squeeze.50) | copy-start | bytes 1179652
  109.6 117.4 %all-gather.15.cloned.1.call-start = ((), (), s32[]{:S(2)}) async-start(), calls=%async_computation.13 | async-start | bytes 7077888 | tf_op jit(solution)/shard_map/all_gather | solution.py:18
  123.5 181.8 %all-gather.13.cloned.1.call-start = ((), (), s32[]{:S(2)}) async-start(), calls=%async_computation.11 | async-start | bytes 1622016 | tf_op jit(solution)/shard_map/all_gather | solution.py:188
  138.8 19.7 %copy-start.11 = (f32[4,6,4,16]{3,2,1,0:T(4,128)S(1)}, f32[4,6,4,16]{3,2,1,0:T(4,128)}, u32[]{:S(2)}) copy-start(f32[4,6,4,16]{3,2,1,0:T(4,128)} %copy-done.10) | copy-start | bytes 18436
  138.8 33.4 %copy-start.2 = (f32[4,6,4,16,1,6]{3,5,1,2,0,4:T(8,128)S(1)}, f32[4,6,4,16,1,6]{3,5,1,2,0,4:T(8,128)}, u32[]{:S(2)}) copy-start(f32[4,6,4,16,1,6]{3,5,1,2,0,4:T(8,128)} %get-tuple-element.182) | copy-start | bytes 110596
  138.8 33.4 %copy-start.16 = (f32[4,6,4,16]{3,1,2,0:T(8,128)S(1)}, f32[4,6,4,16]{3,1,2,0:T(8,128)}, u32[]{:S(2)}) copy-start(f32[4,6,4,16]{3,1,2,0:T(8,128)} %copy-done.15) | copy-start | bytes 18436
  138.8 33.6 %copy-start.18 = (f32[24,6,4,16]{3,1,2,0:T(8,128)S(1)}, f32[24,6,4,16]{3,1,2,0:T(8,128)}, u32[]{:S(2)}) copy-start(f32[24,6,4,16]{3,1,2,0:T(8,128)} %get-tuple-element.119) | copy-start | bytes 110596
  157.7 15.2 %copy-start.3 = (f32[32,6,4,16]{3,2,1,0:T(4,128)}, f32[32,6,4,16]{3,2,1,0:T(4,128)S(1)}, u32[]{:S(2)}) copy-start(f32[32,6,4,16]{3,2,1,0:T(4,128)S(1)} %all-gather.4) | copy-start | bytes 147460
  171.5 15.2 %copy-start.4 = (f32[32,6,4,16]{3,2,1,0:T(4,128)}, f32[32,6,4,16]{3,2,1,0:T(4,128)S(1)}, u32[]{:S(2)}) copy-start(f32[32,6,4,16]{3,2,1,0:T(4,128)S(1)} %all-gather) | copy-start | bytes 147460
  226.7 155.7 %all-gather.11.cloned.1.call-start = ((), (), s32[]{:S(2)}) async-start(), calls=%async_computation.9 | async-start | bytes 1622016 | tf_op jit(solution)/shard_map/all_gather | solution.py:188
  272.6 109.8 %copy-start.8 = (bf16[1024,128]{1,0:T(8,128)(2,1)S(1)}, bf16[1024,128]{1,0:T(8,128)(2,1)}, u32[]{:S(2)}) copy-start(bf16[1024,128]{1,0:T(8,128)(2,1)} %param.32) | copy-start | bytes 786436
  276.1 215.1 %copy-start.21 = (s32[192]{0:T(256)}, s32[192]{0:T(256)S(1)}, u32[]{:S(2)}) copy-start(s32[192]{0:T(256)S(1)} %get-tuple-element.184) | copy-start | bytes 2308
  308.0 77.1 %all-to-all-start.4 = ((bf16[32,24,128]{2,1,0:T(8,128)(2,1)}), bf16[32,24,128]{2,1,0:T(8,128)(2,1)}, u32[]{:S(2)}, u32[]{:S(2)}) async-start(bf16[32,24,128]{2,1,0:T(8,128)(2,1)} %bitcast.266), calls=%async_computation.5 | async-start | bytes 393216 | tf_op jit(solution)/shard_map/all_to_all | solution.py:192
  385.1 17.0 %all-to-all-start.1 = ((bf16[32,24,128]{2,1,0:T(8,128)(2,1)}), bf16[32,24,128]{2,1,0:T(8,128)(2,1)S(1)}, u32[]{:S(2)}, u32[]{:S(2)}) async-start(bf16[32,24,128]{2,1,0:T(8,128)(2,1)} %bitcast.265), calls=%async_computation.1 | async-start | bytes 393216 | tf_op jit(solution)/shard_map/all_to_all | solution.py:192
  391.0 70.3 %all-reduce.5.cloned.1.call-start = ((), (), s32[]{:S(2)}) async-start(), calls=%async_computation.15 | async-start | bytes 786432 | tf_op jit(solution)/shard_map/psum | solution.py:195
  402.8 70.9 %copy-start.26 = (s32[192]{0:T(256)}, s32[192]{0:T(256)S(1)}, u32[]{:S(2)}) copy-start(s32[192]{0:T(256)S(1)} %fusion.163) | copy-start | bytes 2308
  480.9 83.6 %all-to-all-start.5 = ((bf16[2,32,6,4096]{3,0,2,1:T(2,128)(2,1)}), bf16[2,32,6,4096]{3,0,2,1:T(2,128)(2,1)}, u32[]{:S(2)}, u32[]{:S(2)}) async-start(bf16[2,32,6,4096]{3,0,2,1:T(2,128)(2,1)} %copy.337), calls=%async_computation.6 | async-start | bytes 6291456 | tf_op jit(solution)/shard_map/all_to_all | solution.py:219
  564.6 81.3 %all-to-all-start.2 = ((bf16[2,32,6,4096]{3,0,2,1:T(2,128)(2,1)}), bf16[2,32,6,4096]{3,0,2,1:T(2,128)(2,1)}, u32[]{:S(2)}, u32[]{:S(2)}) async-start(bf16[2,32,6,4096]{3,0,2,1:T(2,128)(2,1)} %copy.304), calls=%async_computation.2 | async-start | bytes 6291456 | tf_op jit(solution)/shard_map/all_to_all | solution.py:219
  573.3 86.0 %reduce-scatter.5.cloned.1.call-start = ((), (), s32[]{:S(2)}) async-start(), calls=%async_computation.12 | async-start | bytes 3538944 | tf_op jit(solution)/shard_map/reduce_scatter | solution.py:242
  586.8 105.5 %reduce-scatter.3.cloned.1.call-start = ((), (), s32[]{:S(2)}) async-start(), calls=%async_computation.10 | async-start | bytes 3538944 | tf_op jit(solution)/shard_map/reduce_scatter | solution.py:242
  661.5 32.9 %all-to-all-start.6 = ((bf16[2,32,6,512]{3,0,2,1:T(2,128)(2,1)}), bf16[2,32,6,512]{3,0,2,1:T(2,128)(2,1)}, u32[]{:S(2)}, u32[]{:S(2)}) async-start(bf16[2,32,6,512]{3,0,2,1:T(2,128)(2,1)} %bitcast.258), calls=%async_computation.8 | async-start | bytes 786432 | tf_op jit(solution)/shard_map/all_to_all | solution.py:246
  694.4 28.0 %all-to-all-start.3 = ((bf16[2,32,6,512]{3,0,2,1:T(2,128)(2,1)}), bf16[2,32,6,512]{3,0,2,1:T(2,128)(2,1)}, u32[]{:S(2)}, u32[]{:S(2)}) async-start(bf16[2,32,6,512]{3,0,2,1:T(2,128)(2,1)} %bitcast.257), calls=%async_computation.4 | async-start | bytes 786432 | tf_op jit(solution)/shard_map/all_to_all | solution.py:246
  (17 other events, 77.1 us)
Sparse Core Ops, SparseCore 0:
  109.7 45.9 all-gather.16
  157.5 45.2 all-gather.14
  226.9 78.4 all-gather.12
  307.8 74.6 all-gather.10
  402.9 58.4 all-reduce.4
  586.9 36.6 reduce-scatter.4
  659.4 32.7 reduce-scatter.2
where the time goes:
time: 750 us; the launch traced here: 737 us
  waiting for transfers between devices  305 us (41%)
  local copies, waits for them, and re-layouts  126 us (17%)
  matrix products  94 us (13%)
  other arithmetic  89.6 us (12%)
  blocking collectives  54.2 us (7%)
  starting transfers between devices  53.7 us (7%)
  between operations  14.3 us (2%)
    all_to_all x2, waiting for transfers between devices, body(): lax.all_to_all(packed.reshape(experts_here, exp_count, capacity, model_wi...  116 us
    all_gather x2, waiting for transfers between devices, body(): lax.all_gather(mine_cols, 'exp', axis=0, tiled=True)  96.7 us
    psum x1, waiting for transfers between devices, body(): projected = lax.psum(spread.astype(jnp.bfloat16), 'ctx').astype(jnp.float32)  58.6 us
    all_gather x4, blocking collectives, combined_all(): pieces = jax.tree.map(lambda part: lax.all_gather(part, axis), value)  54.2 us
    add x14, other arithmetic, join_parts(): sum_a * scale_a[..., None] + sum_b * scale_b[..., None]  38.7 us
    reshape x4, local copies, waits for them, and re-layouts, body(): packed.reshape(experts_here, exp_count, capacity, model_width)  25.7 us
    reduce_scatter x2, waiting for transfers between devices, body(): lax.psum_scatter(partial_out.astype(jnp.bfloat16), 'ctx', scatter_dimensi...  24.5 us
    all_to_all x2, starting transfers between devices, body(): lax.all_to_all(packed.reshape(experts_here, exp_count, capacity, model_wi...  19 us
  transfers between devices with their start and end apart: 14, of which 7 were waited for; matrix products, arithmetic and copies ran while one was open for 30% of the time, Pallas kernels for 0%

commit v1 on v0

v1 whole, which is shorter than its diff:
```python
import functools

import jax
import jax.numpy as jnp
from jax import lax
from jax.experimental import pallas as pl
from jax.experimental.pallas import tpu as pltpu
from jax.sharding import Mesh, PartitionSpec as P

HEADS = 64
KV_HEADS = 4
HEAD = 128
TOPK = 8
NY, NCORE, NZ, NX = 4, 2, 8, 4
NC = NY * NCORE
ROWS = 48
ALL = NX * ROWS
KEYS = 1152
CAP = 6
SLOTS = NZ * 2 * NX * 2 * CAP
WIDTH = 4096
COLS = WIDTH // NC
FFS = 192
SCALE = HEAD ** (-0.5)
EPS = 1e-06
MASKED = -1e30
CTX = ("y", "core")
BF = jnp.bfloat16
F32 = jnp.float32


def params(mb=40):
    return pltpu.CompilerParams(vmem_limit_bytes=mb * 1024 * 1024)


def dot(a, b, dims=((1,), (0,))):
    return lax.dot_general(a, b, (dims, ((), ())), preferred_element_type=F32)


def thresholds(value, step, count):
    total = jnp.zeros_like(value)
    for n in range(1, count):
        total = total + (value >= n * step).astype(value.dtype)
    return total


def attention_kernel(
    place, owner, fill, phase_owner, phase_fill, relay, q, kv, ph, fk, fv, out, bias, keys, vals
):
    @pl.when(pl.program_id(0) == 0)
    def _():
        me = place[0]
        key = lax.broadcasted_iota(jnp.int32, (8, KEYS), 1)
        page = lax.shift_right_logical(key, 5)
        own = jnp.full((8, KEYS), -1, jnp.int32)
        cap = jnp.zeros((8, KEYS), jnp.int32)
        for p in range(24):
            own = jnp.where(page == p, owner[0, p], own)
            cap = jnp.where(page == p, fill[0, p], cap)
        for p in range(8):
            sent = relay[me, 0] == p
            for d in range(1, NC):
                sent = sent | (relay[me, d] == p)
            at = me * 8 + p
            own = jnp.where(page == 24 + p, jnp.where(sent, phase_owner[0, at], -1), own)
            cap = jnp.where(page == 24 + p, phase_fill[0, at], cap)
        own = jnp.where((key & 31) < cap, own, -1)[0:1]
        row = lax.broadcasted_iota(jnp.int32, (ROWS, KEYS), 0)
        step = thresholds(row, 24, 2)
        rest = row - 24 * step
        req = thresholds(rest, 6, 4)
        draft = rest - 6 * req
        fresh = lax.broadcasted_iota(jnp.int32, (ROWS, KEYS), 1) - 1024
        f_step = thresholds(fresh, 24, 2)
        f_rest = fresh - 24 * f_step
        f_req = thresholds(f_rest, 6, 4)
        f_draft = f_rest - 6 * f_req
        earlier = (f_step < step) | ((f_step == step) & (f_draft <= draft))
        is_fresh = (fresh >= 0) & (fresh < ROWS) & (f_req == req) & earlier
        is_fresh = is_fresh & (jnp.full((ROWS, KEYS), me, jnp.int32) == 0)
        seen = (jnp.broadcast_to(own, (ROWS, KEYS)) == req) | is_fresh
        bias[...] = jnp.where(seen, 0.0, MASKED)
        keys[1024 + ROWS :, :] = jnp.zeros((KEYS - 1024 - ROWS, HEAD), BF)
        vals[1024 + ROWS :, :] = jnp.zeros((KEYS - 1024 - ROWS, HEAD), BF)

    keys[0:768, :] = kv[:, 0].reshape(768, HEAD)
    keys[768:1024, :] = ph[:, 0].reshape(256, HEAD)
    keys[1024 : 1024 + ROWS, :] = fk[...]
    vals[0:768, :] = kv[:, 1].reshape(768, HEAD)
    vals[768:1024, :] = ph[:, 1].reshape(256, HEAD)
    vals[1024 : 1024 + ROWS, :] = fv[...]
    lane = lax.broadcasted_iota(jnp.int32, (ROWS, HEAD), 1)
    for half in range(2):
        ext = jnp.zeros((ROWS, HEAD), F32)
        for h0 in range(0, 8, 4):
            parts = []
            for h in range(h0, h0 + 4):
                g = half * 8 + h
                parts.append(q[:, g * HEAD : (g + 1) * HEAD])
            qs = jnp.concatenate(parts, axis=0)
            s = dot(qs, keys[...], ((1,), (1,)))
            s = (s.reshape(4, ROWS, KEYS) + bias[...][None]).reshape(4 * ROWS, KEYS)
            top = jnp.max(s, axis=-1, keepdims=True)
            p = jnp.exp((s - top) * SCALE)
            mass = jnp.sum(p, axis=-1, keepdims=True)
            o = dot(p.astype(BF), vals[...]) / mass
            for n in range(4):
                h = h0 + n
                rows = slice(n * ROWS, (n + 1) * ROWS)
                out[half, :, h * HEAD : (h + 1) * HEAD] = o[rows].astype(BF)
                ext = jnp.where(lane == h, top[rows], ext)
                ext = jnp.where(lane == 64 + h, mass[rows], ext)
        high = ext.astype(BF).astype(F32)
        rest = ext - high
        mid = rest.astype(BF).astype(F32)
        low = rest - mid
        packed = high + pltpu.roll(mid, 8, 1) + pltpu.roll(low, 16, 1)
        out[half, :, 8 * HEAD : 9 * HEAD] = packed.astype(BF)


def attention(place, owner, fill, phase_owner, phase_fill, relay, q, kv, ph, fresh):
    smem = pl.BlockSpec(memory_space=pltpu.SMEM)
    return pl.pallas_call(
        attention_kernel,
        grid=(KV_HEADS,),
        in_specs=[smem] * 6
        + [
            pl.BlockSpec((ROWS, 16 * HEAD), lambda k: (0, k)),
            pl.BlockSpec((24, 2, 32, HEAD), lambda k: (0, 0, 0, k)),
            pl.BlockSpec((8, 2, 32, HEAD), lambda k: (0, 0, 0, k)),
            pl.BlockSpec((ROWS, HEAD), lambda k: (0, k)),
            pl.BlockSpec((ROWS, HEAD), lambda k: (0, KV_HEADS + k)),
        ],
        out_specs=pl.BlockSpec((2, ROWS, 9 * HEAD), lambda k: (k, 0, 0)),
        out_shape=jax.ShapeDtypeStruct((NC, ROWS, 9 * HEAD), BF),
        scratch_shapes=[
            pltpu.VMEM((ROWS, KEYS), F32),
            pltpu.VMEM((KEYS, HEAD), BF),
            pltpu.VMEM((KEYS, HEAD), BF),
        ],
        compiler_params=params(),
        name="attention",
    )(place, owner, fill, phase_owner, phase_fill, relay, q, kv, ph, fresh, fresh)


def join_kernel(parts, out):
    tops, masses = [], []
    for c in range(NC):
        ext = parts[c, :, 8 * HEAD :].astype(F32)
        ext = ext + pltpu.roll(ext, HEAD - 8, 1) + pltpu.roll(ext, HEAD - 16, 1)
        tops.append(ext)
        masses.append(pltpu.roll(ext, 64, 1))
    best = functools.reduce(jnp.maximum, tops)
    weights = [m * jnp.exp((t - best) * SCALE) for t, m in zip(tops, masses)]
    total = functools.reduce(jnp.add, weights)
    shares = [w / total for w in weights]
    for h in range(8):
        cols = slice(h * HEAD, (h + 1) * HEAD)
        acc = shares[0][:, h : h + 1] * parts[0, :, cols].astype(F32)
        for c in range(1, NC):
            acc = acc + shares[c][:, h : h + 1] * parts[c, :, cols].astype(F32)
        out[:, cols] = acc.astype(BF)


def join(parts):
    return pl.pallas_call(
        join_kernel,
        out_shape=jax.ShapeDtypeStruct((ROWS, 8 * HEAD), BF),
        compiler_params=params(),
        name="join",
    )(parts)


def project_kernel(place, a0, a1, a2, a3, w, out, rows):
    @pl.when(pl.program_id(0) == 0)
    def _():
        for d, a in enumerate((a0, a1, a2, a3)):
            at = pl.multiple_of(lax.rem(place[1] + d, NX) * ROWS, 16)
            rows[pl.ds(at, ROWS), :] = a[...]

    for n in range(2):
        out[n] = dot(rows[...], w[n]).astype(BF)


def project(place, pieces, w):
    whole = pl.BlockSpec((ROWS, 8 * HEAD), lambda k: (0, 0))
    return pl.pallas_call(
        project_kernel,
        grid=(NZ // 2,),
        in_specs=[pl.BlockSpec(memory_space=pltpu.SMEM)]
        + [whole] * 4
        + [pl.BlockSpec((2, 8 * HEAD, HEAD), lambda k: (k, 0, 0))],
        out_specs=pl.BlockSpec((2, ALL, HEAD), lambda k: (k, 0, 0)),
        out_shape=jax.ShapeDtypeStruct((NZ, ALL, HEAD), BF),
        scratch_shapes=[pltpu.VMEM((ALL, 8 * HEAD), BF)],
        compiler_params=params(),
        name="project",
    )(place, *pieces, w)


def add_kernel(parts, out):
    acc = parts[0].astype(F32)
    for c in range(1, NC):
        acc = acc + parts[c].astype(F32)
    out[...] = acc.astype(BF)


def add_up(parts):
    return pl.pallas_call(
        add_kernel,
        out_shape=jax.ShapeDtypeStruct((ALL, HEAD), BF),
        compiler_params=params(),
        name="add_up",
    )(parts)


def floor_div(value, by):
    return jnp.floor((value + 0.5) * (1.0 / by))


def slot_fields(value):
    z = floor_div(value, 96)
    rest = value - 96 * z
    ex = floor_div(rest, 48)
    rest = rest - 48 * ex
    block = floor_div(rest, CAP)
    spot = rest - CAP * block
    return z, ex, block, spot


def routes_kernel(place, t0, t1, t2, t3, send, mix_high, mix_low, ids, gates):
    for d, t in enumerate((t0, t1, t2, t3)):
        at = pl.multiple_of(lax.rem(place[1] + d, NX) * ROWS, 16)
        ids[pl.ds(at, ROWS), :] = t[0]
        gates[pl.ds(at, ROWS), :] = t[1]
    x_here = place[1].astype(F32)
    expert = lax.broadcasted_iota(jnp.int32, (ALL, 64), 1).astype(F32)
    gate_rows = gates[...]
    share = gate_rows / jnp.sum(gate_rows, axis=-1, keepdims=True)
    id_rows = ids[...]
    hit = jnp.zeros((ALL, 64), F32)
    mix = jnp.zeros((ALL, 64), F32)
    for k in range(TOPK):
        same = id_rows[:, k : k + 1] == expert
        hit = jnp.where(same, 1.0, hit)
        mix = jnp.where(same, share[:, k : k + 1], mix)
    row_a = lax.broadcasted_iota(jnp.int32, (ALL, ALL), 0).astype(F32)
    row_b = lax.broadcasted_iota(jnp.int32, (ALL, ALL), 1).astype(F32)
    earlier = (row_b < row_a) & (floor_div(row_a, 24) == floor_div(row_b, 24))
    before = dot(jnp.where(earlier, 1.0, 0.0).astype(BF), hit.astype(BF))
    mark = jnp.where(hit > 0, before + 1.0, 0.0).astype(BF)
    mix_a = mix.astype(BF)
    mix_b = (mix - mix_a.astype(F32)).astype(BF)

    slot = lax.broadcasted_iota(jnp.int32, (SLOTS, 64), 0).astype(F32)
    z, ex, _, _ = slot_fields(slot)
    e_here = lax.broadcasted_iota(jnp.int32, (SLOTS, 64), 1).astype(F32)
    pick = jnp.where(e_here == 8 * z + 2 * x_here + ex, 1.0, 0.0).astype(BF)
    marked = dot(pick, mark, ((1,), (1,)))
    slot = lax.broadcasted_iota(jnp.int32, (SLOTS, ALL), 0).astype(F32)
    _, _, block, spot = slot_fields(slot)
    row = lax.broadcasted_iota(jnp.int32, (SLOTS, ALL), 1).astype(F32)
    chosen = (marked == spot + 1.0) & (floor_div(row, 24) == block)
    send[...] = jnp.where(chosen, 1.0, 0.0).astype(BF)

    slot = lax.broadcasted_iota(jnp.int32, (64, SLOTS), 1).astype(F32)
    z, ex, _, _ = slot_fields(slot)
    e_here = lax.broadcasted_iota(jnp.int32, (64, SLOTS), 0).astype(F32)
    pick = jnp.where(e_here == 8 * z + 2 * x_here + ex, 1.0, 0.0).astype(BF)
    marked = dot(mark, pick)
    slot = lax.broadcasted_iota(jnp.int32, (ALL, SLOTS), 1).astype(F32)
    _, _, block, spot = slot_fields(slot)
    row = lax.broadcasted_iota(jnp.int32, (ALL, SLOTS), 0).astype(F32)
    chosen = (marked == spot + 1.0) & (floor_div(row, 24) == block)
    mix_high[...] = jnp.where(chosen, dot(mix_a, pick), 0.0).astype(BF)
    mix_low[...] = jnp.where(chosen, dot(mix_b, pick), 0.0).astype(BF)


def routes(place, tables):
    vm = pl.BlockSpec(memory_space=pltpu.VMEM)
    return pl.pallas_call(
        routes_kernel,
        in_specs=[pl.BlockSpec(memory_space=pltpu.SMEM)] + [vm] * 4,
        out_specs=[vm] * 3,
        out_shape=[
            jax.ShapeDtypeStruct((SLOTS, ALL), BF),
            jax.ShapeDtypeStruct((ALL, SLOTS), BF),
            jax.ShapeDtypeStruct((ALL, SLOTS), BF),
        ],
        scratch_shapes=[pltpu.VMEM((ALL, TOPK), F32), pltpu.VMEM((ALL, TOPK), F32)],
        compiler_params=params(),
        name="routes",
    )(place, *tables)


def dispatch_kernel(place, h0, h1, h2, h3, p0, p1, p2, p3, send, packed, mine, rows):
    for d, (h, p) in enumerate(zip((h0, h1, h2, h3), (p0, p1, p2, p3))):
        there = lax.rem(place[1] + d, NX)
        at = pl.multiple_of(there * ROWS, 16)
        rows[pl.ds(at, ROWS), :] = h[...].astype(F32)
    for d, p in enumerate((p0, p1, p2, p3)):
        at = pl.multiple_of(lax.rem(place[1] + d, NX) * HEAD, HEAD)
        rows[:, pl.ds(at, HEAD)] = rows[:, pl.ds(at, HEAD)] + p[...].astype(F32)
    mine[...] = rows[pl.ds(pl.multiple_of(place[1] * ROWS, 16), ROWS), :]
    packed[...] = dot(send[...], rows[...].astype(BF)).astype(BF)


def dispatch(place, hidden, projected, send):
    vm = pl.BlockSpec(memory_space=pltpu.VMEM)
    return pl.pallas_call(
        dispatch_kernel,
        in_specs=[pl.BlockSpec(memory_space=pltpu.SMEM)] + [vm] * 9,
        out_specs=[vm] * 2,
        out_shape=[
            jax.ShapeDtypeStruct((SLOTS, COLS), BF),
            jax.ShapeDtypeStruct((ROWS, COLS), F32),
        ],
        scratch_shapes=[pltpu.VMEM((ALL, COLS), F32)],
        compiler_params=params(),
        name="dispatch",
    )(place, *hidden, *projected, send)


def up_kernel(x, wg, wu, out, gate, up, square):
    c = pl.program_id(1)
    rows = x[...].reshape(NZ * ROWS, COLS)
    part_gate = dot(rows, wg[0])
    part_up = dot(rows, wu[0])
    wide = rows.astype(F32)
    part_square = jnp.sum(wide * wide, axis=-1, keepdims=True)

    @pl.when(c == 0)
    def _():
        gate[...] = part_gate
        up[...] = part_up
        square[...] = part_square

    @pl.when(c > 0)
    def _():
        gate[...] += part_gate
        up[...] += part_up
        square[...] += part_square

    @pl.when(c == NC - 1)
    def _():
        scale = lax.rsqrt(square[...] * (1.0 / WIDTH) + EPS)
        v = gate[...] * scale
        out[0] = (v / (1.0 + jnp.exp(-v)) * (up[...] * scale)).astype(BF)


def expert_up(x, wg, wu):
    n = NZ * ROWS
    return pl.pallas_call(
        up_kernel,
        grid=(2, NC),
        in_specs=[
            pl.BlockSpec((1, NZ, 1, ROWS, COLS), lambda e, c: (c, 0, e, 0, 0)),
            pl.BlockSpec((1, COLS, FFS), lambda e, c: (e, c, 0)),
            pl.BlockSpec((1, COLS, FFS), lambda e, c: (e, c, 0)),
        ],
        out_specs=pl.BlockSpec((1, n, FFS), lambda e, c: (e, 0, 0)),
        out_shape=jax.ShapeDtypeStruct((2, n, FFS), BF),
        scratch_shapes=[pltpu.VMEM((n, FFS), F32), pltpu.VMEM((n, FFS), F32), pltpu.VMEM((n, 1), F32)],
        compiler_params=params(),
        name="expert_up",
    )(x, wg, wu)


def down_kernel(h, w, out):
    acc = dot(h[0, 0], w[0, 0])
    for c in range(1, NC):
        acc = acc + dot(h[c, 0], w[c, 0])
    out[...] = acc.astype(BF).reshape(NZ, 1, ROWS, COLS)


def expert_down(h, w):
    n = NZ * ROWS
    return pl.pallas_call(
        down_kernel,
        grid=(2,),
        in_specs=[
            pl.BlockSpec((NC, 1, n, FFS), lambda e: (0, e, 0, 0)),
            pl.BlockSpec((NC, 1, FFS, COLS), lambda e: (0, e, 0, 0)),
        ],
        out_specs=pl.BlockSpec((NZ, 1, ROWS, COLS), lambda e: (0, e, 0, 0)),
        out_shape=jax.ShapeDtypeStruct((NZ, 2, ROWS, COLS), BF),
        compiler_params=params(),
        name="expert_down",
    )(h, w)


def mix_kernel(place, back, mix_high, mix_low, o0, o1, o2, o3, rows):
    rows[...] = dot(mix_high[...], back[...]) + dot(mix_low[...], back[...])
    for d, o in enumerate((o0, o1, o2, o3)):
        at = pl.multiple_of(lax.rem(place[1] + d, NX) * ROWS, 16)
        o[...] = rows[pl.ds(at, ROWS), :].astype(o.dtype)


def mix_back(place, back, mix_high, mix_low):
    vm = pl.BlockSpec(memory_space=pltpu.VMEM)
    return pl.pallas_call(
        mix_kernel,
        in_specs=[pl.BlockSpec(memory_space=pltpu.SMEM)] + [vm] * 3,
        out_specs=[vm] * 4,
        out_shape=[jax.ShapeDtypeStruct((ROWS, COLS), F32)]
        + [jax.ShapeDtypeStruct((ROWS, COLS), BF)] * 3,
        scratch_shapes=[pltpu.VMEM((ALL, COLS), F32)],
        compiler_params=params(),
        name="mix_back",
    )(place, back, mix_high, mix_low)


def from_x(value, d):
    return lax.ppermute(value, "x", [((i + d) % NX, i) for i in range(NX)])


def along_x(value):
    return [value] + [from_x(value, d) for d in range(1, NX)]


def body(
    kv_cache,
    slot_owner,
    slot_fill,
    phased,
    phase_owner,
    phase_fill,
    relay_page,
    relay_slot,
    queries,
    new_kv,
    hidden_in,
    o_proj,
    expert_ids,
    gate_weights,
    w_gate,
    w_up,
    w_down,
):
    del relay_slot
    ctx = lax.axis_index(CTX)
    place = jnp.stack([ctx, lax.axis_index("x")]).astype(jnp.int32)

    with jax.named_scope("gather_projection"):
        o_cols = lax.all_gather(o_proj, "z")
    with jax.named_scope("gather_tables"):
        table = jnp.stack(
            [expert_ids.reshape(ROWS, TOPK).astype(F32), gate_weights.reshape(ROWS, TOPK)]
        )
        tables = along_x(table)
    with jax.named_scope("gather_hidden"):
        hidden_cols = lax.dynamic_slice_in_dim(hidden_in, ctx * COLS, COLS, 3).reshape(ROWS, COLS)
        hidden = along_x(hidden_cols)
    with jax.named_scope("turn_down"):
        down_cols = lax.all_to_all(
            w_down.reshape(2, FFS, NC, COLS).transpose(2, 0, 1, 3), CTX, 0, 0, tiled=True
        )

    with jax.named_scope("attend"):
        parts = attention(
            place,
            slot_owner,
            slot_fill,
            phase_owner,
            phase_fill,
            relay_page[0],
            queries.reshape(ROWS, HEADS * HEAD),
            kv_cache[0],
            phased[0],
            new_kv.reshape(ROWS, 2 * KV_HEADS * HEAD),
        )
    with jax.named_scope("join_parts"):
        parts = lax.all_to_all(parts, CTX, 0, 0, tiled=True)
        attended = join(parts)
    with jax.named_scope("project_rows"):
        partial = project(place, along_x(attended), o_cols)
    with jax.named_scope("sum_projection"):
        columns = add_up(lax.all_to_all(partial, CTX, 0, 0, tiled=True))
        projected = along_x(columns)
    with jax.named_scope("find_routes"):
        send, mix_high, mix_low = routes(place, tables)
    with jax.named_scope("dispatch_rows"):
        packed, mine = dispatch(place, hidden, projected, send)
        arrived = lax.all_to_all(packed.reshape(NZ, 96, COLS), "z", 0, 0, tiled=True)
    with jax.named_scope("gather_rows"):
        rows = lax.all_gather(arrived, CTX).reshape(NC, NZ, 2, ROWS, COLS)
    with jax.named_scope("up"):
        units = expert_up(rows, w_gate, w_up)
    with jax.named_scope("gather_units"):
        units = lax.all_gather(units, CTX)
    with jax.named_scope("down"):
        outcome = expert_down(units, down_cols)
    with jax.named_scope("return_rows"):
        back = lax.all_to_all(outcome.reshape(NZ, 96, COLS), "z", 0, 0, tiled=True)
    with jax.named_scope("mix"):
        mixed = mix_back(place, back.reshape(SLOTS, COLS), mix_high, mix_low)
        total = mine + mixed[0]
        for d in range(1, NX):
            total = total + from_x(mixed[d], NX - d).astype(F32)
    return total.astype(BF).reshape(2, 4, 6, COLS)


def solution(mesh):
    inner = Mesh(mesh.devices.reshape(NY, NCORE, NZ, NX), ("y", "core", "z", "x"))
    exp = ("z", "x")
    in_specs = (
        P(exp, CTX, None, None, None),
        P(exp, CTX),
        P(exp, CTX),
        P(exp, CTX, None, None, None),
        P(exp, None),
        P(exp, None),
        P(exp, None, None),
        P(exp, None, None),
        P(None, exp, None, None),
        P(None, exp, None, None, None),
        P(None, exp, None, None),
        P(CTX, exp),
        P(None, exp, None, None),
        P(None, exp, None, None),
        P(exp, None, CTX),
        P(exp, None, CTX),
        P(exp, CTX, None),
    )
    out_specs = P(None, exp, None, CTX)
    return jax.shard_map(body, mesh=inner, in_specs=in_specs, out_specs=out_specs, check_vma=False)
```

time: 750 us -> 271 us (0.36); the launches traced: 737 us -> 269 us
  waiting for transfers between devices: 305 us -> 81.4 us
  matrix products: 94 us -> 0 us
  local copies, waits for them, and re-layouts: 126 us -> 34.8 us
  other arithmetic: 89.6 us -> 0.12 us
  Pallas kernels: 0 us -> 33.5 us
  starting transfers between devices: 53.7 us -> 34.5 us
  blocking collectives: 54.2 us -> 71 us
    all_to_all x7 -> x2, waiting for transfers between devices: 126 us -> 12.4 us  [the longest x1 12.4 us: body(): lax.all_to_all(w_down.reshape(2, FFS, NC, COLS).transpose(2, 0, 1, 3), CT...]
    dot_general x28 -> x0, matrix products: 94 us -> none  [the longest x2 15.2 us: body(): jnp.einsum('erf,efd->erd', hidden_units, w_down, preferred_element_type=j...]
    all_to_all x0 -> x3, blocking collectives: none -> 71 us  [the longest x1 29.7 us: body(): back = lax.all_to_all(outcome.reshape(NZ, 96, COLS), 'z', 0, 0, tiled=True)]
    psum x1 -> x0, waiting for transfers between devices: 58.6 us -> none  [body(): projected = lax.psum(spread.astype(jnp.bfloat16), 'ctx').astype(jnp.float32)]
    all_gather x4 -> x0, blocking collectives: 54.2 us -> none  [combined_all(): pieces = jax.tree.map(lambda part: lax.all_gather(part, axis), value)]
    add x30 -> x0, other arithmetic: 51.2 us -> none  [the longest x14 38.7 us: join_parts(): sum_a * scale_a[..., None] + sum_b * scale_b[..., None]]
    all_to_all x7 -> x2, starting transfers between devices: 53.1 us -> 11 us  [the longest x1 5.99 us: body(): lax.all_to_all(w_down.reshape(2, FFS, NC, COLS).transpose(2, 0, 1, 3), CT...]
    all_gather x4 -> x3, waiting for transfers between devices: 96.7 us -> 58.1 us  [the longest x1 28.9 us: body(): units = lax.all_gather(units, CTX)]
  transfers between devices with their start and end apart: 14 -> 20, of which waited for: 7 -> 12; matrix products, arithmetic and copies ran while one was open for 30% -> 9% of each run, Pallas kernels for 0% -> 5%
where the time goes in v1:
time: 271 us; the launch traced here: 269 us
  waiting for transfers between devices  81.4 us (30%)
  blocking collectives  71 us (26%)
  local copies, waits for them, and re-layouts  34.8 us (13%)
  starting transfers between devices  34.5 us (13%)
  Pallas kernels  33.5 us (12%)
  between operations  13.4 us (5%)
    all_to_all x1, blocking collectives, body(): back = lax.all_to_all(outcome.reshape(NZ, 96, COLS), 'z', 0, 0, tiled=True)  29.7 us
    all_gather x1, waiting for transfers between devices, body(): units = lax.all_gather(units, CTX)  28.9 us
    all_gather x1, waiting for transfers between devices, body(): rows = lax.all_gather(arrived, CTX).reshape(NC, NZ, 2, ROWS, COLS)  26.1 us
    all_to_all x1, blocking collectives, body(): lax.all_to_all(packed.reshape(NZ, 96, COLS), 'z', 0, 0, tiled=True)  24.5 us
    ppermute x15, starting transfers between devices, from_x(): return lax.ppermute(value, 'x', [((i + d) % NX, i) for i in range(NX)])  23.4 us
    unnamed x49, local copies, waits for them, and re-layouts  22.9 us
    all_to_all x1, blocking collectives, body(): parts = lax.all_to_all(parts, CTX, 0, 0, tiled=True)  16.7 us
    pallas_call x1, Pallas kernels, expert_up(): pl.pallas_call(up_kernel, grid=(2, NC), in_specs=[pl.BlockSpec((1, NZ, 1,...  12.9 us
  transfers between devices with their start and end apart: 20, of which 12 were waited for; matrix products, arithmetic and copies ran while one was open for 9% of the time, Pallas kernels for 5%

profile of v1, /device:TPU:24, one launch (start us, length us, event | category | flops | bytes accessed | tf_op | source)
XLA Modules:
  0.0 268.6 jit_solution(13413710923835008191)
XLA Ops:
  7.3 2.6 copy.35
  9.9 1.5 reshape.43.q
  11.6 10.4 %attention.1 = bf16[8,48,1152]{2,1,0:T(8,128)(2,1)S(1)} custom-call(s32[2]{0:T(128)S(1)} %pad_add_fusion.place, s32[1,24]{1,0:T(1,128)S(1)} %copy-done.14, s32[1,24]{1,0:T(1,128)S(1)} %copy-done.15, s32[1,64]{1,0:T(1,128)S(1)} %copy-done.16, s32[1,64]{1,0:T(1,128)S(1)} %copy-done.17, s32[8,8]{1,0:T(8,128)S(1)} %bitcast.34, bf16[48,8192]{1,0:T(8,128)(2,1)S(1)} %reshape.43.q, ...), custom_call_target="tpu_custom_call" | custom-call | tf_op jit(solution)/shard_map/attend/attention/pallas_call | solution.py:123
  22.0 16.7 %all_to_all.25.parts = bf16[8,48,1152]{2,1,0:T(8,128)(2,1)S(1)} all-to-all(bf16[8,48,1152]{2,1,0:T(8,128)(2,1)S(1)} %attention.1), channel_id=1, replica_groups=mesh['y'=4,'core'=2,'z'=8,'x'=4] {'y','core'}, dimensions={0} | all-to-all | bytes 1769472 | tf_op jit(solution)/shard_map/join_parts/all_to_all | solution.py:473
  39.5 2.8 %collective-permute-start.3 = (bf16[48,1024]{1,0:T(8,128)(2,1)S(1)}, bf16[48,1024]{1,0:T(8,128)(2,1)S(1)}, u32[]{:S(2)}, u32[]{:S(2)}) collective-permute-start(bf16[48,1024]{1,0:T(8,128)(2,1)S(1)} %join.1.a0), channel_id=1, source_target_pairs={{1,0},{2,1},{3,2},{0,3},{5,4},{6,5},{7,6},{4,7},{9,8},{10,9},{11,1... | collective-permute-start | bytes 294920 | tf_op jit(solution)/shard_map/project_rows/ppermute | solution.py:414
  44.0 2.4 collective-permute-done.3.a1
  46.4 2.7 collective-permute-done.4.a2
  50.1 3.0 %all-gather.7.cloned.1.call-done = bf16[8192,128]{1,0:T(8,128)(2,1)} async-done(((bf16[1024,128]{1,0:T(8,128)(2,1)}), bf16[8192,128]{1,0:T(8,128)(2,1)}) %all-gather.7.cloned.1.call-update) | async-done | bytes 2097168 | tf_op jit(solution)/shard_map/gather_projection/all_gather | solution.py:445
  53.1 1.6 copy-done.4
  54.7 3.0 %project.1 = bf16[8,192,128]{2,1,0:T(8,128)(2,1)} custom-call(s32[2]{0:T(128)S(1)} %pad_add_fusion.place, bf16[48,1024]{1,0:T(8,128)(2,1)S(1)} %join.1.a0, bf16[48,1024]{1,0:T(8,128)(2,1)S(1)} %collective-permute-done.3.a1, bf16[48,1024]{1,0:T(8,128)(2,1)S(1)} %collective-permute-done.4.a2, bf16[48,1024]{1,0:T(8,128)(2,1)S(1)} %collective-permute-done.5.a3, ...), custom_call_target="tpu_custom_call" | custom-call | tf_op jit(solution)/shard_map/project_rows/project/pallas_call | solution.py:187
  57.7 5.0 %all-to-all-start.1 = ((bf16[8,192,128]{2,1,0:T(8,128)(2,1)}), bf16[8,192,128]{2,1,0:T(8,128)(2,1)S(1)}, u32[]{:S(2)}, u32[]{:S(2)}) async-start(bf16[8,192,128]{2,1,0:T(8,128)(2,1)} %project.1), calls=%async_computation.1 | async-start | bytes 786432 | tf_op jit(solution)/shard_map/sum_projection/all_to_all | solution.py:478
  62.8 2.8 %collective-permute-start = (bf16[48,512]{1,0:T(8,128)(2,1)S(1)}, bf16[48,512]{1,0:T(8,128)(2,1)S(1)}, u32[]{:S(2)}, u32[]{:S(2)}) collective-permute-start(bf16[48,512]{1,0:T(8,128)(2,1)S(1)} %reshape.42.h0), channel_id=1, source_target_pairs={{1,0},{2,1},{3,2},{0,3},{5,4},{6,5},{7,6},{4,7},{9,8},{10,9},{11,1... | collective-permute-start | bytes 147464 | tf_op jit(solution)/shard_map/gather_hidden/ppermute | solution.py:414
  68.1 2.3 collective-permute-start.9
  72.5 2.8 %collective-permute-start.6 = (bf16[192,128]{1,0:T(8,128)(2,1)S(1)}, bf16[192,128]{1,0:T(8,128)(2,1)S(1)}, u32[]{:S(2)}, u32[]{:S(2)}) collective-permute-start(bf16[192,128]{1,0:T(8,128)(2,1)S(1)} %add_up.1.p0), channel_id=1, source_target_pairs={{1,0},{2,1},{3,2},{0,3},{5,4},{6,5},{7,6},{4,7},{9,8},{10,9},{11,1... | collective-permute-start | bytes 147464 | tf_op jit(solution)/shard_map/sum_projection/ppermute | solution.py:414
  77.1 1.8 routes.1
  83.1 24.5 %all_to_all.26 = bf16[8,96,512]{2,1,0:T(8,128)(2,1)} all-to-all(bf16[8,96,512]{2,1,0:T(8,128)(2,1)S(1)} %bitcast.32), channel_id=1, replica_groups=mesh['y'=4,'core'=2,'z'=8,'x'=4] {'z'}, dimensions={0} | all-to-all | bytes 1572864 | tf_op jit(solution)/shard_map/dispatch_rows/all_to_all | solution.py:484
  107.7 6.2 %copy.42.wg = bf16[2,4096,192]{2,1,0:T(8,128)(2,1)} copy(bf16[2,4096,192]{1,2,0:T(8,128)(2,1)} %param.30) | data formatting | bytes 6291456 | tf_op args[14]
  113.9 4.0 %copy.43.wu = bf16[2,4096,192]{2,1,0:T(8,128)(2,1)} copy(bf16[2,4096,192]{1,2,0:T(8,128)(2,1)S(1)} %copy-done.18) | data formatting | bytes 6291456 | tf_op args[15]
  117.9 26.1 %all-gather.9.cloned.1.call-done = bf16[64,96,512]{2,1,0:T(8,128)(2,1)} async-done(((bf16[8,96,512]{2,1,0:T(8,128)(2,1)}), bf16[64,96,512]{2,1,0:T(8,128)(2,1)}) %all-gather.9.cloned.1.call-update) | async-done | bytes 6291472 | tf_op jit(solution)/shard_map/gather_rows/all_gather | solution.py:486
  144.1 2.2 copy-done.1
  146.3 2.2 copy-done.2
  148.4 12.9 %expert_up.1 = bf16[2,384,192]{2,1,0:T(8,128)(2,1)S(1)} custom-call(bf16[8,8,2,48,512]{4,3,2,1,0:T(8,128)(2,1)} %bitcast.36, bf16[2,4096,192]{2,1,0:T(8,128)(2,1)S(1)} %copy-done.1, bf16[2,4096,192]{2,1,0:T(8,128)(2,1)S(1)} %copy-done.2), custom_call_target="tpu_custom_call" | custom-call | tf_op jit(solution)/shard_map/up/expert_up/pallas_call | solution.py:353
  162.3 3.9 %copy.51 = bf16[2,24,8,8,512]{4,3,1,0,2:T(8,128)(2,1)} copy(bf16[2,24,8,8,512]{4,3,2,1,0:T(8,128)(2,1)} %bitcast.37) | data formatting | bytes 6291456 | tf_op jit(solution)/shard_map/turn_down/reshape | solution.py:456
  166.1 6.0 %all-to-all-start.3 = ((bf16[8,2,192,512]{3,2,1,0:T(8,128)(2,1)}), bf16[8,2,192,512]{3,2,1,0:T(8,128)(2,1)S(1)}, u32[]{:S(2)}, u32[]{:S(2)}) async-start(bf16[8,2,192,512]{3,2,1,0:T(8,128)(2,1)} %bitcast.35), calls=%async_computation.3 | async-start | bytes 6291456 | tf_op jit(solution)/shard_map/turn_down/all_to_all | solution.py:455
  172.1 28.9 %all-gather.11.cloned.1.call-done = bf16[16,384,192]{1,2,0:T(8,128)(2,1)} async-done(((bf16[2,384,192]{1,2,0:T(8,128)(2,1)}), bf16[16,384,192]{1,2,0:T(8,128)(2,1)}) %all-gather.11.cloned.1.call-update) | async-done | bytes 2359312 | tf_op jit(solution)/shard_map/gather_units/all_gather | solution.py:490
  201.0 4.5 %copy.45 = bf16[16,384,192]{2,1,0:T(8,128)(2,1)} copy(bf16[16,384,192]{1,2,0:T(8,128)(2,1)} %all-gather.11.cloned.1.call-done) | data formatting | bytes 4718592 | tf_op jit(solution)/shard_map/gather_units/all_gather | solution.py:490
  205.5 12.4 %all-to-all-done.3.w = bf16[8,2,192,512]{3,2,1,0:T(8,128)(2,1)S(1)} async-done(((bf16[8,2,192,512]{3,2,1,0:T(8,128)(2,1)}), bf16[8,2,192,512]{3,2,1,0:T(8,128)(2,1)S(1)}, u32[]{:S(2)}, u32[]{:S(2)}) %all-to-all-start.3) | async-done | bytes 3145760 | tf_op jit(solution)/shard_map/turn_down/all_to_all | solution.py:455
  218.0 1.9 copy-done.3
  219.8 2.4 expert_down.1
  222.3 29.7 %all_to_all.27 = bf16[8,96,512]{2,1,0:T(8,128)(2,1)S(1)} all-to-all(bf16[8,96,512]{2,1,0:T(8,128)(2,1)S(1)} %bitcast.26), channel_id=1, replica_groups=mesh['y'=4,'core'=2,'z'=8,'x'=4] {'z'}, dimensions={0} | all-to-all | bytes 1572864 | tf_op jit(solution)/shard_map/return_rows/all_to_all | solution.py:494
  253.1 1.5 collective-permute-start.12
  254.6 2.7 collective-permute-start.13
  (89 shorter events, 21.6 us)
Async XLA Ops:
  6.5 56.2 %copy-start = (bf16[2,4,6,4096]{3,1,2,0:T(4,128)(2,1)S(1)}, bf16[2,4,6,4096]{3,1,2,0:T(4,128)(2,1)}, u32[]{:S(2)}) copy-start(bf16[2,4,6,4096]{3,1,2,0:T(4,128)(2,1)} %param.26) | copy-start | bytes 1179652
  6.5 5.0 %copy-start.13 = (s32[1,8,8]{2,1,0:T(8,128)S(1)}, s32[1,8,8]{2,1,0:T(8,128)}, u32[]{:S(2)}) copy-start(s32[1,8,8]{2,1,0:T(8,128)} %param.23) | copy-start | bytes 772
  6.5 5.0 %copy-start.5 = (bf16[1,24,2,32,512]{4,3,2,1,0:T(8,128)(2,1)S(1)}, bf16[1,24,2,32,512]{4,3,2,1,0:T(8,128)(2,1)}, u32[]{:S(2)}) copy-start(bf16[1,24,2,32,512]{4,3,2,1,0:T(8,128)(2,1)} %param.17) | copy-start | bytes 4718596
  6.5 5.0 %copy-start.6 = (bf16[1,8,2,32,512]{4,3,2,1,0:T(8,128)(2,1)S(1)}, bf16[1,8,2,32,512]{4,3,2,1,0:T(8,128)(2,1)}, u32[]{:S(2)}) copy-start(bf16[1,8,2,32,512]{4,3,2,1,0:T(8,128)(2,1)} %param.20) | copy-start | bytes 1572868
  6.5 5.0 %copy-start.14 = (s32[1,24]{1,0:T(1,128)S(1)}, s32[1,24]{1,0:T(1,128)}, u32[]{:S(2)}) copy-start(s32[1,24]{1,0:T(1,128)} %owner.1) | copy-start | bytes 292
  6.6 5.0 %copy-start.15 = (s32[1,24]{1,0:T(1,128)S(1)}, s32[1,24]{1,0:T(1,128)}, u32[]{:S(2)}) copy-start(s32[1,24]{1,0:T(1,128)} %fill.1) | copy-start | bytes 292
  6.6 46.5 %all-gather.7.cloned.1.call-start = ((), (), s32[]{:S(2)}) async-start(), calls=%async_computation.5 | async-start | bytes 2359296 | tf_op jit(solution)/shard_map/gather_projection/all_gather | solution.py:445
  21.9 43.8 %copy-start.21 = (s32[2,4,6,8]{3,1,2,0:T(4,128)S(1)}, s32[2,4,6,8]{3,1,2,0:T(4,128)}, u32[]{:S(2)}) copy-start(s32[2,4,6,8]{3,1,2,0:T(4,128)} %param.28) | copy-start | bytes 4612
  21.9 44.0 %copy-start.20 = (f32[2,4,6,8]{3,1,2,0:T(4,128)S(1)}, f32[2,4,6,8]{3,1,2,0:T(4,128)}, u32[]{:S(2)}) copy-start(f32[2,4,6,8]{3,1,2,0:T(4,128)} %param.29) | copy-start | bytes 4612
  39.5 6.9 %collective-permute-start.3 = (bf16[48,1024]{1,0:T(8,128)(2,1)S(1)}, bf16[48,1024]{1,0:T(8,128)(2,1)S(1)}, u32[]{:S(2)}, u32[]{:S(2)}) collective-permute-start(bf16[48,1024]{1,0:T(8,128)(2,1)S(1)} %join.1.a0), channel_id=1, source_target_pairs={{1,0},{2,1},{3,2},{0,3},{5,4},{6,5},{7,6},{4,7},{9,8},{10,9},{11,1... | collective-permute-start | bytes 294920 | tf_op jit(solution)/shard_map/project_rows/ppermute | solution.py:414
  42.4 6.7 %collective-permute-start.4 = (bf16[48,1024]{1,0:T(8,128)(2,1)S(1)}, bf16[48,1024]{1,0:T(8,128)(2,1)S(1)}, u32[]{:S(2)}, u32[]{:S(2)}) collective-permute-start(bf16[48,1024]{1,0:T(8,128)(2,1)S(1)} %join.1.a0), channel_id=1, source_target_pairs={{2,0},{3,1},{0,2},{1,3},{6,4},{7,5},{4,6},{5,7},{10,8},{11,9},{8,1... | collective-permute-start | bytes 294920 | tf_op jit(solution)/shard_map/project_rows/ppermute | solution.py:414
  43.2 6.9 %collective-permute-start.5 = (bf16[48,1024]{1,0:T(8,128)(2,1)S(1)}, bf16[48,1024]{1,0:T(8,128)(2,1)S(1)}, u32[]{:S(2)}, u32[]{:S(2)}) collective-permute-start(bf16[48,1024]{1,0:T(8,128)(2,1)S(1)} %join.1.a0), channel_id=1, source_target_pairs={{3,0},{0,1},{1,2},{2,3},{7,4},{4,5},{5,6},{6,7},{11,8},{8,9},{9,10... | collective-permute-start | bytes 294920 | tf_op jit(solution)/shard_map/project_rows/ppermute | solution.py:414
  57.7 14.2 %all-to-all-start.1 = ((bf16[8,192,128]{2,1,0:T(8,128)(2,1)}), bf16[8,192,128]{2,1,0:T(8,128)(2,1)S(1)}, u32[]{:S(2)}, u32[]{:S(2)}) async-start(bf16[8,192,128]{2,1,0:T(8,128)(2,1)} %project.1), calls=%async_computation.1 | async-start | bytes 786432 | tf_op jit(solution)/shard_map/sum_projection/all_to_all | solution.py:478
  62.8 81.3 %all-gather.9.cloned.1.call-start = ((), (), s32[]{:S(2)}) async-start(), calls=%async_computation.6 | async-start | bytes 7077888 | tf_op jit(solution)/shard_map/gather_rows/all_gather | solution.py:486
  62.8 13.3 %collective-permute-start = (bf16[48,512]{1,0:T(8,128)(2,1)S(1)}, bf16[48,512]{1,0:T(8,128)(2,1)S(1)}, u32[]{:S(2)}, u32[]{:S(2)}) collective-permute-start(bf16[48,512]{1,0:T(8,128)(2,1)S(1)} %reshape.42.h0), channel_id=1, source_target_pairs={{1,0},{2,1},{3,2},{0,3},{5,4},{6,5},{7,6},{4,7},{9,8},{10,9},{11,1... | collective-permute-start | bytes 147464 | tf_op jit(solution)/shard_map/gather_hidden/ppermute | solution.py:414
  66.2 5.7 %collective-permute-start.10 = (f32[2,48,8]{2,1,0:T(8,128)S(1)}, f32[2,48,8]{2,1,0:T(8,128)S(1)}, u32[]{:S(2)}, u32[]{:S(2)}) collective-permute-start(f32[2,48,8]{2,1,0:T(8,128)S(1)} %copy.41.t0), channel_id=1, source_target_pairs={{2,0},{3,1},{0,2},{1,3},{6,4},{7,5},{4,6},{5,7},{10,8},{11,9},{8,1... | collective-permute-start | bytes 9224 | tf_op jit(solution)/shard_map/gather_tables/ppermute | solution.py:414
  67.1 5.3 %collective-permute-start.11 = (f32[2,48,8]{2,1,0:T(8,128)S(1)}, f32[2,48,8]{2,1,0:T(8,128)S(1)}, u32[]{:S(2)}, u32[]{:S(2)}) collective-permute-start(f32[2,48,8]{2,1,0:T(8,128)S(1)} %copy.41.t0), channel_id=1, source_target_pairs={{3,0},{0,1},{1,2},{2,3},{7,4},{4,5},{5,6},{6,7},{11,8},{8,9},{9,10... | collective-permute-start | bytes 9224 | tf_op jit(solution)/shard_map/gather_tables/ppermute | solution.py:414
  68.1 7.2 %collective-permute-start.9 = (f32[2,48,8]{2,1,0:T(8,128)S(1)}, f32[2,48,8]{2,1,0:T(8,128)S(1)}, u32[]{:S(2)}, u32[]{:S(2)}) collective-permute-start(f32[2,48,8]{2,1,0:T(8,128)S(1)} %copy.41.t0), channel_id=1, source_target_pairs={{1,0},{2,1},{3,2},{0,3},{5,4},{6,5},{7,6},{4,7},{9,8},{10,9},{11,1... | collective-permute-start | bytes 9224 | tf_op jit(solution)/shard_map/gather_tables/ppermute | solution.py:414
  70.4 9.9 %collective-permute-start.1 = (bf16[48,512]{1,0:T(8,128)(2,1)S(1)}, bf16[48,512]{1,0:T(8,128)(2,1)S(1)}, u32[]{:S(2)}, u32[]{:S(2)}) collective-permute-start(bf16[48,512]{1,0:T(8,128)(2,1)S(1)} %reshape.42.h0), channel_id=1, source_target_pairs={{2,0},{3,1},{0,2},{1,3},{6,4},{7,5},{4,6},{5,7},{10,8},{11,9},{8,1... | collective-permute-start | bytes 147464 | tf_op jit(solution)/shard_map/gather_hidden/ppermute | solution.py:414
  72.0 8.4 %collective-permute-start.2 = (bf16[48,512]{1,0:T(8,128)(2,1)S(1)}, bf16[48,512]{1,0:T(8,128)(2,1)S(1)}, u32[]{:S(2)}, u32[]{:S(2)}) collective-permute-start(bf16[48,512]{1,0:T(8,128)(2,1)S(1)} %reshape.42.h0), channel_id=1, source_target_pairs={{3,0},{0,1},{1,2},{2,3},{7,4},{4,5},{5,6},{6,7},{11,8},{8,9},{9,10... | collective-permute-start | bytes 147464 | tf_op jit(solution)/shard_map/gather_hidden/ppermute | solution.py:414
  72.5 7.9 %collective-permute-start.6 = (bf16[192,128]{1,0:T(8,128)(2,1)S(1)}, bf16[192,128]{1,0:T(8,128)(2,1)S(1)}, u32[]{:S(2)}, u32[]{:S(2)}) collective-permute-start(bf16[192,128]{1,0:T(8,128)(2,1)S(1)} %add_up.1.p0), channel_id=1, source_target_pairs={{1,0},{2,1},{3,2},{0,3},{5,4},{6,5},{7,6},{4,7},{9,8},{10,9},{11,1... | collective-permute-start | bytes 147464 | tf_op jit(solution)/shard_map/sum_projection/ppermute | solution.py:414
  75.3 5.6 %collective-permute-start.7 = (bf16[192,128]{1,0:T(8,128)(2,1)S(1)}, bf16[192,128]{1,0:T(8,128)(2,1)S(1)}, u32[]{:S(2)}, u32[]{:S(2)}) collective-permute-start(bf16[192,128]{1,0:T(8,128)(2,1)S(1)} %add_up.1.p0), channel_id=1, source_target_pairs={{2,0},{3,1},{0,2},{1,3},{6,4},{7,5},{4,6},{5,7},{10,8},{11,9},{8,1... | collective-permute-start | bytes 147464 | tf_op jit(solution)/shard_map/sum_projection/ppermute | solution.py:414
  76.1 5.3 %collective-permute-start.8 = (bf16[192,128]{1,0:T(8,128)(2,1)S(1)}, bf16[192,128]{1,0:T(8,128)(2,1)S(1)}, u32[]{:S(2)}, u32[]{:S(2)}) collective-permute-start(bf16[192,128]{1,0:T(8,128)(2,1)S(1)} %add_up.1.p0), channel_id=1, source_target_pairs={{3,0},{0,1},{1,2},{2,3},{7,4},{4,5},{5,6},{6,7},{11,8},{8,9},{9,10... | collective-permute-start | bytes 147464 | tf_op jit(solution)/shard_map/sum_projection/ppermute | solution.py:414
  107.6 6.3 %copy-start.18 = (bf16[2,4096,192]{1,2,0:T(8,128)(2,1)S(1)}, bf16[2,4096,192]{1,2,0:T(8,128)(2,1)}, u32[]{:S(2)}) copy-start(bf16[2,4096,192]{1,2,0:T(8,128)(2,1)} %param.31) | copy-start | bytes 9437188
  107.6 93.4 %all-gather.11.cloned.1.call-start = ((), (), s32[]{:S(2)}) async-start(), calls=%async_computation.7 | async-start | bytes 2654208 | tf_op jit(solution)/shard_map/gather_units/all_gather | solution.py:490
  166.1 51.8 %all-to-all-start.3 = ((bf16[8,2,192,512]{3,2,1,0:T(8,128)(2,1)}), bf16[8,2,192,512]{3,2,1,0:T(8,128)(2,1)S(1)}, u32[]{:S(2)}, u32[]{:S(2)}) async-start(bf16[8,2,192,512]{3,2,1,0:T(8,128)(2,1)} %bitcast.35), calls=%async_computation.3 | async-start | bytes 6291456 | tf_op jit(solution)/shard_map/turn_down/all_to_all | solution.py:455
  219.8 32.1 %copy-start.8 = (bf16[192,768]{1,0:T(8,128)(2,1)S(1)}, bf16[192,768]{1,0:T(8,128)(2,1)}, u32[]{:S(2)}) copy-start(bf16[192,768]{1,0:T(8,128)(2,1)} %copy-done.7) | copy-start | bytes 884740
  219.8 32.1 %copy-start.10 = (bf16[192,768]{1,0:T(8,128)(2,1)S(1)}, bf16[192,768]{1,0:T(8,128)(2,1)}, u32[]{:S(2)}) copy-start(bf16[192,768]{1,0:T(8,128)(2,1)} %copy-done.9) | copy-start | bytes 884740
  219.8 41.5 %copy-start.12 = (f32[48,512]{1,0:T(8,128)S(1)}, f32[48,512]{1,0:T(8,128)}, u32[]{:S(2)}) copy-start(f32[48,512]{1,0:T(8,128)} %copy-done.11) | copy-start | bytes 294916
  253.1 5.7 %collective-permute-start.12 = (bf16[48,512]{1,0:T(8,128)(2,1)S(1)}, bf16[48,512]{1,0:T(8,128)(2,1)S(1)}, u32[]{:S(2)}, u32[]{:S(2)}) collective-permute-start(bf16[48,512]{1,0:T(8,128)(2,1)S(1)} %get-tuple-element.20), channel_id=1, source_target_pairs={{3,0},{0,1},{1,2},{2,3},{7,4},{4,5},{5,6},{6,7},{11,8},{8,9},{9,10... | collective-permute-start | bytes 147464 | tf_op jit(solution)/shard_map/mix/ppermute | solution.py:414
  254.6 5.6 %collective-permute-start.13 = (bf16[48,512]{1,0:T(8,128)(2,1)S(1)}, bf16[48,512]{1,0:T(8,128)(2,1)S(1)}, u32[]{:S(2)}, u32[]{:S(2)}) collective-permute-start(bf16[48,512]{1,0:T(8,128)(2,1)S(1)} %get-tuple-element.21), channel_id=1, source_target_pairs={{2,0},{3,1},{0,2},{1,3},{6,4},{7,5},{4,6},{5,7},{10,8},{11,9},{8,1... | collective-permute-start | bytes 147464 | tf_op jit(solution)/shard_map/mix/ppermute | solution.py:414
  257.3 4.1 %collective-permute-start.14 = (bf16[48,512]{1,0:T(8,128)(2,1)S(1)}, bf16[48,512]{1,0:T(8,128)(2,1)S(1)}, u32[]{:S(2)}, u32[]{:S(2)}) collective-permute-start(bf16[48,512]{1,0:T(8,128)(2,1)S(1)} %get-tuple-element.22), channel_id=1, source_target_pairs={{1,0},{2,1},{3,2},{0,3},{5,4},{6,5},{7,6},{4,7},{9,8},{10,9},{11,1... | collective-permute-start | bytes 147464 | tf_op jit(solution)/shard_map/mix/ppermute | solution.py:414
  (10 other events, 24.7 us)
Sparse Core Ops, SparseCore 0:
  9.2 43.8 all-gather.6
  107.7 36.2 all-gather.8
  162.4 38.5 all-gather.10

commit v2 on v1

--- a/solution.py
+++ b/solution.py
@@ -17,6 +17,7 @@
 ALL = NX * ROWS
 KEYS = 1152
 CAP = 6
+EXPERT_ROWS = 384
 SLOTS = NZ * 2 * NX * 2 * CAP
 WIDTH = 4096
 COLS = WIDTH // NC
@@ -45,7 +46,7 @@
 
 
 def attention_kernel(
-    place, owner, fill, phase_owner, phase_fill, relay, q, kv, ph, fk, fv, out, bias, keys, vals
+    place, owner, fill, phase_owner, phase_fill, relay, q, kv, ph, fk, fv, out, bias, keys, vals, qf
 ):
     @pl.when(pl.program_id(0) == 0)
     def _():
@@ -68,8 +69,8 @@
         row = lax.broadcasted_iota(jnp.int32, (ROWS, KEYS), 0)
         step = thresholds(row, 24, 2)
         rest = row - 24 * step
-        req = thresholds(rest, 6, 4)
-        draft = rest - 6 * req
+        draft = lax.shift_right_logical(rest, 2)
+        req = rest & 3
         fresh = lax.broadcasted_iota(jnp.int32, (ROWS, KEYS), 1) - 1024
         f_step = thresholds(fresh, 24, 2)
         f_rest = fresh - 24 * f_step
@@ -89,6 +90,8 @@
     vals[0:768, :] = kv[:, 1].reshape(768, HEAD)
     vals[768:1024, :] = ph[:, 1].reshape(256, HEAD)
     vals[1024 : 1024 + ROWS, :] = fv[...]
+    for n in range(12):
+        qf[n * 4 : n * 4 + 4, :] = q[n // 6, n % 6].astype(F32)
     lane = lax.broadcasted_iota(jnp.int32, (ROWS, HEAD), 1)
     for half in range(2):
         ext = jnp.zeros((ROWS, HEAD), F32)
@@ -96,7 +99,7 @@
             parts = []
             for h in range(h0, h0 + 4):
                 g = half * 8 + h
-                parts.append(q[:, g * HEAD : (g + 1) * HEAD])
+                parts.append(qf[:, g * HEAD : (g + 1) * HEAD].astype(BF))
             qs = jnp.concatenate(parts, axis=0)
             s = dot(qs, keys[...], ((1,), (1,)))
             s = (s.reshape(4, ROWS, KEYS) + bias[...][None]).reshape(4 * ROWS, KEYS)
@@ -125,7 +128,7 @@
         grid=(KV_HEADS,),
         in_specs=[smem] * 6
         + [
-            pl.BlockSpec((ROWS, 16 * HEAD), lambda k: (0, k)),
+            pl.BlockSpec((2, 6, 4, 16 * HEAD), lambda k: (0, 0, 0, k)),
             pl.BlockSpec((24, 2, 32, HEAD), lambda k: (0, 0, 0, k)),
             pl.BlockSpec((8, 2, 32, HEAD), lambda k: (0, 0, 0, k)),
             pl.BlockSpec((ROWS, HEAD), lambda k: (0, k)),
@@ -137,8 +140,9 @@
             pltpu.VMEM((ROWS, KEYS), F32),
             pltpu.VMEM((KEYS, HEAD), BF),
             pltpu.VMEM((KEYS, HEAD), BF),
+            pltpu.VMEM((ROWS, 16 * HEAD), F32),
         ],
-        compiler_params=params(),
+        compiler_params=params(62),
         name="attention",
     )(place, owner, fill, phase_owner, phase_fill, relay, q, kv, ph, fresh, fresh)
 
@@ -178,22 +182,23 @@
             at = pl.multiple_of(lax.rem(place[1] + d, NX) * ROWS, 16)
             rows[pl.ds(at, ROWS), :] = a[...]
 
-    for n in range(2):
-        out[n] = dot(rows[...], w[n]).astype(BF)
+    for n in range(0, NZ // 2, 2):
+        both = dot(rows[...], jnp.concatenate([w[n], w[n + 1]], axis=1)).astype(BF)
+        out[n], out[n + 1] = both[:, 0:HEAD], both[:, HEAD:]
 
 
 def project(place, pieces, w):
     whole = pl.BlockSpec((ROWS, 8 * HEAD), lambda k: (0, 0))
     return pl.pallas_call(
         project_kernel,
-        grid=(NZ // 2,),
+        grid=(2,),
         in_specs=[pl.BlockSpec(memory_space=pltpu.SMEM)]
         + [whole] * 4
-        + [pl.BlockSpec((2, 8 * HEAD, HEAD), lambda k: (k, 0, 0))],
-        out_specs=pl.BlockSpec((2, ALL, HEAD), lambda k: (k, 0, 0)),
+        + [pl.BlockSpec((NZ // 2, 8 * HEAD, HEAD), lambda k: (k, 0, 0))],
+        out_specs=pl.BlockSpec((NZ // 2, ALL, HEAD), lambda k: (k, 0, 0)),
         out_shape=jax.ShapeDtypeStruct((NZ, ALL, HEAD), BF),
         scratch_shapes=[pltpu.VMEM((ALL, 8 * HEAD), BF)],
-        compiler_params=params(),
+        compiler_params=params(62),
         name="project",
     )(place, *pieces, w)
 
@@ -321,72 +326,140 @@
     )(place, *hidden, *projected, send)
 
 
-def up_kernel(x, wg, wu, out, gate, up, square):
-    c = pl.program_id(1)
-    rows = x[...].reshape(NZ * ROWS, COLS)
-    part_gate = dot(rows, wg[0])
-    part_up = dot(rows, wu[0])
-    wide = rows.astype(F32)
-    part_square = jnp.sum(wide * wide, axis=-1, keepdims=True)
-
-    @pl.when(c == 0)
-    def _():
-        gate[...] = part_gate
-        up[...] = part_up
-        square[...] = part_square
-
-    @pl.when(c > 0)
-    def _():
-        gate[...] += part_gate
-        up[...] += part_up
-        square[...] += part_square
-
-    @pl.when(c == NC - 1)
-    def _():
-        scale = lax.rsqrt(square[...] * (1.0 / WIDTH) + EPS)
-        v = gate[...] * scale
-        out[0] = (v / (1.0 + jnp.exp(-v)) * (up[...] * scale)).astype(BF)
-
-
-def expert_up(x, wg, wu):
-    n = NZ * ROWS
-    return pl.pallas_call(
-        up_kernel,
-        grid=(2, NC),
-        in_specs=[
-            pl.BlockSpec((1, NZ, 1, ROWS, COLS), lambda e, c: (c, 0, e, 0, 0)),
-            pl.BlockSpec((1, COLS, FFS), lambda e, c: (e, c, 0)),
-            pl.BlockSpec((1, COLS, FFS), lambda e, c: (e, c, 0)),
-        ],
-        out_specs=pl.BlockSpec((1, n, FFS), lambda e, c: (e, 0, 0)),
-        out_shape=jax.ShapeDtypeStruct((2, n, FFS), BF),
-        scratch_shapes=[pltpu.VMEM((n, FFS), F32), pltpu.VMEM((n, FFS), F32), pltpu.VMEM((n, 1), F32)],
-        compiler_params=params(),
+AROUND = [(0, 0), (0, 1), (1, 0), (1, 1), (3, 0), (3, 1), (2, 0), (2, 1)]
+
+
+def up_kernel(around, first, last, place, *refs):
+    count = len(around)
+    xs, gates, ups = refs[:count], refs[count : 2 * count], refs[2 * count : 3 * count]
+    refs = refs[3 * count :]
+    if first:
+        both = jnp.zeros((2 * FFS, EXPERT_ROWS), F32)
+        square = jnp.zeros((EXPERT_ROWS, HEAD), F32)
+    else:
+        both, square = refs[0][0], refs[1][0]
+        refs = refs[2:]
+    for x, wg, wu in zip(xs, gates, ups):
+        rows = x[...].reshape(EXPERT_ROWS, COLS)
+        weights = jnp.concatenate([wg[0], wu[0]], axis=0)
+        both = both + dot(weights, rows, ((1,), (1,)))
+        for m in range(COLS // HEAD):
+            wide = rows[:, m * HEAD : (m + 1) * HEAD].astype(F32)
+            square = square + wide * wide
+    if last:
+        total = lax.dot_general(
+            jnp.ones((8, HEAD), F32),
+            square,
+            (((1,), (1,)), ((), ())),
+            precision=lax.Precision.HIGHEST,
+            preferred_element_type=F32,
+        )[0:1]
+        scale = lax.rsqrt(total * (1.0 / WIDTH) + EPS)
+        v = both[0:FFS] * scale
+        refs[0][...] = (v / (1.0 + jnp.exp(-v)) * (both[FFS:] * scale)).astype(BF)
+    else:
+        refs[0][0], refs[1][0] = both, square
+
+
+def column_of(dy, dc):
+    def index(e, place):
+        core = place[3]
+        return e, 0, lax.rem(place[2] + dy, NY) * NCORE + (1 - core if dc else core)
+
+    return index
+
+
+def expert_up(place, around, xs, wg, wu, sums=()):
+    last = len(sums) > 0
+    w_specs = [pl.BlockSpec((1, FFS, COLS), column_of(dy, dc)) for dy, dc in around]
+    shapes = [(2, 2 * FFS, EXPERT_ROWS), (2, EXPERT_ROWS, HEAD)]
+    sum_specs = [pl.BlockSpec((1,) + shape[1:], lambda e, p: (e, 0, 0)) for shape in shapes]
+    x_specs = []
+    for x in xs:
+        if x.shape[1] == 2:
+            x_specs.append(pl.BlockSpec((NZ, 1, ROWS, COLS), lambda e, p: (0, e, 0, 0)))
+        else:
+            x_specs.append(pl.BlockSpec((1, EXPERT_ROWS, COLS), lambda e, p: (e, 0, 0)))
+    if last:
+        out_specs = pl.BlockSpec((FFS, EXPERT_ROWS), lambda e, p: (e, 0))
+        out_shape = jax.ShapeDtypeStruct((2 * FFS, EXPERT_ROWS), BF)
+    else:
+        out_specs = sum_specs
+        out_shape = [jax.ShapeDtypeStruct(shape, F32) for shape in shapes]
+    n = len(xs)
+    return pl.pallas_call(
+        functools.partial(up_kernel, around, not last, last),
+        grid_spec=pltpu.PrefetchScalarGridSpec(
+            num_scalar_prefetch=1,
+            grid=(2,),
+            in_specs=x_specs + w_specs + w_specs + (sum_specs if last else []),
+            out_specs=out_specs,
+        ),
+        out_shape=out_shape,
+        compiler_params=params(50),
+        cost_estimate=pl.CostEstimate(
+            flops=n * 1000000000, bytes_accessed=n * 2000000, transcendentals=0
+        ),
         name="expert_up",
-    )(x, wg, wu)
-
-
-def down_kernel(h, w, out):
-    acc = dot(h[0, 0], w[0, 0])
-    for c in range(1, NC):
-        acc = acc + dot(h[c, 0], w[c, 0])
-    out[...] = acc.astype(BF).reshape(NZ, 1, ROWS, COLS)
-
-
-def expert_down(h, w):
-    n = NZ * ROWS
-    return pl.pallas_call(
-        down_kernel,
+    )(place, *xs, *[wg] * n, *[wu] * n, *sums)
+
+
+def split_kernel(place, w, *outs):
+    for out, (dy, dc) in zip(outs, AROUND):
+        core = place[3]
+        there = lax.rem(place[2] + NY - dy, NY) * NCORE + (1 - core if dc else core)
+        out[...] = w[:, :, pl.ds(pl.multiple_of(there * COLS, COLS), COLS)]
+
+
+def split_down(place, w):
+    return pl.pallas_call(
+        split_kernel,
         grid=(2,),
         in_specs=[
-            pl.BlockSpec((NC, 1, n, FFS), lambda e: (0, e, 0, 0)),
-            pl.BlockSpec((NC, 1, FFS, COLS), lambda e: (0, e, 0, 0)),
+            pl.BlockSpec(memory_space=pltpu.SMEM),
+            pl.BlockSpec((1, FFS, WIDTH), lambda e: (e, 0, 0)),
         ],
-        out_specs=pl.BlockSpec((NZ, 1, ROWS, COLS), lambda e: (0, e, 0, 0)),
-        out_shape=jax.ShapeDtypeStruct((NZ, 2, ROWS, COLS), BF),
-        compiler_params=params(),
+        out_specs=[pl.BlockSpec((1, FFS, COLS), lambda e: (e, 0, 0))] * NC,
+        out_shape=[jax.ShapeDtypeStruct((2, FFS, COLS), BF)] * NC,
+        compiler_params=params(62),
+        name="split_down",
+    )(place, w)
+
+
+def down_kernel(count, last, *refs):
+    hs, ws, refs = refs[:count], refs[count : 2 * count], refs[2 * count :]
+    total = dot(hs[0][...], ws[0][0], ((0,), (0,)))
+    for h, w in zip(hs[1:], ws[1:]):
+        total = total + dot(h[...], w[0], ((0,), (0,)))
+    if last:
+        total = total + refs[0][0]
+        refs[1][...] = total.astype(BF).reshape(NZ, 1, ROWS, COLS)
+    else:
+        refs[0][0] = total
+
+
+def expert_down(hs, ws, total=None):
+    n, last = len(hs), total is not None
+    sum_spec = pl.BlockSpec((1, EXPERT_ROWS, COLS), lambda e: (e, 0, 0))
+    if last:
+        out_spec = pl.BlockSpec((NZ, 1, ROWS, COLS), lambda e: (0, e, 0, 0))
+        out_shape = jax.ShapeDtypeStruct((NZ, 2, ROWS, COLS), BF)
+    else:
+        out_spec, out_shape = sum_spec, jax.ShapeDtypeStruct((2, EXPERT_ROWS, COLS), F32)
+    return pl.pallas_call(
+        functools.partial(down_kernel, n, last),
+        grid=(2,),
+        in_specs=[pl.BlockSpec((FFS, EXPERT_ROWS), lambda e: (e, 0))] * n
+        + [pl.BlockSpec((1, FFS, COLS), lambda e: (e, 0, 0))] * n
+        + ([sum_spec] if last else []),
+        out_specs=out_spec,
+        out_shape=out_shape,
+        compiler_params=params(62),
+        cost_estimate=pl.CostEstimate(
+            flops=n * 700000000, bytes_accessed=n * 1000000, transcendentals=0
+        ),
         name="expert_down",
-    )(h, w)
+    )(*hs, *ws, *([total] if last else []))
 
 
 def mix_kernel(place, back, mix_high, mix_low, o0, o1, o2, o3, rows):
@@ -414,8 +487,29 @@
     return lax.ppermute(value, "x", [((i + d) % NX, i) for i in range(NX)])
 
 
+def in_rows(value):
+    return value.transpose(0, 2, 1, 3).reshape(ROWS, value.shape[3])
+
+
 def along_x(value):
     return [value] + [from_x(value, d) for d in range(1, NX)]
+
+
+def from_y(value, d):
+    return lax.ppermute(value, "y", [((i + d) % NY, i) for i in range(NY)])
+
+
+def other_core(value):
+    return lax.ppermute(value, "core", [(0, 1), (1, 0)])
+
+
+def from_ctx(value, dy, dc):
+    pairs = []
+    for y in range(NY):
+        for core in range(NCORE):
+            source = (y + dy) % NY * NCORE + (core ^ dc)
+            pairs.append((source, y * NCORE + core))
+    return lax.ppermute(value, CTX, pairs)
 
 
 def body(
@@ -439,23 +533,11 @@
 ):
     del relay_slot
     ctx = lax.axis_index(CTX)
-    place = jnp.stack([ctx, lax.axis_index("x")]).astype(jnp.int32)
+    place = [ctx, lax.axis_index("x"), lax.axis_index("y"), lax.axis_index("core")]
+    place = jnp.stack(place).astype(jnp.int32)
 
     with jax.named_scope("gather_projection"):
         o_cols = lax.all_gather(o_proj, "z")
-    with jax.named_scope("gather_tables"):
-        table = jnp.stack(
-            [expert_ids.reshape(ROWS, TOPK).astype(F32), gate_weights.reshape(ROWS, TOPK)]
-        )
-        tables = along_x(table)
-    with jax.named_scope("gather_hidden"):
-        hidden_cols = lax.dynamic_slice_in_dim(hidden_in, ctx * COLS, COLS, 3).reshape(ROWS, COLS)
-        hidden = along_x(hidden_cols)
-    with jax.named_scope("turn_down"):
-        down_cols = lax.all_to_all(
-            w_down.reshape(2, FFS, NC, COLS).transpose(2, 0, 1, 3), CTX, 0, 0, tiled=True
-        )
-
     with jax.named_scope("attend"):
         parts = attention(
             place,
@@ -464,32 +546,65 @@
             phase_owner,
             phase_fill,
             relay_page[0],
-            queries.reshape(ROWS, HEADS * HEAD),
+            queries.transpose(0, 2, 1, 3),
             kv_cache[0],
             phased[0],
             new_kv.reshape(ROWS, 2 * KV_HEADS * HEAD),
         )
+    with jax.named_scope("gather_tables"):
+        parts, expert_ids, gate_weights, hidden_in, w_down = lax.optimization_barrier(
+            (parts, expert_ids, gate_weights, hidden_in, w_down)
+        )
+        hidden = along_x(in_rows(lax.dynamic_slice_in_dim(hidden_in, ctx * COLS, COLS, 3)))
+        tables = along_x(jnp.stack([in_rows(expert_ids).astype(F32), in_rows(gate_weights)]))
+        down_parts = split_down(place, w_down)
     with jax.named_scope("join_parts"):
         parts = lax.all_to_all(parts, CTX, 0, 0, tiled=True)
+        parts, tables, hidden, down_parts = lax.optimization_barrier(
+            (parts, tables, hidden, down_parts)
+        )
         attended = join(parts)
+    with jax.named_scope("turn_down"):
+        down_cols = list(down_parts)
+        for n in (6, 7):
+            down_cols[n] = from_ctx(down_parts[n], *AROUND[n])
     with jax.named_scope("project_rows"):
         partial = project(place, along_x(attended), o_cols)
     with jax.named_scope("sum_projection"):
-        columns = add_up(lax.all_to_all(partial, CTX, 0, 0, tiled=True))
-        projected = along_x(columns)
+        columns = lax.all_to_all(partial, CTX, 0, 0, tiled=True)
+        columns, down_cols = lax.optimization_barrier((columns, down_cols))
+        projected = along_x(add_up(columns))
+    with jax.named_scope("turn_down"):
+        for n in range(1, 6):
+            down_cols[n] = from_ctx(down_cols[n], *AROUND[n])
     with jax.named_scope("find_routes"):
         send, mix_high, mix_low = routes(place, tables)
     with jax.named_scope("dispatch_rows"):
         packed, mine = dispatch(place, hidden, projected, send)
         arrived = lax.all_to_all(packed.reshape(NZ, 96, COLS), "z", 0, 0, tiled=True)
+        arrived = arrived.reshape(NZ, 2, ROWS, COLS)
+        arrived, down_cols = lax.optimization_barrier((arrived, down_cols))
     with jax.named_scope("gather_rows"):
-        rows = lax.all_gather(arrived, CTX).reshape(NC, NZ, 2, ROWS, COLS)
+        after, before = from_y(arrived, 1), from_y(arrived, 3)
+        far = [from_y(after[:, 0], 1), from_y(before[:, 1], 3)]
+        near = []
+        for value in (arrived, after, before):
+            near += [value, other_core(value)]
     with jax.named_scope("up"):
-        units = expert_up(rows, w_gate, w_up)
+        gate_t, up_t = w_gate.transpose(0, 2, 1), w_up.transpose(0, 2, 1)
+        sums = expert_up(place, AROUND[:6], near, gate_t, up_t)
+        sums, far = lax.optimization_barrier((sums, far))
+        far = jnp.stack(far).reshape(2, EXPERT_ROWS, COLS)
+        units = expert_up(place, AROUND[6:], [far, other_core(far)], gate_t, up_t, sums)
     with jax.named_scope("gather_units"):
-        units = lax.all_gather(units, CTX)
+        after, before, far = from_y(units, 1), from_y(units, 3), from_y(units, 2)
+        near = []
+        for value in (units, after, before):
+            near += [value, other_core(value)]
     with jax.named_scope("down"):
-        outcome = expert_down(units, down_cols)
+        total = expert_down(near, down_cols[:6])
+        total, far = lax.optimization_barrier((total, far))
+        outcome = expert_down([far, other_core(far)], down_cols[6:], total)
     with jax.named_scope("return_rows"):
         back = lax.all_to_all(outcome.reshape(NZ, 96, COLS), "z", 0, 0, tiled=True)
     with jax.named_scope("mix"):
@@ -497,7 +612,7 @@
         total = mine + mixed[0]
         for d in range(1, NX):
             total = total + from_x(mixed[d], NX - d).astype(F32)
-    return total.astype(BF).reshape(2, 4, 6, COLS)
+    return total.astype(BF).reshape(2, 6, 4, COLS).transpose(0, 2, 1, 3)
 
 
 def solution(mesh):

time: 271 us -> 228 us (0.84)
  blocking collectives: 71 us -> 30.3 us
  local copies, waits for them, and re-layouts: 34.8 us -> 6.81 us
  starting transfers between devices: 34.5 us -> 60.8 us
  waiting for transfers between devices: 81.4 us -> 71.5 us
  Pallas kernels: 33.5 us -> 40.6 us
    all_gather x2 -> x0, waiting for transfers between devices: 55.1 us -> none  [the longest x1 28.9 us: body(): units = lax.all_gather(units, CTX)]
    ppermute x0 -> x22, waiting for transfers between devices: none -> 52.2 us  [the longest x7 29.1 us: from_y(): return lax.ppermute(value, 'y', [((i + d) % NY, i) for i in range(NY)])]
    all_to_all x2 -> x0, blocking collectives: 41.2 us -> none  [the longest x1 24.5 us: body(): lax.all_to_all(packed.reshape(NZ, 96, COLS), 'z', 0, 0, tiled=True)]
    ppermute x0 -> x22, starting transfers between devices: none -> 20.2 us  [the longest x7 12.7 us: from_y(): return lax.ppermute(value, 'y', [((i + d) % NY, i) for i in range(NY)])]
    unnamed x49 -> x47, local copies, waits for them, and re-layouts: 22.9 us -> 6.08 us
    all_to_all x2 -> x3, starting transfers between devices: 11 us -> 19.4 us  [the longest x1 8.99 us: body(): lax.all_to_all(packed.reshape(NZ, 96, COLS), 'z', 0, 0, tiled=True)]
    all_to_all x2 -> x3, waiting for transfers between devices: 12.4 us -> 5.06 us  [the longest x1 5.05 us: body(): columns = lax.all_to_all(partial, CTX, 0, 0, tiled=True)]
    reshape x6 -> x2, local copies, waits for them, and re-layouts: 6.15 us -> 0.66 us  [the longest x1 0.64 us: body(): return total.astype(BF).reshape(2, 6, 4, COLS).transpose(0, 2, 1, 3)]
  transfers between devices with their start and end apart: 20 -> 41, of which waited for: 12 -> 19; matrix products, arithmetic and copies ran while one was open for 9% -> 1% of each run, Pallas kernels for 5% -> 14%
where the time goes in v2:
time: 228 us; the launch traced here: 224 us
  waiting for transfers between devices  71.5 us (31%)
  starting transfers between devices  60.8 us (27%)
  Pallas kernels  40.6 us (18%)
  blocking collectives  30.3 us (13%)
  between operations  13.7 us (6%)
  local copies, waits for them, and re-layouts  6.81 us (3%)
    all_to_all x1, blocking collectives, body(): back = lax.all_to_all(outcome.reshape(NZ, 96, COLS), 'z', 0, 0, tiled=True)  30.3 us
    ppermute x7, waiting for transfers between devices, from_y(): return lax.ppermute(value, 'y', [((i + d) % NY, i) for i in range(NY)])  29.1 us
    ppermute x15, starting transfers between devices, from_x(): return lax.ppermute(value, 'x', [((i + d) % NX, i) for i in range(NX)])  21.2 us
    ppermute x7, waiting for transfers between devices, from_ctx(): return lax.ppermute(value, CTX, pairs)  19.1 us
    ppermute x7, starting transfers between devices, from_y(): return lax.ppermute(value, 'y', [((i + d) % NY, i) for i in range(NY)])  12.7 us
    pallas_call x1, Pallas kernels, attention(): pl.pallas_call(attention_kernel, grid=(KV_HEADS,), in_specs=[smem] * 6 +...  11.4 us
    ppermute x15, waiting for transfers between devices, from_x(): return lax.ppermute(value, 'x', [((i + d) % NX, i) for i in range(NX)])  10.7 us
    pallas_call x2, Pallas kernels, expert_up(): pl.pallas_call(functools.partial(up_kernel, around, not last, last), grid...  10.1 us
  transfers between devices with their start and end apart: 41, of which 19 were waited for; matrix products, arithmetic and copies ran while one was open for 1% of the time, Pallas kernels for 14%

profile of v2, /device:TPU:24, one launch (start us, length us, event | category | flops | bytes accessed | tf_op | source)
XLA Modules:
  0.0 224.4 jit_solution(17683716342169024188)
XLA Ops:
  9.5 11.4 %attention.1 = bf16[8,48,1152]{2,1,0:T(8,128)(2,1)} custom-call(s32[4]{0:T(128)} %pad_add_fusion.place, s32[1,24]{1,0:T(1,128)} %owner.1, s32[1,24]{1,0:T(1,128)} %fill.1, s32[1,64]{1,0:T(1,128)} %phase_owner.1, s32[1,64]{1,0:T(1,128)} %phase_fill.1, s32[8,8]{1,0:T(8,128)} %bitcast.66, bf16[2,6,4,8192]{3,2,1,0:T(4,128)(2,1)} %bitcast.59, ...), custom_call_target="tpu_custom_call" | custom-call | tf_op jit(solution)/shard_map/attend/attention/pallas_call | solution.py:126
  20.9 5.4 %all-to-all-start = ((bf16[8,48,1152]{2,1,0:T(8,128)(2,1)}), bf16[8,48,1152]{2,1,0:T(8,128)(2,1)S(1)}, u32[]{:S(2)}, u32[]{:S(2)}) async-start(bf16[8,48,1152]{2,1,0:T(8,128)(2,1)} %attention.1), calls=%async_computation | async-start | bytes 1769472 | tf_op jit(solution)/shard_map/join_parts/all_to_all | solution.py:562
  26.4 2.1 collective-permute-start.3
  30.2 2.4 %collective-permute-start = (f32[2,48,8]{2,1,0:T(8,128)S(1)}, f32[2,48,8]{2,1,0:T(8,128)S(1)}, u32[]{:S(2)}, u32[]{:S(2)}) collective-permute-start(f32[2,48,8]{2,1,0:T(8,128)S(1)} %pad_maximum_fusion.1.t0), channel_id=1, source_target_pairs={{1,0},{2,1},{3,2},{0,3},{5,4},{6,5},{7,6},{4,7},{9,8},{10,9},{11,1... | collective-permute-start | bytes 9224 | tf_op jit(solution)/shard_map/gather_tables/ppermute | solution.py:487
  36.6 3.2 %split_down.1 = (bf16[2,192,512]{2,1,0:T(8,128)(2,1)}, bf16[2,192,512]{2,1,0:T(8,128)(2,1)}, bf16[2,192,512]{2,1,0:T(8,128)(2,1)}, bf16[2,192,512]{2,1,0:T(8,128...) custom-call(s32[4]{0:T(128)} %pad_add_fusion.place, ...), custom_call_target="tpu_custom_call" | custom-call | tf_op jit(solution)/shard_map/gather_tables/split_down/pallas_call | solution.py:415
  41.0 2.0 collective-permute-start.6
  46.5 2.6 %collective-permute-done.7.a2 = bf16[48,1024]{1,0:T(8,128)(2,1)S(1)} collective-permute-done((bf16[48,1024]{1,0:T(8,128)(2,1)S(1)}, bf16[48,1024]{1,0:T(8,128)(2,1)S(1)}, u32[]{:S(2)}, u32[]{:S(2)}) %collective-permute-start.7) | collective-permute-done | bytes 98336 | tf_op jit(solution)/shard_map/project_rows/ppermute | solution.py:487
  50.1 2.9 %all-gather.3.cloned.1.call-done = bf16[8192,128]{1,0:T(8,128)(2,1)} async-done(((bf16[1024,128]{1,0:T(8,128)(2,1)}), bf16[8192,128]{1,0:T(8,128)(2,1)}) %all-gather.3.cloned.1.call-update) | async-done | bytes 2097168 | tf_op jit(solution)/shard_map/gather_projection/all_gather | solution.py:540
  53.0 2.8 %project.1 = bf16[8,192,128]{2,1,0:T(8,128)(2,1)} custom-call(s32[4]{0:T(128)} %pad_add_fusion.place, bf16[48,1024]{1,0:T(8,128)(2,1)} %copy-done.2, bf16[48,1024]{1,0:T(8,128)(2,1)} %copy-done.7, bf16[48,1024]{1,0:T(8,128)(2,1)} %copy-done.8, bf16[48,1024]{1,0:T(8,128)(2,1)} %copy-done.9, bf16[8,1024,128]{2,1,0:T(8,128)(2,1)} %bitcast.54), custom_call_target="tpu_custom_call" | custom-call | tf_op jit(solution)/shard_map/project_rows/project/pallas_call | solution.py:192
  55.9 4.9 %all-to-all-start.1 = ((bf16[8,192,128]{2,1,0:T(8,128)(2,1)}), bf16[8,192,128]{2,1,0:T(8,128)(2,1)S(1)}, u32[]{:S(2)}, u32[]{:S(2)}) async-start(bf16[8,192,128]{2,1,0:T(8,128)(2,1)} %project.1), calls=%async_computation.1 | async-start | bytes 786432 | tf_op jit(solution)/shard_map/sum_projection/all_to_all | solution.py:574
  60.8 2.9 %collective-permute-done.9.refs_2_ = bf16[2,192,512]{2,1,0:T(8,128)(2,1)} collective-permute-done((bf16[2,192,512]{2,1,0:T(8,128)(2,1)}, bf16[2,192,512]{2,1,0:T(8,128)(2,1)}, u32[]{:S(2)}, u32[]{:S(2)}) %collective-permute-start.9) | collective-permute-done | bytes 393248 | tf_op jit(solution)/shard_map/turn_down/ppermute | solution.py:512
  63.7 5.1 %all-to-all-done.1.parts = bf16[8,192,128]{2,1,0:T(8,128)(2,1)S(1)} async-done(((bf16[8,192,128]{2,1,0:T(8,128)(2,1)}), bf16[8,192,128]{2,1,0:T(8,128)(2,1)S(1)}, u32[]{:S(2)}, u32[]{:S(2)}) %all-to-all-start.1) | async-done | bytes 393248 | tf_op jit(solution)/shard_map/sum_projection/all_to_all | solution.py:574
  68.8 2.3 %collective-permute-start.11 = (bf16[192,128]{1,0:T(8,128)(2,1)S(1)}, bf16[192,128]{1,0:T(8,128)(2,1)S(1)}, u32[]{:S(2)}, u32[]{:S(2)}) collective-permute-start(bf16[192,128]{1,0:T(8,128)(2,1)S(1)} %add_up.1.p0), channel_id=1, source_target_pairs={{1,0},{2,1},{3,2},{0,3},{5,4},{6,5},{7,6},{4,7},{9,8},{10,9},{11,1... | collective-permute-start | bytes 147464 | tf_op jit(solution)/shard_map/sum_projection/ppermute | solution.py:487
  74.6 2.2 collective-permute-done.12.p2
  79.6 9.0 %all-to-all-start.2 = ((bf16[8,96,512]{2,1,0:T(8,128)(2,1)}), bf16[8,96,512]{2,1,0:T(8,128)(2,1)S(1)}, u32[]{:S(2)}, u32[]{:S(2)}) async-start(bf16[8,96,512]{2,1,0:T(8,128)(2,1)} %bitcast.14), calls=%async_computation.2 | async-start | bytes 1572864 | tf_op jit(solution)/shard_map/dispatch_rows/all_to_all | solution.py:584
  93.4 8.6 %collective-permute-done.15.refs_8_ = bf16[2,192,512]{2,1,0:T(8,128)(2,1)S(1)} collective-permute-done((bf16[2,192,512]{2,1,0:T(8,128)(2,1)}, bf16[2,192,512]{2,1,0:T(8,128)(2,1)S(1)}, u32[]{:S(2)}, u32[]{:S(2)}) %collective-permute-start.15) | collective-permute-done | bytes 393248 | tf_op jit(solution)/shard_map/turn_down/ppermute | solution.py:512
  102.1 7.5 %collective-permute-done.16.refs_9_ = bf16[2,192,512]{2,1,0:T(8,128)(2,1)S(1)} collective-permute-done((bf16[2,192,512]{2,1,0:T(8,128)(2,1)}, bf16[2,192,512]{2,1,0:T(8,128)(2,1)S(1)}, u32[]{:S(2)}, u32[]{:S(2)}) %collective-permute-start.16) | collective-permute-done | bytes 393248 | tf_op jit(solution)/shard_map/turn_down/ppermute | solution.py:512
  111.6 2.7 %collective-permute-start.22 = (bf16[8,2,48,512]{3,2,1,0:T(8,128)(2,1)S(1)}, bf16[8,2,48,512]{3,2,1,0:T(8,128)(2,1)S(1)}, u32[]{:S(2)}, u32[]{:S(2)}) collective-permute-start(bf16[8,2,48,512]{3,2,1,0:T(8,128)(2,1)S(1)} %bitcast.35), channel_id=1, source_target_pairs={{192,0},{0,64},{64,128},{128,192},{193,1},{1,65},{65,129},{129,193... | collective-permute-start | bytes 2359304 | tf_op jit(solution)/shard_map/gather_rows/ppermute | solution.py:499
  114.3 18.0 %collective-permute-done.20.refs_2_ = bf16[8,2,48,512]{3,2,1,0:T(8,128)(2,1)S(1)} collective-permute-done((bf16[8,2,48,512]{3,2,1,0:T(8,128)(2,1)S(1)}, bf16[8,2,48,512]{3,2,1,0:T(8,128)(2,1)S(1)}, u32[]{:S(2)}, u32[]{:S(2)}) %collective-permute-start.20) | collective-permute-done | bytes 786464 | tf_op jit(solution)/shard_map/gather_rows/ppermute | solution.py:499
  133.1 3.5 %collective-permute-start.25 = (bf16[8,48,512]{2,1,0:T(8,128)(2,1)S(1)}, bf16[8,48,512]{2,1,0:T(8,128)(2,1)S(1)}, u32[]{:S(2)}, u32[]{:S(2)}) collective-permute-start(bf16[8,48,512]{2,1,0:T(8,128)(2,1)S(1)} %slice_bitcast_fusion), channel_id=1, source_target_pairs={{192,0},{0,64},{64,128},{128,192},{193,1},{1,65},{65,129},{129,193... | collective-permute-start | bytes 1179656 | tf_op jit(solution)/shard_map/gather_rows/ppermute | solution.py:499
  137.5 6.4 %expert_up.2 = (f32[2,384,384]{2,1,0:T(8,128)}, f32[2,384,128]{2,1,0:T(8,128)S(1)}) custom-call(s32[4]{0:T(128)S(1)} %copy-done.4, bf16[8,2,48,512]{3,2,1,0:T(8,128)(2,1)S(1)} %bitcast.37, bf16[8,2,48,512]{3,2,1,0:T(8,128)(2,1)S(1)} %collective-permute-done.19.refs_1_, bf16[8,2,48,512]{3,2,1,0:T(8,128)(2,1)S(1)} %collective-permute-done.20.refs_2_, ...), custom_call_target="tpu_custom_call" | custom-call | flops 6000000000 | bytes 12000000 | tf_op jit(solution)/shard_map/up/expert_up/pallas_call | solution.py:390
  145.4 2.3 %collective-permute-done.26.refs_1_ = bf16[2,384,512]{2,1,0:T(8,128)(2,1)S(1)} collective-permute-done((bf16[2,384,512]{2,1,0:T(8,128)(2,1)S(1)}, bf16[2,384,512]{2,1,0:T(8,128)(2,1)S(1)}, u32[]{:S(2)}, u32[]{:S(2)}) %collective-permute-start.26) | collective-permute-done | bytes 786464 | tf_op jit(solution)/shard_map/up/ppermute | solution.py:503
  147.7 3.6 %expert_up.3.refs_0_ = bf16[384,384]{1,0:T(8,128)(2,1)S(1)} custom-call(s32[4]{0:T(128)S(1)} %copy-done.4, bf16[2,384,512]{2,1,0:T(8,128)(2,1)S(1)} %pad_maximum_fusion.refs_0_, bf16[2,384,512]{2,1,0:T(8,128)(2,1)S(1)} %collective-permute-done.26.refs_1_, bf16[2,192,4096]{2,1,0:T(8,128)(2,1)} %bitcast.44, bf16[2,192,4096]{2,1,0:T(8,128)(2,1)} %bitcast.45, ...), custom_call_target="tpu_custom_call" | custom-call | flops 2000000000 | bytes 4000000 | tf_op jit(solution)/shard_map/up/expert_up/pallas_call | solution.py:390
  152.8 2.0 collective-permute-start.30
  154.8 7.2 %collective-permute-done.28.refs_2_ = bf16[384,384]{1,0:T(8,128)(2,1)S(1)} collective-permute-done((bf16[384,384]{1,0:T(8,128)(2,1)S(1)}, bf16[384,384]{1,0:T(8,128)(2,1)S(1)}, u32[]{:S(2)}, u32[]{:S(2)}) %collective-permute-start.28) | collective-permute-done | bytes 294944 | tf_op jit(solution)/shard_map/gather_units/ppermute | solution.py:499
  162.6 2.4 %collective-permute-start.32 = (bf16[384,384]{1,0:T(8,128)(2,1)S(1)}, bf16[384,384]{1,0:T(8,128)(2,1)}, u32[]{:S(2)}, u32[]{:S(2)}) collective-permute-start(bf16[384,384]{1,0:T(8,128)(2,1)S(1)} %expert_up.3.refs_0_), channel_id=1, source_target_pairs={{128,0},{192,64},{0,128},{64,192},{129,1},{193,65},{1,129},{65,193... | collective-permute-start | bytes 884744 | tf_op jit(solution)/shard_map/gather_units/ppermute | solution.py:499
  166.4 4.3 %expert_down.2.refs_4_ = f32[2,384,512]{2,1,0:T(8,128)} custom-call(bf16[384,384]{1,0:T(8,128)(2,1)} %copy-done.3, bf16[384,384]{1,0:T(8,128)(2,1)} %copy-done.20, bf16[384,384]{1,0:T(8,128)(2,1)} %copy-done.18, bf16[384,384]{1,0:T(8,128)(2,1)} %copy-done.21, bf16[384,384]{1,0:T(8,128)(2,1)} %copy-done.19, bf16[384,384]{1,0:T(8,128)(2,1)} %collective-permute-done.31.refs_5_, ...), custom_call_target="tpu_custom_call" | custom-call | flops 4200000000 | bytes 6000000 | tf_op jit(solution)/shard_map/down/expert_down/pallas_call | solution.py:449
  170.7 2.5 %collective-permute-done.32.refs_0_ = bf16[384,384]{1,0:T(8,128)(2,1)} collective-permute-done((bf16[384,384]{1,0:T(8,128)(2,1)S(1)}, bf16[384,384]{1,0:T(8,128)(2,1)}, u32[]{:S(2)}, u32[]{:S(2)}) %collective-permute-start.32) | collective-permute-done | bytes 294944 | tf_op jit(solution)/shard_map/gather_units/ppermute | solution.py:499
  175.7 3.1 %expert_down.3 = bf16[8,2,48,512]{3,2,1,0:T(8,128)(2,1)} custom-call(bf16[384,384]{1,0:T(8,128)(2,1)} %collective-permute-done.32.refs_0_, bf16[384,384]{1,0:T(8,128)(2,1)} %copy-done.22, bf16[2,192,512]{2,1,0:T(8,128)(2,1)} %collective-permute-done.9.refs_2_, bf16[2,192,512]{2,1,0:T(8,128)(2,1)} %copy-done.12, f32[2,384,512]{2,1,0:T(8,128)} %expert_down.2.refs_4_), custom_call_target="tpu_custom_call" | custom-call | flops 1400000000 | bytes 2000000 | tf_op jit(solution)/shard_map/down/expert_down/pallas_call | solution.py:449
  178.8 30.3 %all_to_all.20 = bf16[8,96,512]{2,1,0:T(8,128)(2,1)S(1)} all-to-all(bf16[8,96,512]{2,1,0:T(8,128)(2,1)} %bitcast.58), channel_id=1, replica_groups=mesh['y'=4,'core'=2,'z'=8,'x'=4] {'z'}, dimensions={0} | all-to-all | bytes 1572864 | tf_op jit(solution)/shard_map/return_rows/all_to_all | solution.py:609
  211.7 2.2 collective-permute-start.36
  213.9 2.2 collective-permute-done.34
  (121 shorter events, 40.7 us)
Async XLA Ops:
  6.5 46.5 %all-gather.3.cloned.1.call-start = ((), (), s32[]{:S(2)}) async-start(), calls=%async_computation.4 | async-start | bytes 2359296 | tf_op jit(solution)/shard_map/gather_projection/all_gather | solution.py:540
  20.9 19.2 %all-to-all-start = ((bf16[8,48,1152]{2,1,0:T(8,128)(2,1)}), bf16[8,48,1152]{2,1,0:T(8,128)(2,1)S(1)}, u32[]{:S(2)}, u32[]{:S(2)}) async-start(bf16[8,48,1152]{2,1,0:T(8,128)(2,1)} %attention.1), calls=%async_computation | async-start | bytes 1769472 | tf_op jit(solution)/shard_map/join_parts/all_to_all | solution.py:562
  26.4 13.7 %collective-permute-start.3 = (bf16[48,512]{1,0:T(8,128)(2,1)S(1)}, bf16[48,512]{1,0:T(8,128)(2,1)S(1)}, u32[]{:S(2)}, u32[]{:S(2)}) collective-permute-start(bf16[48,512]{1,0:T(8,128)(2,1)S(1)} %reshape.43.h0), channel_id=1, source_target_pairs={{1,0},{2,1},{3,2},{0,3},{5,4},{6,5},{7,6},{4,7},{9,8},{10,9},{11,1... | collective-permute-start | bytes 147464 | tf_op jit(solution)/shard_map/gather_tables/ppermute | solution.py:487
  28.5 11.6 %collective-permute-start.4 = (bf16[48,512]{1,0:T(8,128)(2,1)S(1)}, bf16[48,512]{1,0:T(8,128)(2,1)S(1)}, u32[]{:S(2)}, u32[]{:S(2)}) collective-permute-start(bf16[48,512]{1,0:T(8,128)(2,1)S(1)} %reshape.43.h0), channel_id=1, source_target_pairs={{2,0},{3,1},{0,2},{1,3},{6,4},{7,5},{4,6},{5,7},{10,8},{11,9},{8,1... | collective-permute-start | bytes 147464 | tf_op jit(solution)/shard_map/gather_tables/ppermute | solution.py:487
  29.3 10.9 %collective-permute-start.5 = (bf16[48,512]{1,0:T(8,128)(2,1)S(1)}, bf16[48,512]{1,0:T(8,128)(2,1)S(1)}, u32[]{:S(2)}, u32[]{:S(2)}) collective-permute-start(bf16[48,512]{1,0:T(8,128)(2,1)S(1)} %reshape.43.h0), channel_id=1, source_target_pairs={{3,0},{0,1},{1,2},{2,3},{7,4},{4,5},{5,6},{6,7},{11,8},{8,9},{9,10... | collective-permute-start | bytes 147464 | tf_op jit(solution)/shard_map/gather_tables/ppermute | solution.py:487
  32.6 7.2 %collective-permute-start.1 = (f32[2,48,8]{2,1,0:T(8,128)S(1)}, f32[2,48,8]{2,1,0:T(8,128)S(1)}, u32[]{:S(2)}, u32[]{:S(2)}) collective-permute-start(f32[2,48,8]{2,1,0:T(8,128)S(1)} %pad_maximum_fusion.1.t0), channel_id=1, source_target_pairs={{2,0},{3,1},{0,2},{1,3},{6,4},{7,5},{4,6},{5,7},{10,8},{11,9},{8,1... | collective-permute-start | bytes 9224 | tf_op jit(solution)/shard_map/gather_tables/ppermute | solution.py:487
  34.8 5.3 %collective-permute-start.2 = (f32[2,48,8]{2,1,0:T(8,128)S(1)}, f32[2,48,8]{2,1,0:T(8,128)S(1)}, u32[]{:S(2)}, u32[]{:S(2)}) collective-permute-start(f32[2,48,8]{2,1,0:T(8,128)S(1)} %pad_maximum_fusion.1.t0), channel_id=1, source_target_pairs={{3,0},{0,1},{1,2},{2,3},{7,4},{4,5},{5,6},{6,7},{11,8},{8,9},{9,10... | collective-permute-start | bytes 9224 | tf_op jit(solution)/shard_map/gather_tables/ppermute | solution.py:487
  41.0 5.5 %collective-permute-start.6 = (bf16[48,1024]{1,0:T(8,128)(2,1)S(1)}, bf16[48,1024]{1,0:T(8,128)(2,1)S(1)}, u32[]{:S(2)}, u32[]{:S(2)}) collective-permute-start(bf16[48,1024]{1,0:T(8,128)(2,1)S(1)} %join.1.a0), channel_id=1, source_target_pairs={{1,0},{2,1},{3,2},{0,3},{5,4},{6,5},{7,6},{4,7},{9,8},{10,9},{11,1... | collective-permute-start | bytes 294920 | tf_op jit(solution)/shard_map/project_rows/ppermute | solution.py:487
  43.0 6.2 %collective-permute-start.7 = (bf16[48,1024]{1,0:T(8,128)(2,1)S(1)}, bf16[48,1024]{1,0:T(8,128)(2,1)S(1)}, u32[]{:S(2)}, u32[]{:S(2)}) collective-permute-start(bf16[48,1024]{1,0:T(8,128)(2,1)S(1)} %join.1.a0), channel_id=1, source_target_pairs={{2,0},{3,1},{0,2},{1,3},{6,4},{7,5},{4,6},{5,7},{10,8},{11,9},{8,1... | collective-permute-start | bytes 294920 | tf_op jit(solution)/shard_map/project_rows/ppermute | solution.py:487
  43.7 6.4 %collective-permute-start.8 = (bf16[48,1024]{1,0:T(8,128)(2,1)S(1)}, bf16[48,1024]{1,0:T(8,128)(2,1)S(1)}, u32[]{:S(2)}, u32[]{:S(2)}) collective-permute-start(bf16[48,1024]{1,0:T(8,128)(2,1)S(1)} %join.1.a0), channel_id=1, source_target_pairs={{3,0},{0,1},{1,2},{2,3},{7,4},{4,5},{5,6},{6,7},{11,8},{8,9},{9,10... | collective-permute-start | bytes 294920 | tf_op jit(solution)/shard_map/project_rows/ppermute | solution.py:487
  45.0 15.7 %collective-permute-start.10 = (bf16[2,192,512]{2,1,0:T(8,128)(2,1)}, bf16[2,192,512]{2,1,0:T(8,128)(2,1)S(1)}, u32[]{:S(2)}, u32[]{:S(2)}) collective-permute-start(bf16[2,192,512]{2,1,0:T(8,128)(2,1)} %get-tuple-element.95), channel_id=1, source_target_pairs={{160,0},{128,32},{224,64},{192,96},{32,128},{0,160},{96,192},{64,2... | collective-permute-start | bytes 1179656 | tf_op jit(solution)/shard_map/turn_down/ppermute | solution.py:512
  45.0 18.7 %collective-permute-start.9 = (bf16[2,192,512]{2,1,0:T(8,128)(2,1)}, bf16[2,192,512]{2,1,0:T(8,128)(2,1)}, u32[]{:S(2)}, u32[]{:S(2)}) collective-permute-start(bf16[2,192,512]{2,1,0:T(8,128)(2,1)} %get-tuple-element.94), channel_id=1, source_target_pairs={{128,0},{160,32},{192,64},{224,96},{0,128},{32,160},{64,192},{96,2... | collective-permute-start | bytes 1179656 | tf_op jit(solution)/shard_map/turn_down/ppermute | solution.py:512
  55.9 12.9 %all-to-all-start.1 = ((bf16[8,192,128]{2,1,0:T(8,128)(2,1)}), bf16[8,192,128]{2,1,0:T(8,128)(2,1)S(1)}, u32[]{:S(2)}, u32[]{:S(2)}) async-start(bf16[8,192,128]{2,1,0:T(8,128)(2,1)} %project.1), calls=%async_computation.1 | async-start | bytes 786432 | tf_op jit(solution)/shard_map/sum_projection/all_to_all | solution.py:574
  68.8 5.8 %collective-permute-start.11 = (bf16[192,128]{1,0:T(8,128)(2,1)S(1)}, bf16[192,128]{1,0:T(8,128)(2,1)S(1)}, u32[]{:S(2)}, u32[]{:S(2)}) collective-permute-start(bf16[192,128]{1,0:T(8,128)(2,1)S(1)} %add_up.1.p0), channel_id=1, source_target_pairs={{1,0},{2,1},{3,2},{0,3},{5,4},{6,5},{7,6},{4,7},{9,8},{10,9},{11,1... | collective-permute-start | bytes 147464 | tf_op jit(solution)/shard_map/sum_projection/ppermute | solution.py:487
  71.1 5.7 %collective-permute-start.12 = (bf16[192,128]{1,0:T(8,128)(2,1)S(1)}, bf16[192,128]{1,0:T(8,128)(2,1)S(1)}, u32[]{:S(2)}, u32[]{:S(2)}) collective-permute-start(bf16[192,128]{1,0:T(8,128)(2,1)S(1)} %add_up.1.p0), channel_id=1, source_target_pairs={{2,0},{3,1},{0,2},{1,3},{6,4},{7,5},{4,6},{5,7},{10,8},{11,9},{8,1... | collective-permute-start | bytes 147464 | tf_op jit(solution)/shard_map/sum_projection/ppermute | solution.py:487
  72.4 5.3 %collective-permute-start.13 = (bf16[192,128]{1,0:T(8,128)(2,1)S(1)}, bf16[192,128]{1,0:T(8,128)(2,1)S(1)}, u32[]{:S(2)}, u32[]{:S(2)}) collective-permute-start(bf16[192,128]{1,0:T(8,128)(2,1)S(1)} %add_up.1.p0), channel_id=1, source_target_pairs={{3,0},{0,1},{1,2},{2,3},{7,4},{4,5},{5,6},{6,7},{11,8},{8,9},{9,10... | collective-permute-start | bytes 147464 | tf_op jit(solution)/shard_map/sum_projection/ppermute | solution.py:487
  79.6 31.4 %all-to-all-start.2 = ((bf16[8,96,512]{2,1,0:T(8,128)(2,1)}), bf16[8,96,512]{2,1,0:T(8,128)(2,1)S(1)}, u32[]{:S(2)}, u32[]{:S(2)}) async-start(bf16[8,96,512]{2,1,0:T(8,128)(2,1)} %bitcast.14), calls=%async_computation.2 | async-start | bytes 1572864 | tf_op jit(solution)/shard_map/dispatch_rows/all_to_all | solution.py:584
  88.6 13.4 %collective-permute-start.15 = (bf16[2,192,512]{2,1,0:T(8,128)(2,1)}, bf16[2,192,512]{2,1,0:T(8,128)(2,1)S(1)}, u32[]{:S(2)}, u32[]{:S(2)}) collective-permute-start(bf16[2,192,512]{2,1,0:T(8,128)(2,1)} %get-tuple-element.106), channel_id=1, source_target_pairs={{64,0},{96,32},{128,64},{160,96},{192,128},{224,160},{0,192},{32,2... | collective-permute-start | bytes 1179656 | tf_op jit(solution)/shard_map/turn_down/ppermute | solution.py:512
  89.3 20.3 %collective-permute-start.16 = (bf16[2,192,512]{2,1,0:T(8,128)(2,1)}, bf16[2,192,512]{2,1,0:T(8,128)(2,1)S(1)}, u32[]{:S(2)}, u32[]{:S(2)}) collective-permute-start(bf16[2,192,512]{2,1,0:T(8,128)(2,1)} %get-tuple-element.107), channel_id=1, source_target_pairs={{96,0},{64,32},{160,64},{128,96},{224,128},{192,160},{32,192},{0,2... | collective-permute-start | bytes 1179656 | tf_op jit(solution)/shard_map/turn_down/ppermute | solution.py:512
  90.5 19.0 %collective-permute-start.17 = (bf16[2,192,512]{2,1,0:T(8,128)(2,1)}, bf16[2,192,512]{2,1,0:T(8,128)(2,1)S(1)}, u32[]{:S(2)}, u32[]{:S(2)}) collective-permute-start(bf16[2,192,512]{2,1,0:T(8,128)(2,1)} %get-tuple-element.108), channel_id=1, source_target_pairs={{192,0},{224,32},{0,64},{32,96},{64,128},{96,160},{128,192},{160,2... | collective-permute-start | bytes 1179656 | tf_op jit(solution)/shard_map/turn_down/ppermute | solution.py:512
  92.3 18.8 %collective-permute-start.18 = (bf16[2,192,512]{2,1,0:T(8,128)(2,1)S(1)}, bf16[2,192,512]{2,1,0:T(8,128)(2,1)}, u32[]{:S(2)}, u32[]{:S(2)}) collective-permute-start(bf16[2,192,512]{2,1,0:T(8,128)(2,1)S(1)} %copy-done.13), channel_id=1, source_target_pairs={{224,0},{192,32},{32,64},{0,96},{96,128},{64,160},{160,192},{128,2... | collective-permute-start | bytes 1179656 | tf_op jit(solution)/shard_map/turn_down/ppermute | solution.py:512
  111.1 21.2 %collective-permute-start.20 = (bf16[8,2,48,512]{3,2,1,0:T(8,128)(2,1)S(1)}, bf16[8,2,48,512]{3,2,1,0:T(8,128)(2,1)S(1)}, u32[]{:S(2)}, u32[]{:S(2)}) collective-permute-start(bf16[8,2,48,512]{3,2,1,0:T(8,128)(2,1)S(1)} %bitcast.34), channel_id=1, source_target_pairs={{64,0},{128,64},{192,128},{0,192},{65,1},{129,65},{193,129},{1,193... | collective-permute-start | bytes 2359304 | tf_op jit(solution)/shard_map/gather_rows/ppermute | solution.py:499
  111.6 20.7 %collective-permute-start.22 = (bf16[8,2,48,512]{3,2,1,0:T(8,128)(2,1)S(1)}, bf16[8,2,48,512]{3,2,1,0:T(8,128)(2,1)S(1)}, u32[]{:S(2)}, u32[]{:S(2)}) collective-permute-start(bf16[8,2,48,512]{3,2,1,0:T(8,128)(2,1)S(1)} %bitcast.35), channel_id=1, source_target_pairs={{192,0},{0,64},{64,128},{128,192},{193,1},{1,65},{65,129},{129,193... | collective-permute-start | bytes 2359304 | tf_op jit(solution)/shard_map/gather_rows/ppermute | solution.py:499
  114.3 22.3 %collective-permute-start.19 = (bf16[8,2,48,512]{3,2,1,0:T(8,128)(2,1)S(1)}, bf16[8,2,48,512]{3,2,1,0:T(8,128)(2,1)S(1)}, u32[]{:S(2)}, u32[]{:S(2)}) collective-permute-start(bf16[8,2,48,512]{3,2,1,0:T(8,128)(2,1)S(1)} %bitcast.36), channel_id=1, source_target_pairs={{0,32},{32,0},{1,33},{33,1},{2,34},{34,2},{3,35},{35,3},{4,36},{36... | collective-permute-start | bytes 2359304 | tf_op jit(solution)/shard_map/gather_rows/ppermute | solution.py:503
  132.9 12.3 %collective-permute-start.24 = (bf16[8,48,512]{2,1,0:T(8,128)(2,1)S(1)}, bf16[8,48,512]{2,1,0:T(8,128)(2,1)S(1)}, u32[]{:S(2)}, u32[]{:S(2)}) collective-permute-start(bf16[8,48,512]{2,1,0:T(8,128)(2,1)S(1)} %slice_bitcast_fusion.1), channel_id=1, source_target_pairs={{64,0},{128,64},{192,128},{0,192},{65,1},{129,65},{193,129},{1,193... | collective-permute-start | bytes 1179656 | tf_op jit(solution)/shard_map/gather_rows/ppermute | solution.py:499
  133.1 12.2 %collective-permute-start.25 = (bf16[8,48,512]{2,1,0:T(8,128)(2,1)S(1)}, bf16[8,48,512]{2,1,0:T(8,128)(2,1)S(1)}, u32[]{:S(2)}, u32[]{:S(2)}) collective-permute-start(bf16[8,48,512]{2,1,0:T(8,128)(2,1)S(1)} %slice_bitcast_fusion), channel_id=1, source_target_pairs={{192,0},{0,64},{64,128},{128,192},{193,1},{1,65},{65,129},{129,193... | collective-permute-start | bytes 1179656 | tf_op jit(solution)/shard_map/gather_rows/ppermute | solution.py:499
  151.4 10.7 %collective-permute-start.28 = (bf16[384,384]{1,0:T(8,128)(2,1)S(1)}, bf16[384,384]{1,0:T(8,128)(2,1)S(1)}, u32[]{:S(2)}, u32[]{:S(2)}) collective-permute-start(bf16[384,384]{1,0:T(8,128)(2,1)S(1)} %expert_up.3.refs_0_), channel_id=1, source_target_pairs={{64,0},{128,64},{192,128},{0,192},{65,1},{129,65},{193,129},{1,193... | collective-permute-start | bytes 884744 | tf_op jit(solution)/shard_map/gather_units/ppermute | solution.py:499
  152.8 9.2 %collective-permute-start.30 = (bf16[384,384]{1,0:T(8,128)(2,1)S(1)}, bf16[384,384]{1,0:T(8,128)(2,1)S(1)}, u32[]{:S(2)}, u32[]{:S(2)}) collective-permute-start(bf16[384,384]{1,0:T(8,128)(2,1)S(1)} %expert_up.3.refs_0_), channel_id=1, source_target_pairs={{192,0},{0,64},{64,128},{128,192},{193,1},{1,65},{65,129},{129,193... | collective-permute-start | bytes 884744 | tf_op jit(solution)/shard_map/gather_units/ppermute | solution.py:499
  154.8 10.1 %collective-permute-start.27 = (bf16[384,384]{1,0:T(8,128)(2,1)S(1)}, bf16[384,384]{1,0:T(8,128)(2,1)S(1)}, u32[]{:S(2)}, u32[]{:S(2)}) collective-permute-start(bf16[384,384]{1,0:T(8,128)(2,1)S(1)} %expert_up.3.refs_0_), channel_id=1, source_target_pairs={{0,32},{32,0},{1,33},{33,1},{2,34},{34,2},{3,35},{35,3},{4,36},{36... | collective-permute-start | bytes 884744 | tf_op jit(solution)/shard_map/gather_units/ppermute | solution.py:503
  162.6 10.6 %collective-permute-start.32 = (bf16[384,384]{1,0:T(8,128)(2,1)S(1)}, bf16[384,384]{1,0:T(8,128)(2,1)}, u32[]{:S(2)}, u32[]{:S(2)}) collective-permute-start(bf16[384,384]{1,0:T(8,128)(2,1)S(1)} %expert_up.3.refs_0_), channel_id=1, source_target_pairs={{128,0},{192,64},{0,128},{64,192},{129,1},{193,65},{1,129},{65,193... | collective-permute-start | bytes 884744 | tf_op jit(solution)/shard_map/gather_units/ppermute | solution.py:499
  210.2 5.9 %collective-permute-start.34 = (bf16[48,512]{1,0:T(8,128)(2,1)S(1)}, bf16[48,512]{1,0:T(8,128)(2,1)S(1)}, u32[]{:S(2)}, u32[]{:S(2)}) collective-permute-start(bf16[48,512]{1,0:T(8,128)(2,1)S(1)} %get-tuple-element.132), channel_id=1, source_target_pairs={{3,0},{0,1},{1,2},{2,3},{7,4},{4,5},{5,6},{6,7},{11,8},{8,9},{9,10... | collective-permute-start | bytes 147464 | tf_op jit(solution)/shard_map/mix/ppermute | solution.py:487
  210.3 5.8 %collective-permute-start.35 = (bf16[48,512]{1,0:T(8,128)(2,1)S(1)}, bf16[48,512]{1,0:T(8,128)(2,1)S(1)}, u32[]{:S(2)}, u32[]{:S(2)}) collective-permute-start(bf16[48,512]{1,0:T(8,128)(2,1)S(1)} %get-tuple-element.133), channel_id=1, source_target_pairs={{2,0},{3,1},{0,2},{1,3},{6,4},{7,5},{4,6},{5,7},{10,8},{11,9},{8,1... | collective-permute-start | bytes 147464 | tf_op jit(solution)/shard_map/mix/ppermute | solution.py:487
  (32 other events, 282.3 us)
Sparse Core Ops, SparseCore 0:
  9.1 43.8 all-gather.2

commit v3 on v2

--- a/solution.py
+++ b/solution.py
@@ -24,13 +24,14 @@
 FFS = 192
 SCALE = HEAD ** (-0.5)
 EPS = 1e-06
+UP_MB = 24
 MASKED = -1e30
 CTX = ("y", "core")
 BF = jnp.bfloat16
 F32 = jnp.float32
 
 
-def params(mb=40):
+def params(mb=16):
     return pltpu.CompilerParams(vmem_limit_bytes=mb * 1024 * 1024)
 
 
@@ -46,7 +47,7 @@
 
 
 def attention_kernel(
-    place, owner, fill, phase_owner, phase_fill, relay, q, kv, ph, fk, fv, out, bias, keys, vals, qf
+    place, owner, fill, phase_owner, phase_fill, relay, q, kv, ph, fk, fv, out, bias, keys, vals, qf, fresh_k, fresh_v
 ):
     @pl.when(pl.program_id(0) == 0)
     def _():
@@ -86,10 +87,14 @@
 
     keys[0:768, :] = kv[:, 0].reshape(768, HEAD)
     keys[768:1024, :] = ph[:, 0].reshape(256, HEAD)
-    keys[1024 : 1024 + ROWS, :] = fk[...]
     vals[0:768, :] = kv[:, 1].reshape(768, HEAD)
     vals[768:1024, :] = ph[:, 1].reshape(256, HEAD)
-    vals[1024 : 1024 + ROWS, :] = fv[...]
+    for n in range(ROWS):
+        at = (n // 24, n % 24 // 6, n % 6)
+        fresh_k[2 * n : 2 * n + 2, :] = fk[at].astype(F32)
+        fresh_v[2 * n : 2 * n + 2, :] = fv[at].astype(F32)
+    keys[1024 : 1024 + ROWS, :] = fresh_k[pl.ds(0, ROWS, 2), :].astype(BF)
+    vals[1024 : 1024 + ROWS, :] = fresh_v[pl.ds(1, ROWS, 2), :].astype(BF)
     for n in range(12):
         qf[n * 4 : n * 4 + 4, :] = q[n // 6, n % 6].astype(F32)
     lane = lax.broadcasted_iota(jnp.int32, (ROWS, HEAD), 1)
@@ -131,8 +136,8 @@
             pl.BlockSpec((2, 6, 4, 16 * HEAD), lambda k: (0, 0, 0, k)),
             pl.BlockSpec((24, 2, 32, HEAD), lambda k: (0, 0, 0, k)),
             pl.BlockSpec((8, 2, 32, HEAD), lambda k: (0, 0, 0, k)),
-            pl.BlockSpec((ROWS, HEAD), lambda k: (0, k)),
-            pl.BlockSpec((ROWS, HEAD), lambda k: (0, KV_HEADS + k)),
+            pl.BlockSpec((2, 4, 6, 2, HEAD), lambda k: (0, 0, 0, 0, k)),
+            pl.BlockSpec((2, 4, 6, 2, HEAD), lambda k: (0, 0, 0, 0, k)),
         ],
         out_specs=pl.BlockSpec((2, ROWS, 9 * HEAD), lambda k: (k, 0, 0)),
         out_shape=jax.ShapeDtypeStruct((NC, ROWS, 9 * HEAD), BF),
@@ -141,6 +146,8 @@
             pltpu.VMEM((KEYS, HEAD), BF),
             pltpu.VMEM((KEYS, HEAD), BF),
             pltpu.VMEM((ROWS, 16 * HEAD), F32),
+            pltpu.VMEM((2 * ROWS, HEAD), F32),
+            pltpu.VMEM((2 * ROWS, HEAD), F32),
         ],
         compiler_params=params(62),
         name="attention",
@@ -329,24 +336,34 @@
 AROUND = [(0, 0), (0, 1), (1, 0), (1, 1), (3, 0), (3, 1), (2, 0), (2, 1)]
 
 
-def up_kernel(around, first, last, place, *refs):
-    count = len(around)
-    xs, gates, ups = refs[:count], refs[count : 2 * count], refs[2 * count : 3 * count]
-    refs = refs[3 * count :]
-    if first:
-        both = jnp.zeros((2 * FFS, EXPERT_ROWS), F32)
-        square = jnp.zeros((EXPERT_ROWS, HEAD), F32)
-    else:
-        both, square = refs[0][0], refs[1][0]
-        refs = refs[2:]
+def squares(rows):
+    total = jnp.zeros((EXPERT_ROWS, HEAD), F32)
+    for m in range(COLS // HEAD):
+        wide = rows[:, m * HEAD : (m + 1) * HEAD].astype(F32)
+        total = total + wide * wide
+    return total
+
+
+def up_near_kernel(place, *refs):
+    n = 6
+    xs, gates, ups, (both_out, square_out) = refs[:n], refs[n : 2 * n], refs[2 * n : 3 * n], refs[3 * n :]
+    both = jnp.zeros((2 * FFS, EXPERT_ROWS), F32)
+    square = jnp.zeros((EXPERT_ROWS, HEAD), F32)
     for x, wg, wu in zip(xs, gates, ups):
         rows = x[...].reshape(EXPERT_ROWS, COLS)
-        weights = jnp.concatenate([wg[0], wu[0]], axis=0)
-        both = both + dot(weights, rows, ((1,), (1,)))
-        for m in range(COLS // HEAD):
-            wide = rows[:, m * HEAD : (m + 1) * HEAD].astype(F32)
-            square = square + wide * wide
-    if last:
+        both = both + dot(jnp.concatenate([wg[0], wu[0]], axis=0), rows, ((1,), (1,)))
+        square = square + squares(rows)
+    both_out[0], square_out[0] = both, square
+
+
+def up_far_kernel(place, *refs):
+    xs, gates, ups, (both_in, square_in, out) = refs[:4], refs[4:6], refs[6:8], refs[8:]
+    for e in range(2):
+        both, square = both_in[e], square_in[e]
+        for x, wg, wu in zip(xs[2 * e : 2 * e + 2], gates, ups):
+            rows = x[...].reshape(EXPERT_ROWS, COLS)
+            both = both + dot(jnp.concatenate([wg[e], wu[e]], axis=0), rows, ((1,), (1,)))
+            square = square + squares(rows)
         total = lax.dot_general(
             jnp.ones((8, HEAD), F32),
             square,
@@ -356,52 +373,55 @@
         )[0:1]
         scale = lax.rsqrt(total * (1.0 / WIDTH) + EPS)
         v = both[0:FFS] * scale
-        refs[0][...] = (v / (1.0 + jnp.exp(-v)) * (both[FFS:] * scale)).astype(BF)
-    else:
-        refs[0][0], refs[1][0] = both, square
-
-
-def column_of(dy, dc):
-    def index(e, place):
-        core = place[3]
-        return e, 0, lax.rem(place[2] + dy, NY) * NCORE + (1 - core if dc else core)
-
-    return index
-
-
-def expert_up(place, around, xs, wg, wu, sums=()):
-    last = len(sums) > 0
-    w_specs = [pl.BlockSpec((1, FFS, COLS), column_of(dy, dc)) for dy, dc in around]
-    shapes = [(2, 2 * FFS, EXPERT_ROWS), (2, EXPERT_ROWS, HEAD)]
-    sum_specs = [pl.BlockSpec((1,) + shape[1:], lambda e, p: (e, 0, 0)) for shape in shapes]
-    x_specs = []
-    for x in xs:
-        if x.shape[1] == 2:
-            x_specs.append(pl.BlockSpec((NZ, 1, ROWS, COLS), lambda e, p: (0, e, 0, 0)))
-        else:
-            x_specs.append(pl.BlockSpec((1, EXPERT_ROWS, COLS), lambda e, p: (e, 0, 0)))
-    if last:
-        out_specs = pl.BlockSpec((FFS, EXPERT_ROWS), lambda e, p: (e, 0))
-        out_shape = jax.ShapeDtypeStruct((2 * FFS, EXPERT_ROWS), BF)
-    else:
-        out_specs = sum_specs
-        out_shape = [jax.ShapeDtypeStruct(shape, F32) for shape in shapes]
-    n = len(xs)
-    return pl.pallas_call(
-        functools.partial(up_kernel, around, not last, last),
+        unit = (v / (1.0 + jnp.exp(-v)) * (both[FFS:] * scale)).astype(BF)
+        out[e * FFS : (e + 1) * FFS, :] = unit
+
+
+def columns_at(place, dy, dc):
+    return lax.rem(place[2] + dy, NY) * NCORE + (1 - place[3] if dc else place[3])
+
+
+SUMS = [(2, 2 * FFS, EXPERT_ROWS), (2, EXPERT_ROWS, HEAD)]
+
+
+def expert_up_near(place, xs, wg, wu):
+    def weight(dy, dc):
+        return pl.BlockSpec((1, FFS, COLS), lambda e, p: (e, 0, columns_at(p, dy, dc)))
+
+    weights = [weight(*at) for at in AROUND[:6]]
+    return pl.pallas_call(
+        up_near_kernel,
         grid_spec=pltpu.PrefetchScalarGridSpec(
             num_scalar_prefetch=1,
             grid=(2,),
-            in_specs=x_specs + w_specs + w_specs + (sum_specs if last else []),
-            out_specs=out_specs,
+            in_specs=[pl.BlockSpec((NZ, 1, ROWS, COLS), lambda e, p: (0, e, 0, 0))] * 6 + weights * 2,
+            out_specs=[pl.BlockSpec((1,) + shape[1:], lambda e, p: (e, 0, 0)) for shape in SUMS],
         ),
-        out_shape=out_shape,
-        compiler_params=params(50),
-        cost_estimate=pl.CostEstimate(
-            flops=n * 1000000000, bytes_accessed=n * 2000000, transcendentals=0
+        out_shape=[jax.ShapeDtypeStruct(shape, F32) for shape in SUMS],
+        compiler_params=params(UP_MB),
+        cost_estimate=pl.CostEstimate(flops=6000000000, bytes_accessed=12000000, transcendentals=0),
+        name="expert_up",
+    )(place, *xs, *[wg] * 6, *[wu] * 6)
+
+
+def expert_up_far(place, xs, wg, wu, sums):
+    def weight(dy, dc):
+        return pl.BlockSpec((2, FFS, COLS), lambda i, p: (0, 0, columns_at(p, dy, dc)))
+
+    whole = lambda shape: pl.BlockSpec(shape, lambda i, p: (0,) * len(shape))
+    weights = [weight(*at) for at in AROUND[6:]]
+    return pl.pallas_call(
+        up_far_kernel,
+        grid_spec=pltpu.PrefetchScalarGridSpec(
+            num_scalar_prefetch=1,
+            grid=(1,),
+            in_specs=[whole((NZ, ROWS, COLS))] * 4 + weights * 2 + [whole(shape) for shape in SUMS],
+            out_specs=whole((2 * FFS, EXPERT_ROWS)),
         ),
-        name="expert_up",
-    )(place, *xs, *[wg] * n, *[wu] * n, *sums)
+        out_shape=jax.ShapeDtypeStruct((2 * FFS, EXPERT_ROWS), BF),
+        compiler_params=params(UP_MB),
+        name="expert_up_far",
+    )(place, *xs, wg, wg, wu, wu, *sums)
 
 
 def split_kernel(place, w, *outs):
@@ -426,40 +446,44 @@
     )(place, w)
 
 
-def down_kernel(count, last, *refs):
-    hs, ws, refs = refs[:count], refs[count : 2 * count], refs[2 * count :]
+def down_near_kernel(*refs):
+    hs, ws, out = refs[:6], refs[6:12], refs[12]
     total = dot(hs[0][...], ws[0][0], ((0,), (0,)))
     for h, w in zip(hs[1:], ws[1:]):
         total = total + dot(h[...], w[0], ((0,), (0,)))
-    if last:
-        total = total + refs[0][0]
-        refs[1][...] = total.astype(BF).reshape(NZ, 1, ROWS, COLS)
-    else:
-        refs[0][0] = total
-
-
-def expert_down(hs, ws, total=None):
-    n, last = len(hs), total is not None
-    sum_spec = pl.BlockSpec((1, EXPERT_ROWS, COLS), lambda e: (e, 0, 0))
-    if last:
-        out_spec = pl.BlockSpec((NZ, 1, ROWS, COLS), lambda e: (0, e, 0, 0))
-        out_shape = jax.ShapeDtypeStruct((NZ, 2, ROWS, COLS), BF)
-    else:
-        out_spec, out_shape = sum_spec, jax.ShapeDtypeStruct((2, EXPERT_ROWS, COLS), F32)
-    return pl.pallas_call(
-        functools.partial(down_kernel, n, last),
+    out[0] = total
+
+
+def expert_down_near(hs, ws):
+    return pl.pallas_call(
+        down_near_kernel,
         grid=(2,),
-        in_specs=[pl.BlockSpec((FFS, EXPERT_ROWS), lambda e: (e, 0))] * n
-        + [pl.BlockSpec((1, FFS, COLS), lambda e: (e, 0, 0))] * n
-        + ([sum_spec] if last else []),
-        out_specs=out_spec,
-        out_shape=out_shape,
-        compiler_params=params(62),
-        cost_estimate=pl.CostEstimate(
-            flops=n * 700000000, bytes_accessed=n * 1000000, transcendentals=0
-        ),
+        in_specs=[pl.BlockSpec((FFS, EXPERT_ROWS), lambda e: (e, 0))] * 6
+        + [pl.BlockSpec((1, FFS, COLS), lambda e: (e, 0, 0))] * 6,
+        out_specs=pl.BlockSpec((1, EXPERT_ROWS, COLS), lambda e: (e, 0, 0)),
+        out_shape=jax.ShapeDtypeStruct((2, EXPERT_ROWS, COLS), F32),
+        compiler_params=params(),
+        cost_estimate=pl.CostEstimate(flops=2000000000, bytes_accessed=6000000, transcendentals=0),
         name="expert_down",
-    )(*hs, *ws, *([total] if last else []))
+    )(*hs, *ws)
+
+
+def down_far_kernel(*refs):
+    hs, ws, total_in, out = refs[:4], refs[4:6], refs[6], refs[7]
+    for e in range(2):
+        total = total_in[e]
+        for h, w in zip(hs[2 * e : 2 * e + 2], ws):
+            total = total + dot(h[...], w[e], ((0,), (0,)))
+        out[:, e] = total.astype(BF).reshape(NZ, ROWS, COLS)
+
+
+def expert_down_far(hs, ws, total):
+    return pl.pallas_call(
+        down_far_kernel,
+        out_shape=jax.ShapeDtypeStruct((NZ, 2, ROWS, COLS), BF),
+        compiler_params=params(),
+        name="expert_down_far",
+    )(*hs, *ws, total)
 
 
 def mix_kernel(place, back, mix_high, mix_low, o0, o1, o2, o3, rows):
@@ -549,7 +573,7 @@
             queries.transpose(0, 2, 1, 3),
             kv_cache[0],
             phased[0],
-            new_kv.reshape(ROWS, 2 * KV_HEADS * HEAD),
+            new_kv,
         )
     with jax.named_scope("gather_tables"):
         parts, expert_ids, gate_weights, hidden_in, w_down = lax.optimization_barrier(
@@ -566,8 +590,7 @@
         attended = join(parts)
     with jax.named_scope("turn_down"):
         down_cols = list(down_parts)
-        for n in (6, 7):
-            down_cols[n] = from_ctx(down_parts[n], *AROUND[n])
+        down_cols[6] = from_ctx(down_parts[6], *AROUND[6])
     with jax.named_scope("project_rows"):
         partial = project(place, along_x(attended), o_cols)
     with jax.named_scope("sum_projection"):
@@ -575,12 +598,15 @@
         columns, down_cols = lax.optimization_barrier((columns, down_cols))
         projected = along_x(add_up(columns))
     with jax.named_scope("turn_down"):
-        for n in range(1, 6):
+        for n in (1, 2, 4, 3, 5, 7):
             down_cols[n] = from_ctx(down_cols[n], *AROUND[n])
     with jax.named_scope("find_routes"):
         send, mix_high, mix_low = routes(place, tables)
     with jax.named_scope("dispatch_rows"):
         packed, mine = dispatch(place, hidden, projected, send)
+        packed, down_cols[1], down_cols[2], down_cols[4] = lax.optimization_barrier(
+            (packed, down_cols[1], down_cols[2], down_cols[4])
+        )
         arrived = lax.all_to_all(packed.reshape(NZ, 96, COLS), "z", 0, 0, tiled=True)
         arrived = arrived.reshape(NZ, 2, ROWS, COLS)
         arrived, down_cols = lax.optimization_barrier((arrived, down_cols))
@@ -592,19 +618,21 @@
             near += [value, other_core(value)]
     with jax.named_scope("up"):
         gate_t, up_t = w_gate.transpose(0, 2, 1), w_up.transpose(0, 2, 1)
-        sums = expert_up(place, AROUND[:6], near, gate_t, up_t)
+        sums = expert_up_near(place, near, gate_t, up_t)
         sums, far = lax.optimization_barrier((sums, far))
-        far = jnp.stack(far).reshape(2, EXPERT_ROWS, COLS)
-        units = expert_up(place, AROUND[6:], [far, other_core(far)], gate_t, up_t, sums)
+        far = [far[0], other_core(far[0]), far[1], other_core(far[1])]
+        units = expert_up_far(place, far, gate_t, up_t, sums)
     with jax.named_scope("gather_units"):
-        after, before, far = from_y(units, 1), from_y(units, 3), from_y(units, 2)
+        after, before = from_y(units, 1), from_y(units, 3)
+        far = [from_y(after[:FFS], 1), from_y(before[FFS:], 3)]
         near = []
         for value in (units, after, before):
             near += [value, other_core(value)]
     with jax.named_scope("down"):
-        total = expert_down(near, down_cols[:6])
+        total = expert_down_near(near, down_cols[:6])
         total, far = lax.optimization_barrier((total, far))
-        outcome = expert_down([far, other_core(far)], down_cols[6:], total)
+        far = [far[0], other_core(far[0]), far[1], other_core(far[1])]
+        outcome = expert_down_far(far, down_cols[6:], total)
     with jax.named_scope("return_rows"):
         back = lax.all_to_all(outcome.reshape(NZ, 96, COLS), "z", 0, 0, tiled=True)
     with jax.named_scope("mix"):

time: 228 us -> 231 us (1.013)
  waiting for transfers between devices: 71.5 us -> 80.8 us
  Pallas kernels: 40.6 us -> 32.3 us
  starting transfers between devices: 60.8 us -> 63.2 us
    pallas_call x4, Pallas kernels: 17.4 us -> 8.99 us  [the longest x1 4.52 us: expert_up_near(): pl.pallas_call(up_near_kernel, grid_spec=pltpu.PrefetchScalarGridSpec(num...]
    ppermute x7 -> x8, starting transfers between devices: 12.7 us -> 18.3 us  [from_y(): return lax.ppermute(value, 'y', [((i + d) % NY, i) for i in range(NY)])]
    ppermute x7 -> x8, waiting for transfers between devices: 29.1 us -> 34.5 us  [from_y(): return lax.ppermute(value, 'y', [((i + d) % NY, i) for i in range(NY)])]
    all_to_all x1, starting transfers between devices: 8.99 us -> 4.08 us  [body(): lax.all_to_all(packed.reshape(NZ, 96, COLS), 'z', 0, 0, tiled=True)]
    ppermute x7, waiting for transfers between devices: 19.1 us -> 16.5 us  [from_ctx(): return lax.ppermute(value, CTX, pairs)]
    unnamed x47 -> x34, local copies, waits for them, and re-layouts: 6.08 us -> 4.11 us
  transfers between devices with their start and end apart: 41 -> 44, of which waited for: 19 -> 27; matrix products, arithmetic and copies ran while one was open for 1% -> 0% of each run, Pallas kernels for 14% -> 13%
where the time goes in v3:
time: 231 us; the launch traced here: 226 us
  waiting for transfers between devices  80.8 us (35%)
  starting transfers between devices  63.2 us (27%)
  Pallas kernels  32.3 us (14%)
  blocking collectives  30.3 us (13%)
  between operations  13.9 us (6%)
  local copies, waits for them, and re-layouts  5.16 us (2%)
    ppermute x8, waiting for transfers between devices, from_y(): return lax.ppermute(value, 'y', [((i + d) % NY, i) for i in range(NY)])  34.5 us
    all_to_all x1, blocking collectives, body(): back = lax.all_to_all(outcome.reshape(NZ, 96, COLS), 'z', 0, 0, tiled=True)  30.3 us
    ppermute x15, starting transfers between devices, from_x(): return lax.ppermute(value, 'x', [((i + d) % NX, i) for i in range(NX)])  20.8 us
    ppermute x8, starting transfers between devices, from_y(): return lax.ppermute(value, 'y', [((i + d) % NY, i) for i in range(NY)])  18.3 us
    ppermute x7, waiting for transfers between devices, from_ctx(): return lax.ppermute(value, CTX, pairs)  16.5 us
    ppermute x15, waiting for transfers between devices, from_x(): return lax.ppermute(value, 'x', [((i + d) % NX, i) for i in range(NX)])  12.4 us
    pallas_call x1, Pallas kernels, attention(): pl.pallas_call(attention_kernel, grid=(KV_HEADS,), in_specs=[smem] * 6 +...  11.5 us
    ppermute x7, starting transfers between devices, from_ctx(): return lax.ppermute(value, CTX, pairs)  7.88 us
  transfers between devices with their start and end apart: 44, of which 27 were waited for; matrix products, arithmetic and copies ran while one was open for 0% of the time, Pallas kernels for 13%

profile of v3, /device:TPU:24, one launch (start us, length us, event | category | flops | bytes accessed | tf_op | source)
XLA Modules:
  0.0 226.3 jit_solution(18402058228997245827)
XLA Ops:
  7.9 11.5 %attention.1 = bf16[8,48,1152]{2,1,0:T(8,128)(2,1)} custom-call(s32[4]{0:T(128)} %pad_add_fusion.place, s32[1,24]{1,0:T(1,128)} %owner.1, s32[1,24]{1,0:T(1,128)} %fill.1, s32[1,64]{1,0:T(1,128)} %phase_owner.1, s32[1,64]{1,0:T(1,128)} %phase_fill.1, s32[8,8]{1,0:T(8,128)} %bitcast.55, bf16[2,6,4,8192]{3,2,1,0:T(4,128)(2,1)} %bitcast.51, ...), custom_call_target="tpu_custom_call" | custom-call | tf_op jit(solution)/shard_map/attend/attention/pallas_call | solution.py:131
  19.5 5.5 %all-to-all-start = ((bf16[8,48,1152]{2,1,0:T(8,128)(2,1)}), bf16[8,48,1152]{2,1,0:T(8,128)(2,1)S(1)}, u32[]{:S(2)}, u32[]{:S(2)}) async-start(bf16[8,48,1152]{2,1,0:T(8,128)(2,1)} %attention.1), calls=%async_computation | async-start | bytes 1769472 | tf_op jit(solution)/shard_map/join_parts/all_to_all | solution.py:586
  25.8 2.7 %collective-permute-start.4 = (bf16[48,512]{1,0:T(8,128)(2,1)S(1)}, bf16[48,512]{1,0:T(8,128)(2,1)S(1)}, u32[]{:S(2)}, u32[]{:S(2)}) collective-permute-start(bf16[48,512]{1,0:T(8,128)(2,1)S(1)} %reshape.34.h0), channel_id=1, source_target_pairs={{2,0},{3,1},{0,2},{1,3},{6,4},{7,5},{4,6},{5,7},{10,8},{11,9},{8,1... | collective-permute-start | bytes 147464 | tf_op jit(solution)/shard_map/gather_tables/ppermute | solution.py:511
  31.5 3.8 %collective-permute-done.2.t3 = f32[2,48,8]{2,1,0:T(8,128)S(1)} collective-permute-done((f32[2,48,8]{2,1,0:T(8,128)S(1)}, f32[2,48,8]{2,1,0:T(8,128)S(1)}, u32[]{:S(2)}, u32[]{:S(2)}) %collective-permute-start.2) | collective-permute-done | bytes 3104 | tf_op jit(solution)/shard_map/gather_tables/ppermute | solution.py:511
  35.4 3.2 %split_down.1 = (bf16[2,192,512]{2,1,0:T(8,128)(2,1)}, bf16[2,192,512]{2,1,0:T(8,128)(2,1)}, bf16[2,192,512]{2,1,0:T(8,128)(2,1)}, bf16[2,192,512]{2,1,0:T(8,128...) custom-call(s32[4]{0:T(128)} %pad_add_fusion.place, ...), custom_call_target="tpu_custom_call" | custom-call | tf_op jit(solution)/shard_map/gather_tables/split_down/pallas_call | solution.py:435
  48.1 4.9 %all-gather.3.cloned.1.call-done = bf16[8192,128]{1,0:T(8,128)(2,1)} async-done(((bf16[1024,128]{1,0:T(8,128)(2,1)}), bf16[8192,128]{1,0:T(8,128)(2,1)}) %all-gather.3.cloned.1.call-update) | async-done | bytes 2097168 | tf_op jit(solution)/shard_map/gather_projection/all_gather | solution.py:564
  53.0 2.8 %project.1 = bf16[8,192,128]{2,1,0:T(8,128)(2,1)} custom-call(s32[4]{0:T(128)} %pad_add_fusion.place, bf16[48,1024]{1,0:T(8,128)(2,1)} %copy-done.3, bf16[48,1024]{1,0:T(8,128)(2,1)} %copy-done.14, bf16[48,1024]{1,0:T(8,128)(2,1)} %copy-done.13, bf16[48,1024]{1,0:T(8,128)(2,1)} %copy-done.12, bf16[8,1024,128]{2,1,0:T(8,128)(2,1)} %bitcast.49), custom_call_target="tpu_custom_call" | custom-call | tf_op jit(solution)/shard_map/project_rows/project/pallas_call | solution.py:199
  55.8 5.0 %all-to-all-start.1 = ((bf16[8,192,128]{2,1,0:T(8,128)(2,1)}), bf16[8,192,128]{2,1,0:T(8,128)(2,1)S(1)}, u32[]{:S(2)}, u32[]{:S(2)}) async-start(bf16[8,192,128]{2,1,0:T(8,128)(2,1)} %project.1), calls=%async_computation.1 | async-start | bytes 786432 | tf_op jit(solution)/shard_map/sum_projection/all_to_all | solution.py:597
  60.9 6.9 %all-to-all-done.1.parts = bf16[8,192,128]{2,1,0:T(8,128)(2,1)S(1)} async-done(((bf16[8,192,128]{2,1,0:T(8,128)(2,1)}), bf16[8,192,128]{2,1,0:T(8,128)(2,1)S(1)}, u32[]{:S(2)}, u32[]{:S(2)}) %all-to-all-start.1) | async-done | bytes 393248 | tf_op jit(solution)/shard_map/sum_projection/all_to_all | solution.py:597
  67.7 3.5 %collective-permute-start.15 = (bf16[2,192,512]{2,1,0:T(8,128)(2,1)}, bf16[2,192,512]{2,1,0:T(8,128)(2,1)S(1)}, u32[]{:S(2)}, u32[]{:S(2)}) collective-permute-start(bf16[2,192,512]{2,1,0:T(8,128)(2,1)} %get-tuple-element.111), channel_id=1, source_target_pairs={{192,0},{224,32},{0,64},{32,96},{64,128},{96,160},{128,192},{160,2... | collective-permute-start | bytes 1179656 | tf_op jit(solution)/shard_map/turn_down/ppermute | solution.py:536
  71.3 1.5 collective-permute-start.12
  72.8 2.7 %collective-permute-start.11 = (bf16[192,128]{1,0:T(8,128)(2,1)S(1)}, bf16[192,128]{1,0:T(8,128)(2,1)S(1)}, u32[]{:S(2)}, u32[]{:S(2)}) collective-permute-start(bf16[192,128]{1,0:T(8,128)(2,1)S(1)} %add_up.1.p0), channel_id=1, source_target_pairs={{2,0},{3,1},{0,2},{1,3},{6,4},{7,5},{4,6},{5,7},{10,8},{11,9},{8,1... | collective-permute-start | bytes 147464 | tf_op jit(solution)/shard_map/sum_projection/ppermute | solution.py:511
  78.2 1.8 routes.1
  80.8 1.9 dispatch.1
  84.2 4.1 %all-to-all-start.2 = ((bf16[8,96,512]{2,1,0:T(8,128)(2,1)}), bf16[8,96,512]{2,1,0:T(8,128)(2,1)S(1)}, u32[]{:S(2)}, u32[]{:S(2)}) async-start(bf16[8,96,512]{2,1,0:T(8,128)(2,1)} %bitcast.14), calls=%async_computation.2 | async-start | bytes 1572864 | tf_op jit(solution)/shard_map/dispatch_rows/all_to_all | solution.py:610
  88.3 2.9 %collective-permute-start.17 = (bf16[2,192,512]{2,1,0:T(8,128)(2,1)}, bf16[2,192,512]{2,1,0:T(8,128)(2,1)S(1)}, u32[]{:S(2)}, u32[]{:S(2)}) collective-permute-start(bf16[2,192,512]{2,1,0:T(8,128)(2,1)} %get-tuple-element.118), channel_id=1, source_target_pairs={{224,0},{192,32},{32,64},{0,96},{96,128},{64,160},{160,192},{128,2... | collective-permute-start | bytes 1179656 | tf_op jit(solution)/shard_map/turn_down/ppermute | solution.py:536
  91.3 8.9 %collective-permute-done.16.refs_9_ = bf16[2,192,512]{2,1,0:T(8,128)(2,1)S(1)} collective-permute-done((bf16[2,192,512]{2,1,0:T(8,128)(2,1)}, bf16[2,192,512]{2,1,0:T(8,128)(2,1)S(1)}, u32[]{:S(2)}, u32[]{:S(2)}) %collective-permute-start.16) | collective-permute-done | bytes 393248 | tf_op jit(solution)/shard_map/turn_down/ppermute | solution.py:536
  100.2 6.8 %collective-permute-done.17.refs_11_ = bf16[2,192,512]{2,1,0:T(8,128)(2,1)S(1)} collective-permute-done((bf16[2,192,512]{2,1,0:T(8,128)(2,1)}, bf16[2,192,512]{2,1,0:T(8,128)(2,1)S(1)}, u32[]{:S(2)}, u32[]{:S(2)}) %collective-permute-start.17) | collective-permute-done | bytes 393248 | tf_op jit(solution)/shard_map/turn_down/ppermute | solution.py:536
  107.8 2.1 all-to-all-done.2
  112.0 16.2 %collective-permute-done.22 = bf16[8,2,48,512]{3,2,0,1:T(8,128)(2,1)S(1)} collective-permute-done((bf16[8,2,48,512]{3,2,0,1:T(8,128)(2,1)S(1)}, bf16[8,2,48,512]{3,2,0,1:T(8,128)(2,1)S(1)}, u32[]{:S(2)}, u32[]{:S(2)}) %collective-permute-start.22) | collective-permute-done | bytes 786464 | tf_op jit(solution)/shard_map/gather_rows/ppermute | solution.py:523
  128.3 2.9 %collective-permute-done.20 = bf16[8,2,48,512]{3,2,0,1:T(8,128)(2,1)S(1)} collective-permute-done((bf16[8,2,48,512]{3,2,0,1:T(8,128)(2,1)S(1)}, bf16[8,2,48,512]{3,2,0,1:T(8,128)(2,1)S(1)}, u32[]{:S(2)}, u32[]{:S(2)}) %collective-permute-start.20) | collective-permute-done | bytes 786464 | tf_op jit(solution)/shard_map/gather_rows/ppermute | solution.py:523
  132.1 11.5 %collective-permute-start.24 = (bf16[8,48,512]{2,1,0:T(8,128)(2,1)S(1)}, bf16[8,48,512]{2,1,0:T(8,128)(2,1)S(1)}, u32[]{:S(2)}, u32[]{:S(2)}) collective-permute-start(bf16[8,48,512]{2,1,0:T(8,128)(2,1)S(1)} %slice_bitcast_fusion.1), channel_id=1, source_target_pairs={{64,0},{128,64},{192,128},{0,192},{65,1},{129,65},{193,129},{1,193... | collective-permute-start | bytes 1179656 | tf_op jit(solution)/shard_map/gather_rows/ppermute | solution.py:523
  143.9 1.6 copy-done.2
  146.5 4.5 %expert_up.1 = (f32[2,384,384]{2,1,0:T(8,128)S(1)}, f32[2,384,128]{2,1,0:T(8,128)S(1)}) custom-call(s32[4]{0:T(128)S(1)} %copy-done.4, bf16[8,2,48,512]{3,2,1,0:T(8,128)(2,1)S(1)} %bitcast.46, bf16[8,2,48,512]{3,2,1,0:T(8,128)(2,1)S(1)} %collective-permute-done.19.refs_1_, bf16[8,2,48,512]{3,2,1,0:T(8,128)(2,1)S(1)} %copy.55.refs_2_, ...), custom_call_target="tpu_custom_call" | custom-call | flops 6000000000 | bytes 12000000 | tf_op jit(solution)/shard_map/up/expert_up/pallas_call | solution.py:392
  151.0 3.3 %collective-permute-done.24.refs_0_ = bf16[8,48,512]{2,1,0:T(8,128)(2,1)S(1)} collective-permute-done((bf16[8,48,512]{2,1,0:T(8,128)(2,1)S(1)}, bf16[8,48,512]{2,1,0:T(8,128)(2,1)S(1)}, u32[]{:S(2)}, u32[]{:S(2)}) %collective-permute-start.24) | collective-permute-done | bytes 393248 | tf_op jit(solution)/shard_map/gather_rows/ppermute | solution.py:523
  156.7 2.2 expert_up_far.1.refs_0_
  159.0 2.0 collective-permute-start.29
  161.0 7.0 %collective-permute-done.31.refs_4_ = bf16[384,384]{1,0:T(8,128)(2,1)S(1)} collective-permute-done((bf16[384,384]{1,0:T(8,128)(2,1)S(1)}, bf16[384,384]{1,0:T(8,128)(2,1)S(1)}, u32[]{:S(2)}, u32[]{:S(2)}) %collective-permute-start.31) | collective-permute-done | bytes 294944 | tf_op jit(solution)/shard_map/gather_units/ppermute | solution.py:523
  171.6 1.7 expert_down.1.refs_6_
  173.3 2.4 %collective-permute-done.34.refs_2_ = bf16[192,384]{1,0:T(8,128)(2,1)S(1)} collective-permute-done((bf16[192,384]{1,0:T(8,128)(2,1)S(1)}, bf16[192,384]{1,0:T(8,128)(2,1)S(1)}, u32[]{:S(2)}, u32[]{:S(2)}) %collective-permute-start.34) | collective-permute-done | bytes 147488 | tf_op jit(solution)/shard_map/gather_units/ppermute | solution.py:523
  179.2 30.3 %all_to_all.20 = bf16[8,96,512]{2,1,0:T(8,128)(2,1)S(1)} all-to-all(bf16[8,96,512]{2,1,0:T(8,128)(2,1)S(1)} %bitcast.47), channel_id=1, replica_groups=mesh['y'=4,'core'=2,'z'=8,'x'=4] {'z'}, dimensions={0} | all-to-all | bytes 1572864 | tf_op jit(solution)/shard_map/return_rows/all_to_all | solution.py:637
  211.0 3.5 %collective-permute-start.38 = (bf16[48,512]{1,0:T(8,128)(2,1)S(1)}, bf16[48,512]{1,0:T(8,128)(2,1)S(1)}, u32[]{:S(2)}, u32[]{:S(2)}) collective-permute-start(bf16[48,512]{1,0:T(8,128)(2,1)S(1)} %get-tuple-element.143), channel_id=1, source_target_pairs={{2,0},{3,1},{0,2},{1,3},{6,4},{7,5},{4,6},{5,7},{10,8},{11,9},{8,1... | collective-permute-start | bytes 147464 | tf_op jit(solution)/shard_map/mix/ppermute | solution.py:511
  (120 shorter events, 40.6 us)
Async XLA Ops:
  6.5 46.5 %all-gather.3.cloned.1.call-start = ((), (), s32[]{:S(2)}) async-start(), calls=%async_computation.4 | async-start | bytes 2359296 | tf_op jit(solution)/shard_map/gather_projection/all_gather | solution.py:564
  19.5 20.0 %all-to-all-start = ((bf16[8,48,1152]{2,1,0:T(8,128)(2,1)}), bf16[8,48,1152]{2,1,0:T(8,128)(2,1)S(1)}, u32[]{:S(2)}, u32[]{:S(2)}) async-start(bf16[8,48,1152]{2,1,0:T(8,128)(2,1)} %attention.1), calls=%async_computation | async-start | bytes 1769472 | tf_op jit(solution)/shard_map/join_parts/all_to_all | solution.py:586
  25.0 14.5 %collective-permute-start.5 = (bf16[48,512]{1,0:T(8,128)(2,1)S(1)}, bf16[48,512]{1,0:T(8,128)(2,1)S(1)}, u32[]{:S(2)}, u32[]{:S(2)}) collective-permute-start(bf16[48,512]{1,0:T(8,128)(2,1)S(1)} %reshape.34.h0), channel_id=1, source_target_pairs={{3,0},{0,1},{1,2},{2,3},{7,4},{4,5},{5,6},{6,7},{11,8},{8,9},{9,10... | collective-permute-start | bytes 147464 | tf_op jit(solution)/shard_map/gather_tables/ppermute | solution.py:511
  25.8 13.7 %collective-permute-start.4 = (bf16[48,512]{1,0:T(8,128)(2,1)S(1)}, bf16[48,512]{1,0:T(8,128)(2,1)S(1)}, u32[]{:S(2)}, u32[]{:S(2)}) collective-permute-start(bf16[48,512]{1,0:T(8,128)(2,1)S(1)} %reshape.34.h0), channel_id=1, source_target_pairs={{2,0},{3,1},{0,2},{1,3},{6,4},{7,5},{4,6},{5,7},{10,8},{11,9},{8,1... | collective-permute-start | bytes 147464 | tf_op jit(solution)/shard_map/gather_tables/ppermute | solution.py:511
  28.5 11.0 %collective-permute-start.3 = (bf16[48,512]{1,0:T(8,128)(2,1)S(1)}, bf16[48,512]{1,0:T(8,128)(2,1)S(1)}, u32[]{:S(2)}, u32[]{:S(2)}) collective-permute-start(bf16[48,512]{1,0:T(8,128)(2,1)S(1)} %reshape.34.h0), channel_id=1, source_target_pairs={{1,0},{2,1},{3,2},{0,3},{5,4},{6,5},{7,6},{4,7},{9,8},{10,9},{11,1... | collective-permute-start | bytes 147464 | tf_op jit(solution)/shard_map/gather_tables/ppermute | solution.py:511
  30.6 8.0 %collective-permute-start.1 = (f32[2,48,8]{2,1,0:T(8,128)S(1)}, f32[2,48,8]{2,1,0:T(8,128)S(1)}, u32[]{:S(2)}, u32[]{:S(2)}) collective-permute-start(f32[2,48,8]{2,1,0:T(8,128)S(1)} %pad_maximum_fusion.t0), channel_id=1, source_target_pairs={{2,0},{3,1},{0,2},{1,3},{6,4},{7,5},{4,6},{5,7},{10,8},{11,9},{8,1... | collective-permute-start | bytes 9224 | tf_op jit(solution)/shard_map/gather_tables/ppermute | solution.py:511
  40.3 5.9 %collective-permute-start.8 = (bf16[48,1024]{1,0:T(8,128)(2,1)S(1)}, bf16[48,1024]{1,0:T(8,128)(2,1)S(1)}, u32[]{:S(2)}, u32[]{:S(2)}) collective-permute-start(bf16[48,1024]{1,0:T(8,128)(2,1)S(1)} %join.1.a0), channel_id=1, source_target_pairs={{3,0},{0,1},{1,2},{2,3},{7,4},{4,5},{5,6},{6,7},{11,8},{8,9},{9,10... | collective-permute-start | bytes 294920 | tf_op jit(solution)/shard_map/project_rows/ppermute | solution.py:511
  41.6 6.1 %collective-permute-start.7 = (bf16[48,1024]{1,0:T(8,128)(2,1)S(1)}, bf16[48,1024]{1,0:T(8,128)(2,1)S(1)}, u32[]{:S(2)}, u32[]{:S(2)}) collective-permute-start(bf16[48,1024]{1,0:T(8,128)(2,1)S(1)} %join.1.a0), channel_id=1, source_target_pairs={{2,0},{3,1},{0,2},{1,3},{6,4},{7,5},{4,6},{5,7},{10,8},{11,9},{8,1... | collective-permute-start | bytes 294920 | tf_op jit(solution)/shard_map/project_rows/ppermute | solution.py:511
  44.4 16.5 %collective-permute-start.9 = (bf16[2,192,512]{2,1,0:T(8,128)(2,1)}, bf16[2,192,512]{2,1,0:T(8,128)(2,1)S(1)}, u32[]{:S(2)}, u32[]{:S(2)}) collective-permute-start(bf16[2,192,512]{2,1,0:T(8,128)(2,1)} %get-tuple-element.99), channel_id=1, source_target_pairs={{128,0},{160,32},{192,64},{224,96},{0,128},{32,160},{64,192},{96,2... | collective-permute-start | bytes 1179656 | tf_op jit(solution)/shard_map/turn_down/ppermute | solution.py:536
  55.8 11.9 %all-to-all-start.1 = ((bf16[8,192,128]{2,1,0:T(8,128)(2,1)}), bf16[8,192,128]{2,1,0:T(8,128)(2,1)S(1)}, u32[]{:S(2)}, u32[]{:S(2)}) async-start(bf16[8,192,128]{2,1,0:T(8,128)(2,1)} %project.1), calls=%async_computation.1 | async-start | bytes 786432 | tf_op jit(solution)/shard_map/sum_projection/all_to_all | solution.py:597
  67.7 15.0 %collective-permute-start.13 = (bf16[2,192,512]{2,1,0:T(8,128)(2,1)}, bf16[2,192,512]{2,1,0:T(8,128)(2,1)S(1)}, u32[]{:S(2)}, u32[]{:S(2)}) collective-permute-start(bf16[2,192,512]{2,1,0:T(8,128)(2,1)} %get-tuple-element.109), channel_id=1, source_target_pairs={{32,0},{0,32},{96,64},{64,96},{160,128},{128,160},{224,192},{192,2... | collective-permute-start | bytes 1179656 | tf_op jit(solution)/shard_map/turn_down/ppermute | solution.py:536
  67.7 15.7 %collective-permute-start.14 = (bf16[2,192,512]{2,1,0:T(8,128)(2,1)}, bf16[2,192,512]{2,1,0:T(8,128)(2,1)S(1)}, u32[]{:S(2)}, u32[]{:S(2)}) collective-permute-start(bf16[2,192,512]{2,1,0:T(8,128)(2,1)} %get-tuple-element.110), channel_id=1, source_target_pairs={{64,0},{96,32},{128,64},{160,96},{192,128},{224,160},{0,192},{32,2... | collective-permute-start | bytes 1179656 | tf_op jit(solution)/shard_map/turn_down/ppermute | solution.py:536
  67.7 16.5 %collective-permute-start.15 = (bf16[2,192,512]{2,1,0:T(8,128)(2,1)}, bf16[2,192,512]{2,1,0:T(8,128)(2,1)S(1)}, u32[]{:S(2)}, u32[]{:S(2)}) collective-permute-start(bf16[2,192,512]{2,1,0:T(8,128)(2,1)} %get-tuple-element.111), channel_id=1, source_target_pairs={{192,0},{224,32},{0,64},{32,96},{64,128},{96,160},{128,192},{160,2... | collective-permute-start | bytes 1179656 | tf_op jit(solution)/shard_map/turn_down/ppermute | solution.py:536
  72.8 7.2 %collective-permute-start.11 = (bf16[192,128]{1,0:T(8,128)(2,1)S(1)}, bf16[192,128]{1,0:T(8,128)(2,1)S(1)}, u32[]{:S(2)}, u32[]{:S(2)}) collective-permute-start(bf16[192,128]{1,0:T(8,128)(2,1)S(1)} %add_up.1.p0), channel_id=1, source_target_pairs={{2,0},{3,1},{0,2},{1,3},{6,4},{7,5},{4,6},{5,7},{10,8},{11,9},{8,1... | collective-permute-start | bytes 147464 | tf_op jit(solution)/shard_map/sum_projection/ppermute | solution.py:511
  84.2 25.6 %all-to-all-start.2 = ((bf16[8,96,512]{2,1,0:T(8,128)(2,1)}), bf16[8,96,512]{2,1,0:T(8,128)(2,1)S(1)}, u32[]{:S(2)}, u32[]{:S(2)}) async-start(bf16[8,96,512]{2,1,0:T(8,128)(2,1)} %bitcast.14), calls=%async_computation.2 | async-start | bytes 1572864 | tf_op jit(solution)/shard_map/dispatch_rows/all_to_all | solution.py:610
  88.3 11.9 %collective-permute-start.16 = (bf16[2,192,512]{2,1,0:T(8,128)(2,1)}, bf16[2,192,512]{2,1,0:T(8,128)(2,1)S(1)}, u32[]{:S(2)}, u32[]{:S(2)}) collective-permute-start(bf16[2,192,512]{2,1,0:T(8,128)(2,1)} %get-tuple-element.116), channel_id=1, source_target_pairs={{96,0},{64,32},{160,64},{128,96},{224,128},{192,160},{32,192},{0,2... | collective-permute-start | bytes 1179656 | tf_op jit(solution)/shard_map/turn_down/ppermute | solution.py:536
  88.3 18.6 %collective-permute-start.17 = (bf16[2,192,512]{2,1,0:T(8,128)(2,1)}, bf16[2,192,512]{2,1,0:T(8,128)(2,1)S(1)}, u32[]{:S(2)}, u32[]{:S(2)}) collective-permute-start(bf16[2,192,512]{2,1,0:T(8,128)(2,1)} %get-tuple-element.118), channel_id=1, source_target_pairs={{224,0},{192,32},{32,64},{0,96},{96,128},{64,160},{160,192},{128,2... | collective-permute-start | bytes 1179656 | tf_op jit(solution)/shard_map/turn_down/ppermute | solution.py:536
  91.3 16.5 %collective-permute-start.18 = (bf16[2,192,512]{2,1,0:T(8,128)(2,1)}, bf16[2,192,512]{2,1,0:T(8,128)(2,1)S(1)}, u32[]{:S(2)}, u32[]{:S(2)}) collective-permute-start(bf16[2,192,512]{2,1,0:T(8,128)(2,1)} %get-tuple-element.120), channel_id=1, source_target_pairs={{160,0},{128,32},{224,64},{192,96},{32,128},{0,160},{96,192},{64,2... | collective-permute-start | bytes 1179656 | tf_op jit(solution)/shard_map/turn_down/ppermute | solution.py:536
  109.9 18.3 %collective-permute-start.22 = (bf16[8,2,48,512]{3,2,0,1:T(8,128)(2,1)S(1)}, bf16[8,2,48,512]{3,2,0,1:T(8,128)(2,1)S(1)}, u32[]{:S(2)}, u32[]{:S(2)}) collective-permute-start(bf16[8,2,48,512]{3,2,0,1:T(8,128)(2,1)S(1)} %copy.53), channel_id=1, source_target_pairs={{192,0},{0,64},{64,128},{128,192},{193,1},{1,65},{65,129},{129,193... | collective-permute-start | bytes 2359304 | tf_op jit(solution)/shard_map/gather_rows/ppermute | solution.py:523
  110.8 20.3 %collective-permute-start.20 = (bf16[8,2,48,512]{3,2,0,1:T(8,128)(2,1)S(1)}, bf16[8,2,48,512]{3,2,0,1:T(8,128)(2,1)S(1)}, u32[]{:S(2)}, u32[]{:S(2)}) collective-permute-start(bf16[8,2,48,512]{3,2,0,1:T(8,128)(2,1)S(1)} %copy.53), channel_id=1, source_target_pairs={{64,0},{128,64},{192,128},{0,192},{65,1},{129,65},{193,129},{1,193... | collective-permute-start | bytes 2359304 | tf_op jit(solution)/shard_map/gather_rows/ppermute | solution.py:523
  128.3 15.5 %collective-permute-start.23 = (bf16[8,2,48,512]{3,2,0,1:T(8,128)(2,1)S(1)}, bf16[8,2,48,512]{3,2,0,1:T(8,128)(2,1)S(1)}, u32[]{:S(2)}, u32[]{:S(2)}) collective-permute-start(bf16[8,2,48,512]{3,2,0,1:T(8,128)(2,1)S(1)} %collective-permute-done.22), channel_id=1, source_target_pairs={{0,32},{32,0},{1,33},{33,1},{2,34},{34,2},{3,35},{35,3},{4,36},{36... | collective-permute-start | bytes 2359304 | tf_op jit(solution)/shard_map/gather_rows/ppermute | solution.py:527
  131.1 12.7 %collective-permute-start.21 = (bf16[8,2,48,512]{3,2,0,1:T(8,128)(2,1)S(1)}, bf16[8,2,48,512]{3,2,0,1:T(8,128)(2,1)S(1)}, u32[]{:S(2)}, u32[]{:S(2)}) collective-permute-start(bf16[8,2,48,512]{3,2,0,1:T(8,128)(2,1)S(1)} %collective-permute-done.20), channel_id=1, source_target_pairs={{0,32},{32,0},{1,33},{33,1},{2,34},{34,2},{3,35},{35,3},{4,36},{36... | collective-permute-start | bytes 2359304 | tf_op jit(solution)/shard_map/gather_rows/ppermute | solution.py:527
  131.1 12.8 %collective-permute-start.19 = (bf16[8,2,48,512]{3,2,1,0:T(8,128)(2,1)S(1)}, bf16[8,2,48,512]{3,2,1,0:T(8,128)(2,1)S(1)}, u32[]{:S(2)}, u32[]{:S(2)}) collective-permute-start(bf16[8,2,48,512]{3,2,1,0:T(8,128)(2,1)S(1)} %bitcast.45), channel_id=1, source_target_pairs={{0,32},{32,0},{1,33},{33,1},{2,34},{34,2},{3,35},{35,3},{4,36},{36... | collective-permute-start | bytes 2359304 | tf_op jit(solution)/shard_map/gather_rows/ppermute | solution.py:527
  131.7 19.3 %collective-permute-start.25 = (bf16[8,48,512]{2,1,0:T(8,128)(2,1)S(1)}, bf16[8,48,512]{2,1,0:T(8,128)(2,1)S(1)}, u32[]{:S(2)}, u32[]{:S(2)}) collective-permute-start(bf16[8,48,512]{2,1,0:T(8,128)(2,1)S(1)} %slice_bitcast_fusion), channel_id=1, source_target_pairs={{192,0},{0,64},{64,128},{128,192},{193,1},{1,65},{65,129},{129,193... | collective-permute-start | bytes 1179656 | tf_op jit(solution)/shard_map/gather_rows/ppermute | solution.py:523
  132.1 22.2 %collective-permute-start.24 = (bf16[8,48,512]{2,1,0:T(8,128)(2,1)S(1)}, bf16[8,48,512]{2,1,0:T(8,128)(2,1)S(1)}, u32[]{:S(2)}, u32[]{:S(2)}) collective-permute-start(bf16[8,48,512]{2,1,0:T(8,128)(2,1)S(1)} %slice_bitcast_fusion.1), channel_id=1, source_target_pairs={{64,0},{128,64},{192,128},{0,192},{65,1},{129,65},{193,129},{1,193... | collective-permute-start | bytes 1179656 | tf_op jit(solution)/shard_map/gather_rows/ppermute | solution.py:523
  158.9 9.1 %collective-permute-start.31 = (bf16[384,384]{1,0:T(8,128)(2,1)S(1)}, bf16[384,384]{1,0:T(8,128)(2,1)S(1)}, u32[]{:S(2)}, u32[]{:S(2)}) collective-permute-start(bf16[384,384]{1,0:T(8,128)(2,1)S(1)} %expert_up_far.1.refs_0_), channel_id=1, source_target_pairs={{192,0},{0,64},{64,128},{128,192},{193,1},{1,65},{65,129},{129,193... | collective-permute-start | bytes 884744 | tf_op jit(solution)/shard_map/gather_units/ppermute | solution.py:523
  159.0 10.3 %collective-permute-start.29 = (bf16[384,384]{1,0:T(8,128)(2,1)S(1)}, bf16[384,384]{1,0:T(8,128)(2,1)S(1)}, u32[]{:S(2)}, u32[]{:S(2)}) collective-permute-start(bf16[384,384]{1,0:T(8,128)(2,1)S(1)} %expert_up_far.1.refs_0_), channel_id=1, source_target_pairs={{64,0},{128,64},{192,128},{0,192},{65,1},{129,65},{193,129},{1,193... | collective-permute-start | bytes 884744 | tf_op jit(solution)/shard_map/gather_units/ppermute | solution.py:523
  161.0 10.6 %collective-permute-start.28 = (bf16[384,384]{1,0:T(8,128)(2,1)S(1)}, bf16[384,384]{1,0:T(8,128)(2,1)S(1)}, u32[]{:S(2)}, u32[]{:S(2)}) collective-permute-start(bf16[384,384]{1,0:T(8,128)(2,1)S(1)} %expert_up_far.1.refs_0_), channel_id=1, source_target_pairs={{0,32},{32,0},{1,33},{33,1},{2,34},{34,2},{3,35},{35,3},{4,36},{36... | collective-permute-start | bytes 884744 | tf_op jit(solution)/shard_map/gather_units/ppermute | solution.py:527
  169.4 6.3 %collective-permute-start.34 = (bf16[192,384]{1,0:T(8,128)(2,1)S(1)}, bf16[192,384]{1,0:T(8,128)(2,1)S(1)}, u32[]{:S(2)}, u32[]{:S(2)}) collective-permute-start(bf16[192,384]{1,0:T(8,128)(2,1)S(1)} %slice.19), channel_id=1, source_target_pairs={{192,0},{0,64},{64,128},{128,192},{193,1},{1,65},{65,129},{129,193... | collective-permute-start | bytes 442376 | tf_op jit(solution)/shard_map/gather_units/ppermute | solution.py:523
  170.2 6.9 %collective-permute-start.33 = (bf16[192,384]{1,0:T(8,128)(2,1)S(1)}, bf16[192,384]{1,0:T(8,128)(2,1)S(1)}, u32[]{:S(2)}, u32[]{:S(2)}) collective-permute-start(bf16[192,384]{1,0:T(8,128)(2,1)S(1)} %slice.18), channel_id=1, source_target_pairs={{64,0},{128,64},{192,128},{0,192},{65,1},{129,65},{193,129},{1,193... | collective-permute-start | bytes 442376 | tf_op jit(solution)/shard_map/gather_units/ppermute | solution.py:523
  210.6 5.9 %collective-permute-start.37 = (bf16[48,512]{1,0:T(8,128)(2,1)S(1)}, bf16[48,512]{1,0:T(8,128)(2,1)S(1)}, u32[]{:S(2)}, u32[]{:S(2)}) collective-permute-start(bf16[48,512]{1,0:T(8,128)(2,1)S(1)} %get-tuple-element.142), channel_id=1, source_target_pairs={{3,0},{0,1},{1,2},{2,3},{7,4},{4,5},{5,6},{6,7},{11,8},{8,9},{9,10... | collective-permute-start | bytes 147464 | tf_op jit(solution)/shard_map/mix/ppermute | solution.py:511
  211.0 6.1 %collective-permute-start.38 = (bf16[48,512]{1,0:T(8,128)(2,1)S(1)}, bf16[48,512]{1,0:T(8,128)(2,1)S(1)}, u32[]{:S(2)}, u32[]{:S(2)}) collective-permute-start(bf16[48,512]{1,0:T(8,128)(2,1)S(1)} %get-tuple-element.143), channel_id=1, source_target_pairs={{2,0},{3,1},{0,2},{1,3},{6,4},{7,5},{4,6},{5,7},{10,8},{11,9},{8,1... | collective-permute-start | bytes 147464 | tf_op jit(solution)/shard_map/mix/ppermute | solution.py:511
  (29 other events, 250.3 us)
Sparse Core Ops, SparseCore 0:
  9.1 43.8 all-gather.2
